TPU v7x, 32 devices: a whole 2x2x4 slice. The times are simulated.
32 devices in a mesh: dp: 8 (over y, x, core), tensor: 4 (over z).
Axes of the slice: x: 2, y: 2, z: 4, core: 2. Of those that a mesh axis runs over, the one named last changes fastest.
Arguments:
- tokens: bfloat16 [2, 8, 2048, 768], P(None, 'dp', 'tensor'), may hold values from -6 to 6
- segments: int32 [2, 8, 2048], P(None, 'dp'), may hold values from 0 to 127, never falling along the last dimension, each value on 1 to 1024 neighbouring positions
- w_query: bfloat16 [768, 768], P(('dp', 'tensor')), may hold values from -0.21875 to 0.21875
- w_key: bfloat16 [768, 768], P(('dp', 'tensor')), may hold values from -0.21875 to 0.21875
- w_value: bfloat16 [768, 768], P(('dp', 'tensor')), may hold values from -0.21875 to 0.21875
- w_out: bfloat16 [768, 768], P(('dp', 'tensor')), may hold values from -0.875 to 0.875
- norm_attn: bfloat16 [768], P(('dp', 'tensor')), may hold values from 0.5 to 1.5
- norm_ffn: bfloat16 [768], P(('dp', 'tensor')), may hold values from 0.5 to 1.5
- pre_mix: bfloat16 [12, 12], replicated, may hold values from -1.75 to 1.75
- post_mix: bfloat16 [12, 12], replicated, may hold values from -1.75 to 1.75
- w_up: bfloat16 [768, 3072], P('dp', 'tensor'), may hold values from -0.21875 to 0.21875
- w_down: bfloat16 [768, 3072], P('dp', 'tensor'), may hold values from -0.15625 to 0.15625
- out_grad: bfloat16 [2, 8, 2048, 768], P(None, 'dp', 'tensor'), may hold values from -6 to 6
Outputs:
- out: bfloat16 [2, 8, 2048, 768], P(None, 'dp', 'tensor')
- d_tokens: float32 [2, 8, 2048, 768], P(None, 'dp', 'tensor')
- d_w_query: float32 [768, 768], P(('dp', 'tensor'))
- d_w_key: float32 [768, 768], P(('dp', 'tensor'))
- d_w_value: float32 [768, 768], P(('dp', 'tensor'))
- d_w_out: float32 [768, 768], P(('dp', 'tensor'))
- d_norm_attn: float32 [768], P(('dp', 'tensor'))
- d_norm_ffn: float32 [768], P(('dp', 'tensor'))
- d_pre_mix: float32 [12, 12], replicated
- d_post_mix: float32 [12, 12], replicated
- d_w_up: float32 [768, 3072], P('dp', 'tensor')
- d_w_down: float32 [768, 3072], P('dp', 'tensor')
Inputs may be any that keep to these rules, and one draw needn't show every extreme that they name: `segments`: within each sequence the numbers never fall; a run of equal numbers is one document, and some document is 1024 tokens long.
All inputs are finite; a program needn't handle non-finite values.
Results may differ from a plain program's by a relative error of at most 0.018.
Values may be sent and summed in bfloat16 or wider, within the bound.
A program may use at most 512 MiB of HBM per device.

v0:
```python
import jax
import jax.numpy as jnp
from jax import lax
from jax.sharding import PartitionSpec as P


def split_up(x, dim, devices):
    before, after = (x.shape[:dim], x.shape[dim + 1 :])
    return jnp.moveaxis(x.reshape(*before, devices, -1, *after), dim, 0)


def sum_at_owner(x, axis, dim):
    devices = lax.axis_size(axis)
    blocks = lax.all_to_all(split_up(x, dim, devices), axis, 0, 0, tiled=True)
    return jnp.sum(blocks.astype(jnp.float32), axis=0)


def in_one_piece(arrays, axis, dim, along):
    widths = [a.shape[along] for a in arrays]
    both = jnp.concatenate(arrays, axis=along)
    filled = sum_at_owner(both, axis, dim)
    return tuple(jnp.split(filled, [sum(widths[:k]) for k in range(1, len(widths))], axis=along))


def matmul(left, right):
    return jnp.dot(left, right, preferred_element_type=jnp.float32)


def right_t(left, right):
    return lax.dot_general(
        left, right, (((1,), (1,)), ((), ())), preferred_element_type=jnp.float32
    )


def left_t(left, right):
    return lax.dot_general(
        left, right, (((0,), (0,)), ((), ())), preferred_element_type=jnp.float32
    )


def gelu_exact(values):
    return jax.nn.gelu(values, approximate=False)


def gelu_back(upper, grad):
    unused, pull = jax.vjp(gelu_exact, upper)
    return pull(grad)[0]


def rms_scale(values):
    return lax.rsqrt(jnp.mean(values * values, axis=-1, keepdims=True) + 1e-06)


def rms_back(grad_norm, normed, scale, gain):
    scaled = grad_norm * gain
    return scale * (scaled - normed * jnp.mean(scaled * normed, axis=-1, keepdims=True))


def mixed_scores(query_block, key_rows, pre_mix, row_seg, col_seg, row_place, col_place):
    heads = pre_mix.shape[0]
    block_rows, width = query_block.shape
    length = key_rows.shape[0]
    head_width = width // heads
    query_heads = query_block.reshape(block_rows, heads, head_width)
    key_heads = key_rows.reshape(length, heads, head_width)
    logits = jnp.einsum(
        "qgd,kgd->gqk", query_heads, key_heads, preferred_element_type=jnp.float32
    ) * head_width ** (-0.5)
    logits = logits.astype(jnp.bfloat16)
    mixed = jnp.einsum("gh,gqk->hqk", pre_mix, logits, preferred_element_type=jnp.float32)
    allowed = (row_seg[:, None] == col_seg[None, :]) & (col_place[None, :] <= row_place[:, None])
    return (logits, jnp.where(allowed[None], mixed, -1e30))


def attend_block(query_block, key_rows, value_rows, row_seg, col_seg, row_place, pre_mix, post_mix):
    heads = pre_mix.shape[0]
    block_rows, width = query_block.shape
    length = key_rows.shape[0]
    head_width = width // heads
    col_place = jnp.arange(length, dtype=jnp.int32)
    logits, mixed = mixed_scores(
        query_block, key_rows, pre_mix, row_seg, col_seg, row_place, col_place
    )
    top = jnp.max(mixed, axis=-1, keepdims=True)
    expd = jnp.exp(mixed - top)
    total = jnp.sum(expd, axis=-1, keepdims=True)
    weights_low = (expd / total).astype(jnp.bfloat16)
    post = jnp.einsum(
        "gh,gqk->hqk", post_mix, weights_low, preferred_element_type=jnp.float32
    ).astype(jnp.bfloat16)
    value_heads = value_rows.reshape(length, heads, head_width)
    result = jnp.einsum("hqk,khd->qhd", post, value_heads, preferred_element_type=jnp.float32)
    return (result.reshape(block_rows, width).astype(jnp.bfloat16), top + jnp.log(total))


def score_grads(
    query_block,
    grad_block,
    log_total,
    key_rows,
    value_rows,
    row_seg,
    col_seg,
    row_place,
    col_place,
    pre_mix,
    post_mix,
):
    heads = pre_mix.shape[0]
    block_rows, width = query_block.shape
    length = key_rows.shape[0]
    head_width = width // heads
    logits, mixed = mixed_scores(
        query_block, key_rows, pre_mix, row_seg, col_seg, row_place, col_place
    )
    weights = jnp.exp(mixed - log_total)
    weights_low = weights.astype(jnp.bfloat16)
    post = jnp.einsum(
        "gh,gqk->hqk", post_mix, weights_low, preferred_element_type=jnp.float32
    ).astype(jnp.bfloat16)
    grad_heads = grad_block.reshape(block_rows, heads, head_width)
    value_heads = value_rows.reshape(length, heads, head_width)
    grad_post = jnp.einsum(
        "qhd,khd->hqk", grad_heads, value_heads, preferred_element_type=jnp.float32
    ).astype(jnp.bfloat16)
    grad_value = jnp.einsum("hqk,qhd->khd", post, grad_heads, preferred_element_type=jnp.float32)
    grad_weights = jnp.einsum(
        "gh,hqk->gqk", post_mix, grad_post, preferred_element_type=jnp.float32
    )
    return (logits, weights, weights_low, grad_post, grad_value, grad_weights)


def attend_back(
    query_block,
    grad_block,
    log_total,
    key_rows,
    value_rows,
    row_seg,
    col_seg,
    row_place,
    pre_mix,
    post_mix,
):
    heads = pre_mix.shape[0]
    block_rows, width = query_block.shape
    length = key_rows.shape[0]
    head_width = width // heads
    scale = head_width ** (-0.5)
    col_place = jnp.arange(length, dtype=jnp.int32)
    logits, weights, weights_low, grad_post, grad_value, grad_weights = score_grads(
        query_block,
        grad_block,
        log_total,
        key_rows,
        value_rows,
        row_seg,
        col_seg,
        row_place,
        col_place,
        pre_mix,
        post_mix,
    )
    key_heads = key_rows.reshape(length, heads, head_width)
    query_heads = query_block.reshape(block_rows, heads, head_width)
    mix_post = jnp.einsum("gqk,hqk->gh", weights_low, grad_post, preferred_element_type=jnp.float32)
    row_term = jnp.sum(weights * grad_weights, axis=-1, keepdims=True)
    grad_mixed = (weights * (grad_weights - row_term)).astype(jnp.bfloat16)
    grad_logits = jnp.einsum(
        "gh,hqk->gqk", pre_mix, grad_mixed, preferred_element_type=jnp.float32
    ).astype(jnp.bfloat16)
    mix_pre = jnp.einsum("gqk,hqk->gh", logits, grad_mixed, preferred_element_type=jnp.float32)
    grad_query = (
        jnp.einsum("gqk,kgd->qgd", grad_logits, key_heads, preferred_element_type=jnp.float32)
        * scale
    )
    grad_key = (
        jnp.einsum("gqk,qgd->kgd", grad_logits, query_heads, preferred_element_type=jnp.float32)
        * scale
    )
    return (
        grad_query.reshape(block_rows, width),
        grad_key.reshape(length, width),
        grad_value.reshape(length, width),
        mix_pre,
        mix_post,
        row_term,
    )


def per_device(
    tokens,
    segments,
    w_query,
    w_key,
    w_value,
    w_out,
    norm_attn,
    norm_ffn,
    pre_mix,
    post_mix,
    w_up,
    w_down,
    out_grad,
):
    micro, single, rows, width = tokens.shape
    part = lax.axis_index("tensor")
    length = rows * lax.axis_size("tensor")
    block_rows = min(512, rows)
    blocks = rows // block_rows
    items = micro * blocks
    count = micro * rows
    all_query, all_key, all_value, all_out, gain_attn, gain_ffn = (
        lax.all_gather(w_query, ("dp", "tensor"), axis=0, tiled=True),
        lax.all_gather(w_key, ("dp", "tensor"), axis=0, tiled=True),
        lax.all_gather(w_value, ("dp", "tensor"), axis=0, tiled=True),
        lax.all_gather(w_out, ("dp", "tensor"), axis=0, tiled=True),
        lax.all_gather(norm_attn, ("dp", "tensor"), axis=0, tiled=True),
        lax.all_gather(norm_ffn, ("dp", "tensor"), axis=0, tiled=True),
    )
    gain_attn = gain_attn.astype(jnp.float32)
    gain_ffn = gain_ffn.astype(jnp.float32)
    up_rows, down_rows = (
        lax.all_gather(w_up, "dp", axis=0, tiled=True),
        lax.all_gather(w_down, "dp", axis=0, tiled=True),
    )
    inputs = tokens.reshape(count, width).astype(jnp.float32)
    scale_attn = rms_scale(inputs)
    normed_attn = inputs * scale_attn
    h_attn = (normed_attn * gain_attn).astype(jnp.bfloat16)
    query_rows = matmul(h_attn, all_query).astype(jnp.bfloat16)
    key_local = matmul(h_attn, all_key).astype(jnp.bfloat16).reshape(micro, rows, width)
    value_local = matmul(h_attn, all_value).astype(jnp.bfloat16).reshape(micro, rows, width)
    key_whole, value_whole = (
        lax.all_gather(key_local, "tensor", axis=1, tiled=True),
        lax.all_gather(value_local, "tensor", axis=1, tiled=True),
    )
    seg_whole = segments.reshape(micro, length)
    seg_local = lax.dynamic_slice_in_dim(seg_whole, part * rows, rows, 1)
    query_items = query_rows.reshape(items, block_rows, width)
    place_rows = (part * rows + jnp.arange(rows, dtype=jnp.int32)).reshape(blocks, block_rows)
    place_items = jnp.tile(place_rows, (micro, 1))
    micro_items = jnp.arange(items, dtype=jnp.int32) // blocks

    def forward_item(packed):
        query_block, row_seg, row_place, index = packed
        key_rows = lax.dynamic_index_in_dim(key_whole, index, 0, keepdims=False)
        value_rows = lax.dynamic_index_in_dim(value_whole, index, 0, keepdims=False)
        col_seg = lax.dynamic_index_in_dim(seg_whole, index, 0, keepdims=False)
        return attend_block(
            query_block, key_rows, value_rows, row_seg, col_seg, row_place, pre_mix, post_mix
        )

    attended, log_totals = lax.map(forward_item, (query_items, seg_local, place_items, micro_items))
    attended = attended.reshape(count, width)
    after_attn = inputs + matmul(attended, all_out)
    scale_ffn = rms_scale(after_attn)
    normed_ffn = after_attn * scale_ffn
    h_ffn = (normed_ffn * gain_ffn).astype(jnp.bfloat16)
    grad_out = out_grad.reshape(count, width)
    h_whole = lax.all_gather(
        h_ffn.reshape(micro, rows, width), "tensor", axis=1, tiled=True
    ).reshape(micro * length, width)
    upper = matmul(h_whole, up_rows)
    hidden = gelu_exact(upper).astype(jnp.bfloat16)
    partial_out = right_t(hidden, down_rows).reshape(micro, length, width)
    output = after_attn + lax.psum_scatter(
        partial_out.astype(jnp.bfloat16), "tensor", scatter_dimension=1, tiled=True
    ).astype(jnp.float32).reshape(count, width)
    grad_whole = lax.all_gather(
        grad_out.reshape(micro, rows, width), "tensor", axis=1, tiled=True
    ).reshape(micro * length, width)
    d_hidden = gelu_back(upper, matmul(grad_whole, down_rows)).astype(jnp.bfloat16)
    grad_down = left_t(grad_whole, hidden)
    grad_up = left_t(h_whole, d_hidden)
    partial_grad = right_t(d_hidden, up_rows).reshape(micro, length, width)
    grad_h_ffn = (
        lax.psum_scatter(
            partial_grad.astype(jnp.bfloat16), "tensor", scatter_dimension=1, tiled=True
        )
        .astype(jnp.float32)
        .reshape(count, width)
    )
    grad_up, grad_down = in_one_piece(
        (grad_up.astype(jnp.bfloat16), grad_down.astype(jnp.bfloat16)), "dp", 0, 1
    )
    grad_gain_ffn = jnp.sum(grad_h_ffn * normed_ffn, axis=0)
    grad_after = grad_out.astype(jnp.float32) + rms_back(
        grad_h_ffn, normed_ffn, scale_ffn, gain_ffn
    )
    grad_branch = grad_after.astype(jnp.bfloat16)
    grad_w_out = left_t(attended, grad_branch)
    grad_attended = (
        right_t(grad_branch, all_out).astype(jnp.bfloat16).reshape(items, block_rows, width)
    )

    def backward_item(packed):
        query_block, grad_block, log_total, row_seg, row_place, index = packed
        key_rows = lax.dynamic_index_in_dim(key_whole, index, 0, keepdims=False)
        value_rows = lax.dynamic_index_in_dim(value_whole, index, 0, keepdims=False)
        col_seg = lax.dynamic_index_in_dim(seg_whole, index, 0, keepdims=False)
        return attend_back(
            query_block,
            grad_block,
            log_total,
            key_rows,
            value_rows,
            row_seg,
            col_seg,
            row_place,
            pre_mix,
            post_mix,
        )

    grad_query, grad_key, grad_value, grad_pre, grad_post, row_terms = lax.map(
        backward_item, (query_items, grad_attended, log_totals, seg_local, place_items, micro_items)
    )
    grad_query = grad_query.astype(jnp.bfloat16).reshape(count, width)
    grad_key = jnp.sum(grad_key.reshape(micro, blocks, length, width), axis=1)
    grad_value = jnp.sum(grad_value.reshape(micro, blocks, length, width), axis=1)
    grad_key, grad_value = (
        lax.psum_scatter(
            grad_key.astype(jnp.bfloat16), "tensor", scatter_dimension=1, tiled=True
        ).astype(jnp.float32),
        lax.psum_scatter(
            grad_value.astype(jnp.bfloat16), "tensor", scatter_dimension=1, tiled=True
        ).astype(jnp.float32),
    )
    grad_key = grad_key.astype(jnp.bfloat16).reshape(count, width)
    grad_value = grad_value.astype(jnp.bfloat16).reshape(count, width)
    grad_pre = jnp.sum(grad_pre, axis=0)
    grad_post = jnp.sum(grad_post, axis=0)
    grad_w_query = left_t(h_attn, grad_query)
    grad_w_key = left_t(h_attn, grad_key)
    grad_w_value = left_t(h_attn, grad_value)
    grad_h_attn = (
        right_t(grad_query, all_query) + right_t(grad_key, all_key) + right_t(grad_value, all_value)
    )
    grad_gain_attn = jnp.sum(grad_h_attn * normed_attn, axis=0)
    grad_tokens = grad_after + rms_back(grad_h_attn, normed_attn, scale_attn, gain_attn)
    owned = (
        lax.psum_scatter(grad_w_query, ("dp", "tensor"), scatter_dimension=0, tiled=True),
        lax.psum_scatter(grad_w_key, ("dp", "tensor"), scatter_dimension=0, tiled=True),
        lax.psum_scatter(grad_w_value, ("dp", "tensor"), scatter_dimension=0, tiled=True),
        lax.psum_scatter(grad_w_out, ("dp", "tensor"), scatter_dimension=0, tiled=True),
        lax.psum_scatter(grad_gain_attn, ("dp", "tensor"), scatter_dimension=0, tiled=True),
        lax.psum_scatter(grad_gain_ffn, ("dp", "tensor"), scatter_dimension=0, tiled=True),
    )
    grad_pre, grad_post = lax.psum((grad_pre, grad_post), ("dp", "tensor"))
    return (
        output.astype(jnp.bfloat16).reshape(tokens.shape),
        grad_tokens.reshape(tokens.shape),
        owned[0],
        owned[1],
        owned[2],
        owned[3],
        owned[4],
        owned[5],
        grad_pre,
        grad_post,
        grad_up,
        grad_down,
    )


def solution(mesh):
    return jax.shard_map(
        per_device,
        mesh=mesh,
        in_specs=(
            P(None, "dp", "tensor", None),
            P(None, "dp", None),
            P(("dp", "tensor"), None),
            P(("dp", "tensor"), None),
            P(("dp", "tensor"), None),
            P(("dp", "tensor"), None),
            P(("dp", "tensor")),
            P(("dp", "tensor")),
            P(),
            P(),
            P("dp", "tensor"),
            P("dp", "tensor"),
            P(None, "dp", "tensor", None),
        ),
        out_specs=(
            P(None, "dp", "tensor", None),
            P(None, "dp", "tensor", None),
            P(("dp", "tensor"), None),
            P(("dp", "tensor"), None),
            P(("dp", "tensor"), None),
            P(("dp", "tensor"), None),
            P(("dp", "tensor")),
            P(("dp", "tensor")),
            P(),
            P(),
            P("dp", "tensor"),
            P("dp", "tensor"),
        ),
        check_vma=False,
    )
```

profile of v0, /device:TPU:0, one launch (start us, length us, event | category | flops | bytes accessed | tf_op | source)
XLA Modules:
  0.0 3009.8 jit_solution(13048826008616669471)
XLA Ops:
  11.1 42.1 %all-reduce.5 = (bf16[768]{0:T(1024)(128)(2,1)S(1)}, bf16[768]{0:T(1024)(128)(2,1)S(1)}) all-reduce(bf16[768]{0:T(1024)(128)(2,1)S(1)} %dynamic-update-slice, bf16[768]{0:T(1024)(128)(2,1)S(1)} %dynamic-update-slice.1), channel_id=1, replica_groups=mesh['dp'=8,'tensor'=4] {'dp','tensor'}, use_global_device_ids=true, to_apply=%add | all-reduce | flops 1536 | bytes 6144
  72.0 51.5 %all-gather.12.cloned.1.call-done = bf16[768,768]{1,0:T(8,128)(2,1)} async-done(((bf16[24,768]{1,0:T(8,128)(2,1)}), bf16[768,768]{1,0:T(8,128)(2,1)}) %all-gather.12.cloned.1.call-update) | async-done | bytes 1179664 | tf_op jit(solution)/shard_map/all_gather | solution.py:216
  131.9 47.5 %all-gather.16.cloned.1.call-done = bf16[768,768]{1,0:T(8,128)(2,1)} async-done(((bf16[24,768]{1,0:T(8,128)(2,1)}), bf16[768,768]{1,0:T(8,128)(2,1)}) %all-gather.16.cloned.1.call-update) | async-done | bytes 1179664 | tf_op jit(solution)/shard_map/all_gather | solution.py:214
  183.6 112.1 %all-gather.20.cloned.1.call-done = bf16[2,2048,768]{1,2,0:T(8,128)(2,1)} async-done(((bf16[2,512,768]{1,2,0:T(8,128)(2,1)}), bf16[2,2048,768]{1,2,0:T(8,128)(2,1)}) %all-gather.20.cloned.1.call-update) | async-done | bytes 6291472 | tf_op jit(solution)/shard_map/all_gather | solution.py:235
  295.7 115.6 %all-gather.14.cloned.1.call-done = bf16[2,2048,768]{1,2,0:T(8,128)(2,1)} async-done(((bf16[2,512,768]{1,2,0:T(8,128)(2,1)}), bf16[2,2048,768]{1,2,0:T(8,128)(2,1)}) %all-gather.14.cloned.1.call-update) | async-done | bytes 6291472 | tf_op jit(solution)/shard_map/all_gather | solution.py:236
  411.9 413.1 %while.30 = (s32[]{:T(128)}, bf16[2,512,768]{2,1,0:T(8,128)(2,1)}, f32[2,12,512,1]{1,2,3,0:T(8,128)}, s32[2]{0:T(128)S(1)}, bf16[2,2048,768]{1,2,0:T(8,128)(2,1)...) while((s32[]{:T(128)}, bf16[2,512,768]{2,1,0:T(8,128)(2,1)}, ...), condition=%wide.region_4.5_spmd, body=%wide.region_1.4_spmd.sunk | while | flops 3979732992 | bytes 285684640 | solution.py:254
  460.3 69.8 %bitcast_reduce_fusion.2 = (f32[12,512]{0,1:T(8,128)S(1)}, f32[512,2048,12]{1,2,0:T(8,128)}) fusion(pred[512,2048]{1,0:T(8,128)(4,1)} %fusion.202, bf16[12,12]{0,1:T(8,128)(2,1)S(1)} %get-tuple-element.621, bf16[12,512,2048]{2,1,0:T(8,128)(2,1)} %multiply_convert_fusion.6), kind=kOutput, calls=%fused_computation.1.clone.1 | convolution fusion | flops 327149568 | bytes 76570912 | tf_op jit(solution)/shard_map/while/body/eval_jaxpr/gh,gqk->hqk/dot_general | solution.py:70
  551.8 39.8 %convert_bitcast_fusion.6 = bf16[12,512,2048]{2,0,1:T(8,128)(2,1)} fusion(f32[512,2048,12]{1,2,0:T(8,128)} %get-tuple-element.558, f32[12,512]{0,1:T(8,128)S(1)} %fusion.203, f32[12,512]{0,1:T(8,128)S(1)} %get-tuple-element.559, pred[512,2048]{1,0:T(8,128)(4,1)S(1)} %copy-done.2, bf16[12,12]{0,1:T(8,128)(2,1)S(1)} %get-tuple-element.622), kind=kOutput, calls=%fused_computation.8.clone.2 | convolution fusion | flops 364904448 | bytes 76595488 | tf_op jit(solution)/shard_map/while/body/eval_jaxpr/gh,gqk->hqk/dot_general | solution.py:88
  652.1 69.8 %bitcast_reduce_fusion.2 = (f32[12,512]{0,1:T(8,128)S(1)}, f32[512,2048,12]{1,2,0:T(8,128)}) fusion(pred[512,2048]{1,0:T(8,128)(4,1)} %fusion.202, bf16[12,12]{0,1:T(8,128)(2,1)S(1)} %get-tuple-element.621, bf16[12,512,2048]{2,1,0:T(8,128)(2,1)} %multiply_convert_fusion.6), kind=kOutput, calls=%fused_computation.1.clone.1 | convolution fusion | flops 327149568 | bytes 76570912 | tf_op jit(solution)/shard_map/while/body/eval_jaxpr/gh,gqk->hqk/dot_general | solution.py:70
  743.5 39.8 %convert_bitcast_fusion.6 = bf16[12,512,2048]{2,0,1:T(8,128)(2,1)} fusion(f32[512,2048,12]{1,2,0:T(8,128)} %get-tuple-element.558, f32[12,512]{0,1:T(8,128)S(1)} %fusion.203, f32[12,512]{0,1:T(8,128)S(1)} %get-tuple-element.559, pred[512,2048]{1,0:T(8,128)(4,1)S(1)} %copy-done.2, bf16[12,12]{0,1:T(8,128)(2,1)S(1)} %get-tuple-element.622), kind=kOutput, calls=%fused_computation.8.clone.2 | convolution fusion | flops 364904448 | bytes 76595488 | tf_op jit(solution)/shard_map/while/body/eval_jaxpr/gh,gqk->hqk/dot_general | solution.py:88
  831.8 112.3 %all-gather.24.cloned.1.call-done = bf16[2,2048,768]{2,1,0:T(8,128)(2,1)} async-done(((bf16[2,512,768]{2,1,0:T(8,128)(2,1)}), bf16[2,2048,768]{2,1,0:T(8,128)(2,1)}) %all-gather.24.cloned.1.call-update) | async-done | bytes 6291472 | tf_op jit(solution)/shard_map/all_gather | solution.py:261
  968.2 116.8 %all-gather.30.cloned.1.call-done = bf16[2,1,2048,768]{3,2,1,0:T(8,128)(2,1)} async-done(((bf16[2,1,512,768]{3,2,1,0:T(8,128)(2,1)}), bf16[2,1,2048,768]{3,2,1,0:T(8,128)(2,1)}) %all-gather.30.cloned.1.call-update) | async-done | bytes 6291472 | tf_op jit(solution)/shard_map/all_gather | solution.py:270
  1145.8 91.3 %reduce-scatter.11.cloned.1.call-done = bf16[2,512,768]{2,1,0:T(8,128)(2,1)} async-done(((bf16[2,2048,768]{2,1,0:T(8,128)(2,1)}), bf16[2,512,768]{2,1,0:T(8,128)(2,1)}) %reduce-scatter.11.cloned.1.call-update) | async-done | bytes 1572880 | tf_op jit(solution)/shard_map/reduce_scatter | solution.py:278
  1240.2 110.4 %reduce-scatter.9.cloned.1.call-done = bf16[2,512,768]{2,1,0:T(8,128)(2,1)} async-done(((bf16[2,2048,768]{2,1,0:T(8,128)(2,1)}), bf16[2,512,768]{2,1,0:T(8,128)(2,1)}) %reduce-scatter.9.cloned.1.call-update) | async-done | bytes 1572880 | tf_op jit(solution)/shard_map/reduce_scatter | solution.py:267
  1358.8 1000.3 %while.31 = (s32[]{:T(128)}, bf16[2,512,768]{2,1,0:T(8,128)(2,1)}, bf16[2,2048,768]{2,1,0:T(8,128)(2,1)}, bf16[2,2048,768]{2,1,0:T(8,128)(2,1)}, f32[2,12,12]{2,...) while((s32[]{:T(128)}, bf16[2,512,768]{2,1,0:T(8,128)(2,1)}, ...), condition=%wide.region_11.12_spmd, body=%wide.region_9.11_spmd.sunk | while | flops 10123732992 | bytes 879238528 | solution.py:315
  1536.3 44.0 %fusion.230 = bf16[12,64,2048]{2,1,0:T(8,128)(2,1)} fusion(bf16[512,12,64]{0,2,1:T(8,128)(2,1)S(1)} %bitcast.346, bf16[12,512,2048]{2,0,1:T(8,128)(2,1)} %convert_bitcast_fusion.8), kind=kOutput, calls=%fused_computation.46.clone.1 | convolution fusion | flops 1610612736 | bytes 29097984 | tf_op jit(solution)/shard_map/while/body/eval_jaxpr/hqk,qhd->khd/dot_general | solution.py:126
  1584.9 62.4 %fusion.227 = (f32[12,512]{0,1:T(8,128)S(1)}, f32[512,2048,12]{1,2,0:T(8,128)}) fusion(f32[512,2048,12]{1,2,0:T(8,128)} %fusion.225, f32[12,512]{0,1:T(8,128)S(1)} %dynamic-slice_bitcast_fusion.2, pred[512,2048]{1,0:T(8,128)(4,1)S(1)} %fusion.226, bf16[12,12]{0,1:T(8,128)(2,1)S(1)} %get-tuple-element.682, ...), kind=kOutput, calls=%fused_computation.29.clone.1 | convolution fusion | flops 352315392 | bytes 126927136 | tf_op jit(solution)/shard_map/while/body/eval_jaxpr/gh,hqk->gqk/dot_general | solution.py:127
  1647.3 52.7 %fusion.228 = bf16[12,512,2048]{2,0,1:T(8,128)(2,1)} fusion(f32[512,2048,12]{1,2,0:T(8,128)} %get-tuple-element.577, f32[512,2048,12]{1,2,0:T(8,128)} %fusion.225, f32[12,512]{0,1:T(8,128)S(1)} %get-tuple-element.578, f32[12,512]{0,1:T(8,128)S(1)} %dynamic-slice_bitcast_fusion.2, pred[512,2048]{1,0:T(8,128)(4,1)S(1)} %fusion.226), kind=kLoop, calls=%fused_computation.31.clone.1 | loop fusion | flops 62914560 | bytes 126926848 | tf_op jit(solution)/shard_map/while/body/eval_jaxpr/convert_element_type | solution.py:168
  1753.4 43.4 %fusion.229 = bf16[12,64,512]{2,1,0:T(8,128)(2,1)} fusion(bf16[2048,12,64]{0,2,1:T(8,128)(2,1)S(1)} %bitcast.340, bf16[12,512,2048]{2,0,1:T(8,128)(2,1)} %convert_bitcast_fusion.7), kind=kOutput, calls=%fused_computation.56.clone.1 | convolution fusion | flops 1611399168 | bytes 29097984 | tf_op jit(solution)/shard_map/while/body/eval_jaxpr/gqk,kgd->qgd/dot_general | solution.py:174
  1796.9 44.0 %fusion.231 = bf16[12,64,2048]{2,1,0:T(8,128)(2,1)} fusion(bf16[512,12,64]{0,2,1:T(8,128)(2,1)} %bitcast.344, bf16[12,512,2048]{2,0,1:T(8,128)(2,1)} %convert_bitcast_fusion.7), kind=kOutput, calls=%fused_computation.55.clone.1 | convolution fusion | flops 1613758464 | bytes 29097984 | tf_op jit(solution)/shard_map/while/body/eval_jaxpr/gqk,qgd->kgd/dot_general | solution.py:178
  2032.5 44.0 %fusion.230 = bf16[12,64,2048]{2,1,0:T(8,128)(2,1)} fusion(bf16[512,12,64]{0,2,1:T(8,128)(2,1)S(1)} %bitcast.346, bf16[12,512,2048]{2,0,1:T(8,128)(2,1)} %convert_bitcast_fusion.8), kind=kOutput, calls=%fused_computation.46.clone.1 | convolution fusion | flops 1610612736 | bytes 29097984 | tf_op jit(solution)/shard_map/while/body/eval_jaxpr/hqk,qhd->khd/dot_general | solution.py:126
  2081.2 62.4 %fusion.227 = (f32[12,512]{0,1:T(8,128)S(1)}, f32[512,2048,12]{1,2,0:T(8,128)}) fusion(f32[512,2048,12]{1,2,0:T(8,128)} %fusion.225, f32[12,512]{0,1:T(8,128)S(1)} %dynamic-slice_bitcast_fusion.2, pred[512,2048]{1,0:T(8,128)(4,1)S(1)} %fusion.226, bf16[12,12]{0,1:T(8,128)(2,1)S(1)} %get-tuple-element.682, ...), kind=kOutput, calls=%fused_computation.29.clone.1 | convolution fusion | flops 352315392 | bytes 126927136 | tf_op jit(solution)/shard_map/while/body/eval_jaxpr/gh,hqk->gqk/dot_general | solution.py:127
  2143.6 52.7 %fusion.228 = bf16[12,512,2048]{2,0,1:T(8,128)(2,1)} fusion(f32[512,2048,12]{1,2,0:T(8,128)} %get-tuple-element.577, f32[512,2048,12]{1,2,0:T(8,128)} %fusion.225, f32[12,512]{0,1:T(8,128)S(1)} %get-tuple-element.578, f32[12,512]{0,1:T(8,128)S(1)} %dynamic-slice_bitcast_fusion.2, pred[512,2048]{1,0:T(8,128)(4,1)S(1)} %fusion.226), kind=kLoop, calls=%fused_computation.31.clone.1 | loop fusion | flops 62914560 | bytes 126926848 | tf_op jit(solution)/shard_map/while/body/eval_jaxpr/convert_element_type | solution.py:168
  2249.7 43.4 %fusion.229 = bf16[12,64,512]{2,1,0:T(8,128)(2,1)} fusion(bf16[2048,12,64]{0,2,1:T(8,128)(2,1)S(1)} %bitcast.340, bf16[12,512,2048]{2,0,1:T(8,128)(2,1)} %convert_bitcast_fusion.7), kind=kOutput, calls=%fused_computation.56.clone.1 | convolution fusion | flops 1611399168 | bytes 29097984 | tf_op jit(solution)/shard_map/while/body/eval_jaxpr/gqk,kgd->qgd/dot_general | solution.py:174
  2293.1 44.0 %fusion.231 = bf16[12,64,2048]{2,1,0:T(8,128)(2,1)} fusion(bf16[512,12,64]{0,2,1:T(8,128)(2,1)} %bitcast.344, bf16[12,512,2048]{2,0,1:T(8,128)(2,1)} %convert_bitcast_fusion.7), kind=kOutput, calls=%fused_computation.55.clone.1 | convolution fusion | flops 1613758464 | bytes 29097984 | tf_op jit(solution)/shard_map/while/body/eval_jaxpr/gqk,qgd->kgd/dot_general | solution.py:178
  2370.6 100.0 %reduce-scatter.13.cloned.1.call-done = bf16[2,512,768]{2,1,0:T(8,128)(2,1)} async-done(((bf16[2,2048,768]{2,1,0:T(8,128)(2,1)}), bf16[2,512,768]{2,1,0:T(8,128)(2,1)}) %reduce-scatter.13.cloned.1.call-update) | async-done | bytes 1572880 | tf_op jit(solution)/shard_map/reduce_scatter | solution.py:322
  2503.5 80.5 %reduce-scatter.15.cloned.1.call-done = bf16[2,512,768]{2,1,0:T(8,128)(2,1)} async-done(((bf16[2,2048,768]{2,1,0:T(8,128)(2,1)}), bf16[2,512,768]{2,1,0:T(8,128)(2,1)}) %reduce-scatter.15.cloned.1.call-update) | async-done | bytes 1572880 | tf_op jit(solution)/shard_map/reduce_scatter | solution.py:325
  2601.1 41.0 %all-reduce.4 = (f32[768]{0:T(1024)S(1)}, f32[768]{0:T(1024)S(1)}, f32[12,12]{1,0:T(8,128)}, f32[12,12]{1,0:T(8,128)}) all-reduce(f32[768]{0:T(1024)S(1)} %get-tuple-element.298, f32[768]{0:T(1024)S(1)} %copy-done.19, f32[12,12]{1,0:T(8,128)S(1)} %reduce_sum.113, ...), channel_id=11, replica_groups=mesh['dp'=8,'tensor'=4] {'dp','tensor'}, use_global_device_ids=true, to_apply=%region_20.21.clone | all-reduce | flops 1824 | bytes 14592
  2648.6 40.9 %reduce-scatter.23.cloned.1.call-done = f32[24,768]{1,0:T(8,128)} async-done(((f32[768,768]{1,0:T(8,128)}), f32[24,768]{1,0:T(8,128)}) %reduce-scatter.23.cloned.1.call-update) | async-done | bytes 73744 | tf_op jit(solution)/shard_map/reduce_scatter | solution.py:345
  2689.5 104.7 %reduce-scatter.17.cloned.1.call-done = f32[24,768]{1,0:T(8,128)} async-done(((f32[768,768]{1,0:T(8,128)}), f32[24,768]{1,0:T(8,128)}) %reduce-scatter.17.cloned.1.call-update) | async-done | bytes 73744 | tf_op jit(solution)/shard_map/reduce_scatter | solution.py:342
  2794.2 103.9 %reduce-scatter.19.cloned.1.call-done = f32[24,768]{1,0:T(8,128)} async-done(((f32[768,768]{1,0:T(8,128)}), f32[24,768]{1,0:T(8,128)}) %reduce-scatter.19.cloned.1.call-update) | async-done | bytes 73744 | tf_op jit(solution)/shard_map/reduce_scatter | solution.py:343
  2898.0 104.7 %reduce-scatter.21.cloned.1.call-done = f32[24,768]{1,0:T(8,128)} async-done(((f32[768,768]{1,0:T(8,128)}), f32[24,768]{1,0:T(8,128)}) %reduce-scatter.21.cloned.1.call-update) | async-done | bytes 73744 | tf_op jit(solution)/shard_map/reduce_scatter | solution.py:344
  (276 shorter events, 861.1 us)
Async XLA Ops:
  7.2 60.5 %all-gather.18.cloned.1.call-start = ((), (), s32[]{:S(2)}) async-start(), calls=%async_computation.12 | async-start | bytes 1216512 | tf_op jit(solution)/shard_map/all_gather | solution.py:215
  7.9 115.6 %all-gather.12.cloned.1.call-start = ((), (), s32[]{:S(2)}) async-start(), calls=%async_computation.9 | async-start | bytes 1216512 | tf_op jit(solution)/shard_map/all_gather | solution.py:216
  8.7 170.7 %all-gather.16.cloned.1.call-start = ((), (), s32[]{:S(2)}) async-start(), calls=%async_computation.11 | async-start | bytes 1216512 | tf_op jit(solution)/shard_map/all_gather | solution.py:214
  9.4 286.3 %all-gather.20.cloned.1.call-start = ((), (), s32[]{:S(2)}) async-start(), calls=%async_computation.13 | async-start | bytes 7864320 | tf_op jit(solution)/shard_map/all_gather | solution.py:235
  71.9 57.3 %copy-start.17 = (s32[2,1,2048]{2,1,0:T(1,128)S(1)}, s32[2,1,2048]{2,1,0:T(1,128)}, u32[]{:S(2)}) copy-start(s32[2,1,2048]{2,1,0:T(1,128)} %param.18) | copy-start | bytes 49156
  71.9 59.1 %copy-start.25 = (bf16[12,12]{1,0:T(8,128)(2,1)S(1)}, bf16[12,12]{1,0:T(8,128)(2,1)}, u32[]{:S(2)}) copy-start(bf16[12,12]{1,0:T(8,128)(2,1)} %param.26) | copy-start | bytes 868
  72.0 339.3 %all-gather.14.cloned.1.call-start = ((), (), s32[]{:S(2)}) async-start(), calls=%async_computation.10 | async-start | bytes 7864320 | tf_op jit(solution)/shard_map/all_gather | solution.py:236
  127.8 697.3 %all-gather.22.cloned.1.call-start = ((), (), s32[]{:S(2)}) async-start(), calls=%async_computation.14 | async-start | bytes 1216512 | tf_op jit(solution)/shard_map/all_gather | solution.py:217
  128.4 703.4 %all-gather.26.cloned.1.call-start = ((), (), s32[]{:S(2)}) async-start(), calls=%async_computation.16 | async-start | bytes 1327104 | tf_op jit(solution)/shard_map/all_gather | solution.py:224
  129.1 814.9 %all-gather.24.cloned.1.call-start = ((), (), s32[]{:S(2)}) async-start(), calls=%async_computation.15 | async-start | bytes 7864320 | tf_op jit(solution)/shard_map/all_gather | solution.py:261
  460.3 69.8 %copy-start.2 = (pred[512,2048]{1,0:T(8,128)(4,1)S(1)}, pred[512,2048]{1,0:T(8,128)(4,1)}, u32[]{:S(2)}) copy-start(pred[512,2048]{1,0:T(8,128)(4,1)} %fusion.202) | copy-start | bytes 3145732 | tf_op jit(solution)/shard_map/while
  591.6 34.0 %copy-start.34 = (s32[2]{0:T(128)S(1)}, s32[2]{0:T(128)}, u32[]{:S(2)}) copy-start(s32[2]{0:T(128)} %copy-done.33) | copy-start | bytes 28 | tf_op jit(solution)/shard_map/while
  652.1 69.8 %copy-start.2 = (pred[512,2048]{1,0:T(8,128)(4,1)S(1)}, pred[512,2048]{1,0:T(8,128)(4,1)}, u32[]{:S(2)}) copy-start(pred[512,2048]{1,0:T(8,128)(4,1)} %fusion.202) | copy-start | bytes 3145732 | tf_op jit(solution)/shard_map/while
  783.4 34.0 %copy-start.34 = (s32[2]{0:T(128)S(1)}, s32[2]{0:T(128)}, u32[]{:S(2)}) copy-start(s32[2]{0:T(128)} %copy-done.33) | copy-start | bytes 28 | tf_op jit(solution)/shard_map/while
  830.4 137.9 %all-gather.28.cloned.1.call-start = ((), (), s32[]{:S(2)}) async-start(), calls=%async_computation.17 | async-start | bytes 1327104 | tf_op jit(solution)/shard_map/all_gather | solution.py:225
  831.1 253.9 %all-gather.30.cloned.1.call-start = ((), (), s32[]{:S(2)}) async-start(), calls=%async_computation.26 | async-start | bytes 7864320 | tf_op jit(solution)/shard_map/all_gather | solution.py:270
  831.7 405.4 %reduce-scatter.11.cloned.1.call-start = ((), (), s32[]{:S(2)}) async-start(), calls=%async_computation.19 | async-start | bytes 7864320 | tf_op jit(solution)/shard_map/reduce_scatter | solution.py:278
  1085.0 35.8 %copy-start.29 = (bf16[768,768]{1,0:T(8,128)(2,1)S(1)}, bf16[768,768]{1,0:T(8,128)(2,1)}, u32[]{:S(2)}) copy-start(bf16[768,768]{1,0:T(8,128)(2,1)} %all-gather.26.cloned.1.call-done) | copy-start | bytes 3538948
  1128.0 222.6 %reduce-scatter.9.cloned.1.call-start = ((), (), s32[]{:S(2)}) async-start(), calls=%async_computation.18 | async-start | bytes 7864320 | tf_op jit(solution)/shard_map/reduce_scatter | solution.py:267
  1145.7 1324.9 %reduce-scatter.13.cloned.1.call-start = ((), (), s32[]{:S(2)}) async-start(), calls=%async_computation.20 | async-start | bytes 7864320 | tf_op jit(solution)/shard_map/reduce_scatter | solution.py:322
  1497.6 38.6 %copy-start.20 = (f32[2,12,12]{2,1,0:T(8,128)}, f32[2,12,12]{2,1,0:T(8,128)S(1)}, u32[]{:S(2)}) copy-start(f32[2,12,12]{2,1,0:T(8,128)S(1)} %fusion.234) | copy-start | bytes 3460 | tf_op jit(solution)/shard_map/while
  1647.3 52.7 %copy-start.22 = (f32[2,12,12]{2,1,0:T(8,128)S(1)}, f32[2,12,12]{2,1,0:T(8,128)}, u32[]{:S(2)}) copy-start(f32[2,12,12]{2,1,0:T(8,128)} %get-tuple-element.650) | copy-start | bytes 3460 | tf_op jit(solution)/shard_map/while
  1730.2 23.2 copy-start.23
  1993.9 38.6 %copy-start.20 = (f32[2,12,12]{2,1,0:T(8,128)}, f32[2,12,12]{2,1,0:T(8,128)S(1)}, u32[]{:S(2)}) copy-start(f32[2,12,12]{2,1,0:T(8,128)S(1)} %fusion.234) | copy-start | bytes 3460 | tf_op jit(solution)/shard_map/while
  2143.6 52.7 %copy-start.22 = (f32[2,12,12]{2,1,0:T(8,128)S(1)}, f32[2,12,12]{2,1,0:T(8,128)}, u32[]{:S(2)}) copy-start(f32[2,12,12]{2,1,0:T(8,128)} %get-tuple-element.650) | copy-start | bytes 3460 | tf_op jit(solution)/shard_map/while
  2226.5 23.2 copy-start.23
  2359.1 224.9 %reduce-scatter.15.cloned.1.call-start = ((), (), s32[]{:S(2)}) async-start(), calls=%async_computation.21 | async-start | bytes 7864320 | tf_op jit(solution)/shard_map/reduce_scatter | solution.py:325
  2359.8 329.7 %reduce-scatter.23.cloned.1.call-start = ((), (), s32[]{:S(2)}) async-start(), calls=%async_computation.25 | async-start | bytes 2433024 | tf_op jit(solution)/shard_map/reduce_scatter | solution.py:345
  2365.3 428.8 %reduce-scatter.17.cloned.1.call-start = ((), (), s32[]{:S(2)}) async-start(), calls=%async_computation.22 | async-start | bytes 2433024 | tf_op jit(solution)/shard_map/reduce_scatter | solution.py:342
  2370.5 527.5 %reduce-scatter.19.cloned.1.call-start = ((), (), s32[]{:S(2)}) async-start(), calls=%async_computation.23 | async-start | bytes 2433024 | tf_op jit(solution)/shard_map/reduce_scatter | solution.py:343
  2498.8 89.6 %all-to-all-start = ((bf16[8,96,1536]{2,1,0:T(8,128)(2,1)}), bf16[8,96,1536]{2,1,0:T(8,128)(2,1)}, u32[]{:S(2)}, u32[]{:S(2)}) async-start(bf16[8,96,1536]{2,1,0:T(8,128)(2,1)} %bitcast.354), calls=%async_computation.8 | async-start | bytes 4718592 | tf_op jit(solution)/shard_map/all_to_all | solution.py:14
  2503.2 499.4 %reduce-scatter.21.cloned.1.call-start = ((), (), s32[]{:S(2)}) async-start(), calls=%async_computation.24 | async-start | bytes 2433024 | tf_op jit(solution)/shard_map/reduce_scatter | solution.py:344
  (36 other events, 283.0 us)
Sparse Core Ops, SparseCore 0:
  10.8 56.8 all-gather.17
  70.5 53.0 all-gather.11
  126.3 53.0 all-gather.15
  181.4 114.2 all-gather.19
  297.7 113.5 all-gather.13
  413.9 52.2 all-gather.21
  468.1 22.9 all-gather.25
  830.5 113.5 all-gather.23
  945.9 22.2 all-gather.27
  969.6 115.3 all-gather.29
  1128.1 108.9 reduce-scatter.10
  1239.3 111.2 reduce-scatter.8
  2359.3 111.2 reduce-scatter.12
  2472.7 111.2 reduce-scatter.14
  2589.8 99.6 reduce-scatter.22
  2696.0 98.0 reduce-scatter.16
  2799.9 98.1 reduce-scatter.18
  2904.6 98.0 reduce-scatter.20
where the time goes:
time: 3020 us; the launch traced here: 3010 us
  waiting for transfers between devices  1320 us (44%)
  matrix products  1180 us (39%)
  other arithmetic  257 us (9%)
  local copies, waits for them, and re-layouts  103 us (3%)
  blocking collectives  83.1 us (3%)
  loops' own time  46.2 us (2%)
    dot_general x4, matrix products, mixed_scores(): jnp.einsum('gh,gqk->hqk', pre_mix, logits, preferred_element_type=jnp.flo...  209 us
    dot_general x2, matrix products, score_grads(): jnp.einsum('gh,hqk->gqk', post_mix, grad_post, preferred_element_type=jnp...  125 us
    all_gather x1, waiting for transfers between devices, per_device(): lax.all_gather(grad_out.reshape(micro, rows, width), 'tensor', axis=1, ti...  117 us
    all_gather x1, waiting for transfers between devices, per_device(): lax.all_gather(value_local, 'tensor', axis=1, tiled=True)  116 us
    all_gather x1, waiting for transfers between devices, per_device(): lax.all_gather(h_ffn.reshape(micro, rows, width), 'tensor', axis=1, tiled...  112 us
    all_gather x1, waiting for transfers between devices, per_device(): lax.all_gather(key_local, 'tensor', axis=1, tiled=True)  112 us
    reduce_scatter x1, waiting for transfers between devices, per_device(): lax.psum_scatter(partial_out.astype(jnp.bfloat16), 'tensor', scatter_dime...  110 us
    convert_element_type x2, other arithmetic, attend_back(): grad_mixed = (weights * (grad_weights - row_term)).astype(jnp.bfloat16)  105 us
  transfers between devices with their start and end apart: 19, of which 16 were waited for; matrix products, arithmetic and copies ran while one was open for 17% of the time, Pallas kernels for 0%

commit v1 on v0

v1 whole, which is shorter than its diff:
```python
import functools

import jax
import jax.numpy as jnp
from jax import lax
from jax.experimental import pallas as pl
from jax.experimental.pallas import tpu as pltpu
from jax.sharding import PartitionSpec as P

F32 = jnp.float32
BF16 = jnp.bfloat16
BLOCK = 128
TILE = 2 * BLOCK
AXES = ("dp", "tensor")


def matmul(left, right):
    return jnp.dot(left, right, preferred_element_type=F32)


def right_t(left, right):
    return lax.dot_general(left, right, (((1,), (1,)), ((), ())), preferred_element_type=F32)


def left_t(left, right):
    return lax.dot_general(left, right, (((0,), (0,)), ((), ())), preferred_element_type=F32)


def rms_scale(values):
    return lax.rsqrt(jnp.mean(values * values, axis=-1, keepdims=True) + 1e-06)


def rms_back(grad_norm, normed, scale, gain):
    scaled = grad_norm * gain
    return scale * (scaled - normed * jnp.mean(scaled * normed, axis=-1, keepdims=True))


def gelu_exact(values):
    return jax.nn.gelu(values, approximate=False)


def gelu_back(upper, grad):
    unused, pull = jax.vjp(gelu_exact, upper)
    return pull(grad)[0]


def send(x, to):
    nd, nt = lax.axis_size("dp"), lax.axis_size("tensor")
    pairs = []
    for d in range(nd):
        for t in range(nt):
            d2, t2 = to(d, t)
            pairs.append((d * nt + t, d2 * nt + t2))
    return lax.ppermute(x, AXES, pairs)


def by_shift(shift):
    nt = lax.axis_size("tensor")
    return lambda d, t: (d, (t + shift) % nt)


def by_bit(bit):
    return lambda d, t: (d ^ bit, t)


def gather(piece, bits):
    nt = lax.axis_size("tensor")
    have = {0: jnp.stack([piece] + [send(piece, by_shift(s)) for s in range(1, nt)])}
    for bit in bits:
        have.update({mask | bit: send(block, by_bit(bit)) for mask, block in have.items()})
    return [have[mask] for mask in range(len(have))]


def place_kernel(slot_of, *refs):
    pieces, out, sem = refs[:-2], refs[-2], refs[-1]
    copies = []
    for mask, piece in enumerate(pieces):
        for shift in range(piece.shape[0]):
            copies.append(
                pltpu.make_async_copy(piece.at[shift], out.at[slot_of(mask, shift)], sem)
            )
    for copy in copies:
        copy.start()
    for copy in copies:
        copy.wait()


def placed(pieces, tensor_first):
    nd, nt = len(pieces), pieces[0].shape[0]

    def slot_of(mask, shift):
        d = lax.axis_index("dp") ^ mask
        t = lax.rem(lax.axis_index("tensor") + (nt - shift), nt)
        return t * nd + d if tensor_first else d * nt + t

    return pl.pallas_call(
        functools.partial(place_kernel, slot_of),
        out_shape=jax.ShapeDtypeStruct((nd * nt,) + pieces[0].shape[1:], pieces[0].dtype),
        in_specs=[pl.BlockSpec(memory_space=pl.ANY)] * nd,
        out_specs=pl.BlockSpec(memory_space=pl.ANY),
        scratch_shapes=[pltpu.SemaphoreType.DMA],
        name="place",
    )(*pieces)


def pick(x, index, axis):
    return lax.dynamic_index_in_dim(x, index, axis, keepdims=False)


def sum_to_owner(x, bits):
    nt, nd = x.shape[:2]
    d, t = lax.axis_index("dp"), lax.axis_index("tensor")
    rest = x.shape[2:]
    names = [1 << k for k in range(nd.bit_length() - 1)][::-1]
    x = x.reshape((nt,) + (2,) * len(names) + rest)
    for bit in bits:
        axis = 1 + names.index(bit)
        names.remove(bit)
        mine = (d // bit) % 2
        got = send(pick(x, 1 - mine, axis), by_bit(bit))
        x = pick(x, mine, axis).astype(F32) + got.astype(F32)
        if names or nt > 1:
            x = x.astype(BF16)
    total = pick(x, t, 0).astype(F32)
    for shift in range(1, nt):
        total = total + send(pick(x, lax.rem(t + shift, nt), 0), by_shift(shift)).astype(F32)
    return total


def seat(turn):
    nt = lax.axis_size("tensor")
    t, core = lax.axis_index("tensor"), lax.axis_index("dp") % 2
    block = lax.rem(turn + t, nt)
    source = lax.rem(2 * (t // 2) + core + nt - turn, nt)
    return block, source


def turn_to(turn):
    nt = lax.axis_size("tensor")

    def to(d, t):
        block = (turn + t) % nt
        return d - d % 2 + block % 2, 2 * (block // 2) + d % 2

    return to


def turn_back(turn):
    nt = lax.axis_size("tensor")

    def to(d, t):
        return d - d % 2 + t % 2, (2 * (t // 2) + d % 2 + nt - turn) % nt

    return to


def to_sequences(x):
    micro, _, rows, width = x.shape
    nt = lax.axis_size("tensor")
    x = x.reshape(micro, rows // TILE, 2, BLOCK, width).transpose(0, 2, 1, 3, 4)
    x = x.reshape(nt, rows // 2, width)
    return [send(pick(x, seat(turn)[0], 0), turn_to(turn)) for turn in range(nt)]


def from_sequences(pieces, micro):
    nt = len(pieces)
    half, width = pieces[0].shape
    back = [send(piece, turn_back(turn)) for turn, piece in enumerate(pieces)]
    back = jnp.stack(back + back[:-1])
    t = lax.axis_index("tensor")
    x = lax.dynamic_slice_in_dim(back, lax.rem(nt - t, nt), nt, 0)
    x = x.reshape(micro, 2, half // BLOCK, BLOCK, width).transpose(0, 2, 1, 3, 4)
    return x.reshape(micro, 1, 2 * half, width)


def load_rows(core, own, other, scratch, sem):
    blocks = own.shape[0]
    copies = []
    for k in range(blocks):
        copies.append(pltpu.make_async_copy(own.at[k], scratch.at[1 + 2 * k + core], sem))
        copies.append(pltpu.make_async_copy(other.at[k], scratch.at[2 + 2 * k - core], sem))
    return copies


def row_mask(row_seg, col_seg, row_place, col_start):
    rows, cols = row_seg.shape[0], col_seg.shape[1]
    place = col_start + lax.broadcasted_iota(jnp.int32, (rows, cols), 1)
    allowed = (row_seg == col_seg) & (place <= row_place)
    return jnp.where(allowed, 0.0, -1e30).astype(F32)


def spread(row, heads, query):
    return [(query * row[h : h + 1, :]).astype(BF16) for h in range(heads)]


def forward_kernel(
    heads, groups, info, q_ref, ko, kx, vo, vx, seg_rows, seg_cols, pre_ref, post_ref,
    att_ref, u_ref, lse_ref, k_s, v_s, qp_s, s_s, m_s, l_s, u_s, sem,
):
    step = pl.program_id(0)
    core = info[0]
    blocks = ko.shape[0]

    @pl.when(step == 0)
    def _():
        copies = load_rows(core, ko, kx, k_s, sem) + load_rows(core, vo, vx, v_s, sem)
        for copy in copies:
            copy.start()
        k_s[0] = jnp.zeros(k_s.shape[1:], BF16)
        v_s[0] = jnp.zeros(v_s.shape[1:], BF16)
        for copy in copies:
            copy.wait()

    block = info[1 + step]
    tiles = info[1 + blocks + step]
    query = q_ref[...].astype(F32)
    for h, part in enumerate(spread(pre_ref, heads, query)):
        qp_s[h * BLOCK : (h + 1) * BLOCK, :] = part
    row_seg = seg_rows[0]
    row_place = block * BLOCK + lax.broadcasted_iota(jnp.int32, (BLOCK, 1), 0)
    m_s[...] = jnp.full(m_s.shape, -3e38, F32)
    l_s[...] = jnp.zeros(l_s.shape, F32)
    u_s[...] = jnp.zeros(u_s.shape, F32)
    size = heads // groups * BLOCK

    def scores(tile, carry):
        first = block + 2 - 2 * (tile + 1)
        keys = k_s[pl.ds(first, 2)].reshape(TILE, -1)
        col_seg = jnp.concatenate([seg_cols[first], seg_cols[first + 1]], axis=1)
        mask = row_mask(row_seg, col_seg, row_place, (first - 1) * BLOCK)
        for g in range(groups):
            rows = pl.ds(g * size, size)
            s = right_t(qp_s[rows, :], keys)
            s = (s.reshape(heads // groups, BLOCK, TILE) + mask[None]).reshape(size, TILE)
            s_s[tile, rows, :] = s
            m_s[rows, :] = jnp.maximum(m_s[rows, :], jnp.maximum(s[:, :BLOCK], s[:, BLOCK:]))
        return carry

    lax.fori_loop(0, tiles, scores, 0)
    m_s[...] = jnp.broadcast_to(jnp.max(m_s[...], axis=-1, keepdims=True), m_s.shape)

    def weigh(tile, carry):
        first = block + 2 - 2 * (tile + 1)
        values = v_s[pl.ds(first, 2)].reshape(TILE, -1)
        for g in range(groups):
            rows = pl.ds(g * size, size)
            top = m_s[rows, :]
            p = jnp.exp(s_s[tile, rows, :] - jnp.concatenate([top, top], axis=1))
            l_s[rows, :] += p[:, :BLOCK] + p[:, BLOCK:]
            u_s[rows, :] += matmul(p.astype(BF16), values)
        return carry

    lax.fori_loop(0, tiles, weigh, 0)
    att = jnp.zeros((BLOCK, att_ref.shape[1]), F32)
    for h in range(heads):
        rows = slice(h * BLOCK, (h + 1) * BLOCK)
        total = jnp.sum(l_s[rows, :], axis=-1, keepdims=True)
        lse_ref[0, rows, :] = m_s[rows, :] + jnp.log(total)
        u = u_s[rows, :] * (1.0 / total)
        u_ref[0, h] = u.astype(BF16)
        att = att + u * post_ref[h : h + 1, :]
    att_ref[...] = att.astype(BF16)


def whole(shape):
    return pl.BlockSpec(shape, lambda i, info: (0,) * len(shape))


ANY = pl.BlockSpec(memory_space=pl.ANY)


def attend(info, query, k_own, k_other, v_own, v_other, seg_rows, seg_cols, pre, post):
    heads, width = pre.shape
    blocks = k_own.shape[0]
    rows, stack = blocks * BLOCK, heads * BLOCK
    most = info.shape[0] and (1024 // BLOCK + 2) // 2
    groups = 4
    return pl.pallas_call(
        functools.partial(forward_kernel, heads, groups),
        grid_spec=pltpu.PrefetchScalarGridSpec(
            num_scalar_prefetch=1,
            grid=(blocks,),
            in_specs=[
                pl.BlockSpec((BLOCK, width), lambda i, info: (i, 0)),
                ANY, ANY, ANY, ANY,
                pl.BlockSpec((1, BLOCK, 1), lambda i, info: (i, 0, 0)),
                whole(seg_cols.shape), whole(pre.shape), whole(post.shape),
            ],
            out_specs=[
                pl.BlockSpec((BLOCK, width), lambda i, info: (i, 0)),
                pl.BlockSpec((1, heads, BLOCK, width), lambda i, info: (i, 0, 0, 0)),
                pl.BlockSpec((1, stack, BLOCK), lambda i, info: (i, 0, 0)),
            ],
            scratch_shapes=[
                pltpu.VMEM((2 * blocks + 1, BLOCK, width), BF16),
                pltpu.VMEM((2 * blocks + 1, BLOCK, width), BF16),
                pltpu.VMEM((stack, width), BF16),
                pltpu.VMEM((most, stack, TILE), F32),
                pltpu.VMEM((stack, BLOCK), F32),
                pltpu.VMEM((stack, BLOCK), F32),
                pltpu.VMEM((stack, width), F32),
                pltpu.SemaphoreType.DMA,
            ],
        ),
        out_shape=[
            jax.ShapeDtypeStruct((rows, width), BF16),
            jax.ShapeDtypeStruct((blocks, heads, BLOCK, width), BF16),
            jax.ShapeDtypeStruct((blocks, stack, BLOCK), F32),
        ],
        compiler_params=pltpu.CompilerParams(vmem_limit_bytes=60 << 20),
        name="attend",
    )(info, query, k_own, k_other, v_own, v_other, seg_rows, seg_cols, pre, post)


def backward_kernel(
    heads, groups, info, q_ref, g_ref, u_ref, lse_ref, ko, kx, vo, vx, seg_rows, seg_cols, pre_ref, post_ref,
    dq_ref, dk_ref, dv_ref, dpre_ref, dpost_ref,
    k_s, v_s, dk_s, dv_s, qp_s, gp_s, d_s, t_s, sem,
):
    step = pl.program_id(0)
    core = info[0]
    blocks = ko.shape[0]

    @pl.when(step == 0)
    def _():
        copies = load_rows(core, ko, kx, k_s, sem) + load_rows(core, vo, vx, v_s, sem)
        for copy in copies:
            copy.start()
        k_s[0] = jnp.zeros(k_s.shape[1:], BF16)
        v_s[0] = jnp.zeros(v_s.shape[1:], BF16)
        dk_s[...] = jnp.zeros(dk_s.shape, F32)
        dv_s[...] = jnp.zeros(dv_s.shape, F32)
        dpre_ref[...] = jnp.zeros(dpre_ref.shape, F32)
        dpost_ref[...] = jnp.zeros(dpost_ref.shape, F32)
        for copy in copies:
            copy.wait()

    block = info[1 + step]
    tiles = info[1 + blocks + step]
    query = q_ref[...].astype(F32)
    grad = g_ref[...].astype(F32)
    for h in range(heads):
        rows = slice(h * BLOCK, (h + 1) * BLOCK)
        qp_s[rows, :] = (query * pre_ref[h : h + 1, :]).astype(BF16)
        gain = post_ref[h : h + 1, :]
        gp_s[rows, :] = (grad * gain).astype(BF16)
        both = grad * u_ref[0, h].astype(F32)
        d_s[rows, :] = jnp.broadcast_to(jnp.sum(both * gain, axis=-1, keepdims=True), (BLOCK, BLOCK))
        dpost_ref[h] += jnp.sum(both.reshape(BLOCK // 8, 8, -1), axis=0)
    row_seg = seg_rows[0]
    row_place = block * BLOCK + lax.broadcasted_iota(jnp.int32, (BLOCK, 1), 0)
    t_s[...] = jnp.zeros(t_s.shape, F32)
    size = heads // groups * BLOCK

    def tile_step(tile, carry):
        first = block + 2 - 2 * (tile + 1)
        keys = k_s[pl.ds(first, 2)].reshape(TILE, -1)
        values = v_s[pl.ds(first, 2)].reshape(TILE, -1)
        col_seg = jnp.concatenate([seg_cols[first], seg_cols[first + 1]], axis=1)
        mask = row_mask(row_seg, col_seg, row_place, (first - 1) * BLOCK)
        dk = jnp.zeros((TILE, keys.shape[1]), F32)
        dv = jnp.zeros((TILE, keys.shape[1]), F32)
        for g in range(groups):
            rows = pl.ds(g * size, size)
            s = right_t(qp_s[rows, :], keys)
            s = (s.reshape(heads // groups, BLOCK, TILE) + mask[None]).reshape(size, TILE)
            top = lse_ref[0, rows, :]
            p = jnp.exp(s - jnp.concatenate([top, top], axis=1))
            dw = right_t(gp_s[rows, :], values)
            term = d_s[rows, :]
            ds = (p * (dw - jnp.concatenate([term, term], axis=1))).astype(BF16)
            t_s[rows, :] += matmul(ds, keys)
            dv = dv + left_t(p.astype(BF16), gp_s[rows, :])
            dk = dk + left_t(ds, qp_s[rows, :])
        dk_s[pl.ds(first, 2)] += dk.reshape(2, BLOCK, -1)
        dv_s[pl.ds(first, 2)] += dv.reshape(2, BLOCK, -1)
        return carry

    lax.fori_loop(0, tiles, tile_step, 0)
    dq = jnp.zeros(query.shape, F32)
    for h in range(heads):
        part = t_s[h * BLOCK : (h + 1) * BLOCK, :]
        dq = dq + part * pre_ref[h : h + 1, :]
        dpre_ref[h] += jnp.sum((query * part).reshape(BLOCK // 8, 8, -1), axis=0)
    dq_ref[...] = dq.astype(BF16)

    @pl.when(step == blocks - 1)
    def _():
        for k in range(blocks):
            for part in range(2):
                place = 1 + 2 * k + (core if part == 0 else 1 - core)
                dk_ref[part, k] = dk_s[place].astype(BF16)
                dv_ref[part, k] = dv_s[place].astype(BF16)


def attend_back(info, query, grad, u, lse, k_own, k_other, v_own, v_other, seg_rows, seg_cols, pre, post):
    heads, width = pre.shape
    blocks = k_own.shape[0]
    rows, stack = blocks * BLOCK, heads * BLOCK
    groups = 4
    return pl.pallas_call(
        functools.partial(backward_kernel, heads, groups),
        grid_spec=pltpu.PrefetchScalarGridSpec(
            num_scalar_prefetch=1,
            grid=(blocks,),
            in_specs=[
                pl.BlockSpec((BLOCK, width), lambda i, info: (i, 0)),
                pl.BlockSpec((BLOCK, width), lambda i, info: (i, 0)),
                pl.BlockSpec((1, heads, BLOCK, width), lambda i, info: (i, 0, 0, 0)),
                pl.BlockSpec((1, stack, BLOCK), lambda i, info: (i, 0, 0)),
                ANY, ANY, ANY, ANY,
                pl.BlockSpec((1, BLOCK, 1), lambda i, info: (i, 0, 0)),
                whole(seg_cols.shape), whole(pre.shape), whole(post.shape),
            ],
            out_specs=[
                pl.BlockSpec((BLOCK, width), lambda i, info: (i, 0)),
                whole((2, blocks, BLOCK, width)),
                whole((2, blocks, BLOCK, width)),
                whole((heads, 8, width)),
                whole((heads, 8, width)),
            ],
            scratch_shapes=[
                pltpu.VMEM((2 * blocks + 1, BLOCK, width), BF16),
                pltpu.VMEM((2 * blocks + 1, BLOCK, width), BF16),
                pltpu.VMEM((2 * blocks + 1, BLOCK, width), F32),
                pltpu.VMEM((2 * blocks + 1, BLOCK, width), F32),
                pltpu.VMEM((stack, width), BF16),
                pltpu.VMEM((stack, width), BF16),
                pltpu.VMEM((stack, BLOCK), F32),
                pltpu.VMEM((stack, width), F32),
                pltpu.SemaphoreType.DMA,
            ],
        ),
        out_shape=[
            jax.ShapeDtypeStruct((rows, width), BF16),
            jax.ShapeDtypeStruct((2, blocks, BLOCK, width), BF16),
            jax.ShapeDtypeStruct((2, blocks, BLOCK, width), BF16),
            jax.ShapeDtypeStruct((heads, 8, width), F32),
            jax.ShapeDtypeStruct((heads, 8, width), F32),
        ],
        compiler_params=pltpu.CompilerParams(vmem_limit_bytes=62 << 20),
        name="attend_back",
    )(info, query, grad, u, lse, k_own, k_other, v_own, v_other, seg_rows, seg_cols, pre, post)


def per_device(
    tokens, segments, w_query, w_key, w_value, w_out, norm_attn, norm_ffn, pre_mix, post_mix, w_up, w_down, out_grad,
):
    micro, _, rows, width = tokens.shape
    nd, nt = lax.axis_size("dp"), lax.axis_size("tensor")
    heads = pre_mix.shape[0]
    head_width = width // heads
    length = rows * nt
    count = length // 2
    blocks = count // BLOCK
    share = w_query.shape[0]
    bits = [1 << k for k in range(nd.bit_length() - 1)]
    d, t = lax.axis_index("dp"), lax.axis_index("tensor")
    core = d % 2

    gains = jnp.concatenate([norm_attn, norm_ffn, jnp.zeros((width - 2 * share,), BF16)])[None]
    gains = jnp.concatenate([gains, jnp.zeros((7, width), BF16)])
    bundle = jnp.concatenate([w_query, w_key, w_value, w_out, gains])
    order = bits[1:][::-1] + bits[:1]
    everything = placed(gather(bundle, order), False)
    all_query, all_key, all_value, all_out = (
        everything[:, k * share : (k + 1) * share].reshape(width, width) for k in range(4)
    )
    gain_attn = everything[:, 4 * share, :share].reshape(width).astype(F32)
    gain_ffn = everything[:, 4 * share, share : 2 * share].reshape(width).astype(F32)
    all_up = placed(gather(w_up, order), True).reshape(nt, width, -1)
    all_down = placed(gather(w_down, bits[1:] + bits[:1]), True).reshape(nt, width, -1)

    token_turns = to_sequences(tokens)
    grad_turns = to_sequences(out_grad)
    segs = segments.reshape(micro, length)
    segs = jnp.where(t % 2 == core, segs, send(segs, by_bit(1)))
    segs = pick(segs, t // 2, 0)
    sources = jnp.stack([seat(turn)[1] for turn in range(nt)])
    per_turn = blocks // nt
    block_ids = (2 * (sources[:, None] * per_turn + jnp.arange(per_turn)) + core).reshape(blocks)
    block_segs = segs.reshape(2 * blocks, BLOCK)
    starts = jnp.sum(segs[None, :] < block_segs[:, :1], axis=1) // BLOCK
    tiles = (jnp.arange(2 * blocks) + 2 - starts) // 2
    info = jnp.concatenate([core[None], block_ids, tiles[block_ids]]).astype(jnp.int32)
    seg_rows = block_segs[block_ids][:, :, None]
    seg_cols = jnp.concatenate([jnp.full((1, BLOCK), -1, jnp.int32), block_segs])[:, None, :]

    def by_lane(mix):
        return jnp.repeat(mix.astype(F32), head_width, axis=1)

    pre = by_lane(pre_mix.T) * head_width ** (-0.5)
    post = by_lane(post_mix)

    inputs = jnp.concatenate(token_turns).astype(F32)
    grad_out = jnp.concatenate(grad_turns)
    scale_attn = rms_scale(inputs)
    normed_attn = inputs * scale_attn
    h_attn = (normed_attn * gain_attn).astype(BF16)
    query = matmul(h_attn, all_query).astype(BF16)
    k_turn = matmul(h_attn, all_key).astype(BF16)
    v_turn = matmul(h_attn, all_value).astype(BF16)

    by_place = jnp.argsort(block_ids)
    in_turns = block_ids // 2

    def ordered(x):
        return x.reshape(blocks, BLOCK, width)[by_place]

    def turned(x):
        return x[in_turns].reshape(count, width)

    k_own, v_own = ordered(k_turn), ordered(v_turn)
    k_other, v_other = send(k_own, by_bit(1)), send(v_own, by_bit(1))
    attended, u, lse = attend(info, query, k_own, k_other, v_own, v_other, seg_rows, seg_cols, pre, post)

    after_attn = inputs + matmul(attended, all_out)
    scale_ffn = rms_scale(after_attn)
    normed_ffn = after_attn * scale_ffn
    h_ffn = (normed_ffn * gain_ffn).astype(BF16)
    upper = [matmul(h_ffn, all_up[k]) for k in range(nt)]
    hidden = [gelu_exact(up).astype(BF16) for up in upper]
    output = after_attn + sum(right_t(hidden[k], all_down[k]) for k in range(nt))
    d_hidden = [gelu_back(upper[k], matmul(grad_out, all_down[k])).astype(BF16) for k in range(nt)]
    grad_h_ffn = sum(right_t(d_hidden[k], all_up[k]) for k in range(nt))
    grad_up = jnp.stack([left_t(h_ffn, d_hidden[k]).astype(BF16) for k in range(nt)])
    grad_down = jnp.stack([left_t(grad_out, hidden[k]).astype(BF16) for k in range(nt)])
    grad_gain_ffn = jnp.sum(grad_h_ffn * normed_ffn, axis=0)
    grad_after = grad_out.astype(F32) + rms_back(grad_h_ffn, normed_ffn, scale_ffn, gain_ffn)
    grad_branch = grad_after.astype(BF16)
    grad_w_out = left_t(attended, grad_branch)
    grad_attended = right_t(grad_branch, all_out).astype(BF16)

    out_turns = jnp.split(output.astype(BF16), nt)
    out = from_sequences(out_turns, micro)
    part_up = sum_to_owner(grad_up.reshape(nt, nd, -1, grad_up.shape[2]), bits)
    part_down = sum_to_owner(grad_down.reshape(nt, nd, -1, grad_down.shape[2]), bits[:1] + bits[1:][::-1])

    grad_query, grad_key, grad_value, d_pre, d_post = attend_back(
        info, query, grad_attended, u, lse, k_own, k_other, v_own, v_other, seg_rows, seg_cols, pre, post
    )
    grad_key = turned((grad_key[0].astype(F32) + send(grad_key[1], by_bit(1)).astype(F32)).astype(BF16))
    grad_value = turned((grad_value[0].astype(F32) + send(grad_value[1], by_bit(1)).astype(F32)).astype(BF16))

    grad_h_attn = (
        right_t(grad_query, all_query) + right_t(grad_key, all_key) + right_t(grad_value, all_value)
    )
    grad_gain_attn = jnp.sum(grad_h_attn * normed_attn, axis=0)
    grad_tokens = grad_after + rms_back(grad_h_attn, normed_attn, scale_attn, gain_attn)
    d_tokens = from_sequences(jnp.split(grad_tokens.astype(BF16), nt), micro).astype(F32)

    grads = [left_t(h_attn, grad_query), left_t(h_attn, grad_key), left_t(h_attn, grad_value), grad_w_out]
    grads = jnp.stack([g.astype(BF16).reshape(nd, nt, share, width) for g in grads], axis=2)
    owned = sum_to_owner(grads.transpose(1, 0, 2, 3, 4), bits)

    d_pre = d_pre.reshape(heads, 8, heads, head_width).sum((1, 3)).T * head_width ** (-0.5)
    d_post = d_post.reshape(heads, 8, heads, head_width).sum((1, 3))
    small = jnp.concatenate([grad_gain_attn, grad_gain_ffn, d_pre.reshape(-1), d_post.reshape(-1)])
    small = lax.psum(small, AXES)
    place = (d * nt + t) * share
    return (
        out,
        d_tokens,
        owned[0],
        owned[1],
        owned[2],
        owned[3],
        lax.dynamic_slice_in_dim(small, place, share),
        lax.dynamic_slice_in_dim(small, width + place, share),
        small[2 * width : 2 * width + heads * heads].reshape(heads, heads),
        small[2 * width + heads * heads :].reshape(heads, heads),
        part_up,
        part_down,
    )


def solution(mesh):
    both = P(("dp", "tensor"), None)
    gain = P(("dp", "tensor"))
    data = P(None, "dp", "tensor", None)
    ffn = P("dp", "tensor")
    return jax.shard_map(
        per_device,
        mesh=mesh,
        in_specs=(data, P(None, "dp", None), both, both, both, both, gain, gain, P(), P(), ffn, ffn, data),
        out_specs=(data, data, both, both, both, both, gain, gain, P(), P(), ffn, ffn),
        check_vma=False,
    )
```

time: 3020 us -> 1160 us (0.38)
  waiting for transfers between devices: 1320 us -> 108 us
  matrix products: 1180 us -> 129 us
  Pallas kernels: 0 us -> 599 us
  other arithmetic: 257 us -> 40.9 us
  starting transfers between devices: 5.31 us -> 132 us
  loops' own time: 46.2 us -> 0 us
  blocking collectives: 83.1 us -> 36.9 us
    dot_general x36 -> x12, matrix products: 1120 us -> 60 us  [matmul(): return jnp.dot(left, right, preferred_element_type=F32)]
    reduce_scatter x8 -> x0, waiting for transfers between devices: 736 us -> none  [the longest x1 110 us: per_device(): lax.psum_scatter(partial_out.astype(jnp.bfloat16), 'tensor', scatter_dime...]
    pallas_call x0 -> x5, Pallas kernels: none -> 599 us  [the longest x3 444 us: placed(): pl.pallas_call(functools.partial(place_kernel, slot_of), out_shape=jax.Sh...]
    all_gather x10 -> x0, waiting for transfers between devices: 579 us -> none  [the longest x1 117 us: per_device(): lax.all_gather(grad_out.reshape(micro, rows, width), 'tensor', axis=1, ti...]
    ppermute x0 -> x69, starting transfers between devices: none -> 132 us  [send(): return lax.ppermute(x, AXES, pairs)]
    ppermute x0 -> x69, waiting for transfers between devices: none -> 108 us  [send(): return lax.ppermute(x, AXES, pairs)]
    convert_element_type x8 -> x19, other arithmetic: 120 us -> 23.3 us  [the longest x9 10.7 us: sum_to_owner(): x = x.astype(BF16)]
    unnamed x2 -> x0, blocking collectives: 83.1 us -> none
  transfers between devices with their start and end apart: 19 -> 69, of which waited for: 16 -> 12; matrix products, arithmetic and copies ran while one was open for 17% -> 14% of each run, Pallas kernels for 0% -> 39%
where the time goes in v1:
time: 1160 us; the launch traced here: 1150 us
  Pallas kernels  599 us (52%)
  starting transfers between devices  132 us (11%)
  matrix products  129 us (11%)
  waiting for transfers between devices  108 us (9%)
  local copies, waits for them, and re-layouts  104 us (9%)
  other arithmetic  40.9 us (4%)
  blocking collectives  36.9 us (3%)
    pallas_call x3, Pallas kernels, placed(): pl.pallas_call(functools.partial(place_kernel, slot_of), out_shape=jax.Sh...  444 us
    ppermute x69, starting transfers between devices, send(): return lax.ppermute(x, AXES, pairs)  132 us
    ppermute x69, waiting for transfers between devices, send(): return lax.ppermute(x, AXES, pairs)  108 us
    pallas_call x1, Pallas kernels, attend_back(): pl.pallas_call(functools.partial(backward_kernel, heads, groups), grid_sp...  105 us
    dot_general x12, matrix products, matmul(): return jnp.dot(left, right, preferred_element_type=F32)  60 us
    pallas_call x1, Pallas kernels, attend(): pl.pallas_call(functools.partial(forward_kernel, heads, groups), grid_spe...  50.6 us
    psum x1, blocking collectives, per_device(): small = lax.psum(small, AXES)  36.9 us
    dot_general x12, matrix products, left_t(): lax.dot_general(left, right, (((0,), (0,)), ((), ())), preferred_element_...  36.4 us
  transfers between devices with their start and end apart: 69, of which 12 were waited for; matrix products, arithmetic and copies ran while one was open for 14% of the time, Pallas kernels for 39%

profile of v1, /device:TPU:0, one launch (start us, length us, event | category | flops | bytes accessed | tf_op | source)
XLA Modules:
  0.0 1151.9 jit_solution(15825657198933418760)
XLA Ops:
  36.6 7.0 collective-permute-start.3
  43.5 4.4 collective-permute-done.6
  52.2 18.6 %collective-permute-start.44 = (bf16[256,768]{0,1:T(8,128)(2,1)}, bf16[256,768]{0,1:T(8,128)(2,1)S(1)}, u32[]{:S(2)}, u32[]{:S(2)}) collective-permute-start(bf16[256,768]{0,1:T(8,128)(2,1)} %get-tuple-element.95), channel_id=1, source_target_pairs={{0,6},{1,0},{2,4},{3,2},{4,7},{5,1},{6,5},{7,3},{8,14},{9,8},{10,1... | collective-permute-start | bytes 1179656 | tf_op jit(solution)/shard_map/ppermute | solution.py:54
  72.5 17.4 %collective-permute-done.2 = bf16[256,768]{0,1:T(8,128)(2,1)S(1)} collective-permute-done((bf16[256,768]{0,1:T(8,128)(2,1)}, bf16[256,768]{0,1:T(8,128)(2,1)S(1)}, u32[]{:S(2)}, u32[]{:S(2)}) %collective-permute-start.2) | collective-permute-done | bytes 393248 | tf_op jit(solution)/shard_map/ppermute | solution.py:54
  89.9 4.8 collective-permute-start.41
  98.7 16.4 %collective-permute-done.43 = bf16[256,768]{0,1:T(8,128)(2,1)S(1)} collective-permute-done((bf16[256,768]{0,1:T(8,128)(2,1)}, bf16[256,768]{0,1:T(8,128)(2,1)S(1)}, u32[]{:S(2)}, u32[]{:S(2)}) %collective-permute-start.43) | collective-permute-done | bytes 393248 | tf_op jit(solution)/shard_map/ppermute | solution.py:54
  119.9 12.1 %collective-permute-start.14 = (bf16[4,104,768]{2,1,0:T(8,128)(2,1)}, bf16[4,104,768]{2,1,0:T(8,128)(2,1)}, u32[]{:S(2)}, u32[]{:S(2)}) collective-permute-start(bf16[4,104,768]{2,1,0:T(8,128)(2,1)} %collective-permute-done.13.refs_6_), channel_id=1, source_target_pairs={{0,4},{1,5},{2,6},{3,7},{4,0},{5,1},{6,2},{7,3},{8,12},{9,13},{10,... | collective-permute-start | bytes 1916936 | tf_op jit(solution)/shard_map/ppermute | solution.py:54
  135.0 4.8 collective-permute-start.30
  148.3 156.0 %place.3 = bf16[32,104,768]{2,1,0:T(8,128)(2,1)} custom-call(bf16[4,104,768]{2,1,0:T(8,128)(2,1)} %copy-done.21, bf16[4,104,768]{2,1,0:T(8,128)(2,1)} %collective-permute-done.8.refs_1_, bf16[4,104,768]{2,1,0:T(8,128)(2,1)} %collective-permute-done.9.refs_2_, bf16[4,104,768]{2,1,0:T(8,128)(2,1)} %collective-permute-done.10.refs_3_, ...), custom_call_target="tpu_custom_call" | custom-call | tf_op jit(solution)/shard_map/place/pallas_call | solution.py:96
  305.7 4.2 fusion.69
  316.1 5.2 collective-permute-done.25.refs_6_
  337.5 144.0 %place.5 = bf16[32,96,768]{2,1,0:T(8,128)(2,1)} custom-call(bf16[4,96,768]{2,1,0:T(8,128)(2,1)} %copy-done.22, bf16[4,96,768]{2,1,0:T(8,128)(2,1)} %copy-done.67, bf16[4,96,768]{2,1,0:T(8,128)(2,1)} %collective-permute-done.31.refs_2_, bf16[4,96,768]{2,1,0:T(8,128)(2,1)} %collective-permute-done.32.refs_3_, ...), custom_call_target="tpu_custom_call" | custom-call | tf_op jit(solution)/shard_map/place/pallas_call | solution.py:96
  481.6 144.1 %place.4 = bf16[32,96,768]{2,1,0:T(8,128)(2,1)} custom-call(bf16[4,96,768]{2,1,0:T(8,128)(2,1)} %copy-done.23, bf16[4,96,768]{2,1,0:T(8,128)(2,1)} %collective-permute-done.20.refs_1_, bf16[4,96,768]{2,1,0:T(8,128)(2,1)} %collective-permute-done.21.refs_2_, bf16[4,96,768]{2,1,0:T(8,128)(2,1)} %collective-permute-done.22.refs_3_, ...), custom_call_target="tpu_custom_call" | custom-call | tf_op jit(solution)/shard_map/place/pallas_call | solution.py:96
  625.7 4.7 fusion.71
  633.3 4.3 convolution_convert_fusion.3.q_ref
  637.7 50.6 %attend.1 = (bf16[1024,768]{1,0:T(8,128)(2,1)}, bf16[8,12,128,768]{3,2,1,0:T(8,128)(2,1)}, f32[8,1536,128]{2,1,0:T(8,128)}) custom-call(s32[17]{0:T(128)} %pad_add_fusion.info, bf16[1024,768]{1,0:T(8,128)(2,1)} %convolution_convert_fusion.3.q_ref, bf16[8,128,768]{2,1,0:T(8,128)(2,1)} %copy-done.4, bf16[8,128,768]{2,1,0:T(8,128)(2,1)} %collective-permute-done.15.kx, ...), custom_call_target="tpu_custom_call" | custom-call | tf_op jit(solution)/shard_map/attend/pallas_call | solution.py:278
  695.1 9.7 add_convert_fusion.3
  717.6 9.7 add_convert_fusion.2
  738.4 9.8 add_convert_fusion.1
  759.2 10.0 add_convert_fusion
  790.5 104.6 %attend_back.1 = (bf16[1024,768]{1,0:T(8,128)(2,1)}, bf16[2,8,128,768]{3,2,1,0:T(8,128)(2,1)}, bf16[2,8,128,768]{3,2,1,0:T(8,128)(2,1)}, f32[12,8,768]{2,1,0:T(8,128)}, f32[12,8,768]{2,1,0:T(8,128)}) custom-call(s32[17]{0:T(128)} %pad_add_fusion.info, bf16[1024,768]{1,0:T(8,128)(2,1)} %convolution_convert_fusion.3.q_ref, ...), custom_call_target="tpu_custom_call" | custom-call | tf_op jit(solution)/shard_map/attend_back/pallas_call | solution.py:401
  899.0 6.7 collective-permute-start.40
  905.8 4.2 collective-permute-start.39
  913.5 4.5 collective-permute-start.37
  918.0 4.6 fusion.86
  959.7 4.9 fusion.13
  965.3 36.9 %psum.7 = f32[1824]{0:T(1024)} all-reduce(f32[1824]{0:T(1024)S(1)} %concatenate.33), channel_id=1, replica_groups=mesh['dp'=8,'tensor'=4] {'dp','tensor'}, use_global_device_ids=true, to_apply=%region_12.13 | all-reduce | flops 1824 | bytes 14592 | tf_op jit(solution)/shard_map/psum | solution.py:559
  1027.4 12.3 %collective-permute-done.48 = bf16[256,768]{0,1:T(8,128)(2,1)S(1)} collective-permute-done((bf16[256,768]{0,1:T(8,128)(2,1)S(1)}, bf16[256,768]{0,1:T(8,128)(2,1)S(1)}, u32[]{:S(2)}, u32[]{:S(2)}) %collective-permute-start.48) | collective-permute-done | bytes 393248 | tf_op jit(solution)/shard_map/ppermute | solution.py:54
  1039.8 17.3 %collective-permute-done.49 = bf16[256,768]{0,1:T(8,128)(2,1)S(1)} collective-permute-done((bf16[256,768]{0,1:T(8,128)(2,1)S(1)}, bf16[256,768]{0,1:T(8,128)(2,1)S(1)}, u32[]{:S(2)}, u32[]{:S(2)}) %collective-permute-start.49) | collective-permute-done | bytes 393248 | tf_op jit(solution)/shard_map/ppermute | solution.py:54
  1070.2 18.7 %collective-permute-done.58 = bf16[4,2,96,768]{3,2,0,1:T(8,128)(2,1)S(1)} collective-permute-done((bf16[4,2,96,768]{3,2,0,1:T(8,128)(2,1)S(1)}, bf16[4,2,96,768]{3,2,0,1:T(8,128)(2,1)S(1)}, u32[]{:S(2)}, u32[]{:S(2)}) %collective-permute-start.58) | collective-permute-done | bytes 1179680 | tf_op jit(solution)/shard_map/ppermute | solution.py:54
  1137.1 7.4 collective-permute-done.67
  1145.3 5.5 collective-permute-done.55
  (476 shorter events, 284.2 us)
Async XLA Ops:
  36.6 35.2 %collective-permute-start.3 = (bf16[256,768]{0,1:T(8,128)(2,1)}, bf16[256,768]{0,1:T(8,128)(2,1)S(1)}, u32[]{:S(2)}, u32[]{:S(2)}) collective-permute-start(bf16[256,768]{0,1:T(8,128)(2,1)} %get-tuple-element.100), channel_id=1, source_target_pairs={{0,6},{1,0},{2,4},{3,2},{4,7},{5,1},{6,5},{7,3},{8,14},{9,8},{10,1... | collective-permute-start | bytes 1179656 | tf_op jit(solution)/shard_map/ppermute | solution.py:54
  47.9 42.0 %collective-permute-start.2 = (bf16[256,768]{0,1:T(8,128)(2,1)}, bf16[256,768]{0,1:T(8,128)(2,1)S(1)}, u32[]{:S(2)}, u32[]{:S(2)}) collective-permute-start(bf16[256,768]{0,1:T(8,128)(2,1)} %get-tuple-element.101), channel_id=1, source_target_pairs={{0,2},{1,6},{2,0},{3,4},{4,3},{5,7},{6,1},{7,5},{8,10},{9,14},{10,... | collective-permute-start | bytes 1179656 | tf_op jit(solution)/shard_map/ppermute | solution.py:54
  47.9 42.0 %collective-permute-start.1 = (bf16[256,768]{0,1:T(8,128)(2,1)}, bf16[256,768]{0,1:T(8,128)(2,1)}, u32[]{:S(2)}, u32[]{:S(2)}) collective-permute-start(bf16[256,768]{0,1:T(8,128)(2,1)} %get-tuple-element.102), channel_id=1, source_target_pairs={{0,4},{1,2},{2,6},{3,0},{4,5},{5,3},{6,7},{7,1},{8,12},{9,10},{10,... | collective-permute-start | bytes 1179656 | tf_op jit(solution)/shard_map/ppermute | solution.py:54
  49.4 46.9 %collective-permute-start.11 = (bf16[4,104,768]{2,1,0:T(8,128)(2,1)S(1)}, bf16[4,104,768]{2,1,0:T(8,128)(2,1)}, u32[]{:S(2)}, u32[]{:S(2)}) collective-permute-start(bf16[4,104,768]{2,1,0:T(8,128)(2,1)S(1)} %pad_maximum_fusion.4.refs_0_), channel_id=1, source_target_pairs={{0,16},{1,17},{2,18},{3,19},{4,20},{5,21},{6,22},{7,23},{8,24},{9,... | collective-permute-start | bytes 1916936 | tf_op jit(solution)/shard_map/ppermute | solution.py:54
  52.2 42.6 %collective-permute-start.44 = (bf16[256,768]{0,1:T(8,128)(2,1)}, bf16[256,768]{0,1:T(8,128)(2,1)S(1)}, u32[]{:S(2)}, u32[]{:S(2)}) collective-permute-start(bf16[256,768]{0,1:T(8,128)(2,1)} %get-tuple-element.95), channel_id=1, source_target_pairs={{0,6},{1,0},{2,4},{3,2},{4,7},{5,1},{6,5},{7,3},{8,14},{9,8},{10,1... | collective-permute-start | bytes 1179656 | tf_op jit(solution)/shard_map/ppermute | solution.py:54
  71.8 43.3 %collective-permute-start.43 = (bf16[256,768]{0,1:T(8,128)(2,1)}, bf16[256,768]{0,1:T(8,128)(2,1)S(1)}, u32[]{:S(2)}, u32[]{:S(2)}) collective-permute-start(bf16[256,768]{0,1:T(8,128)(2,1)} %get-tuple-element.96), channel_id=1, source_target_pairs={{0,2},{1,6},{2,0},{3,4},{4,3},{5,7},{6,1},{7,5},{8,10},{9,14},{10,... | collective-permute-start | bytes 1179656 | tf_op jit(solution)/shard_map/ppermute | solution.py:54
  89.9 26.7 %collective-permute-start.42 = (bf16[256,768]{0,1:T(8,128)(2,1)}, bf16[256,768]{0,1:T(8,128)(2,1)}, u32[]{:S(2)}, u32[]{:S(2)}) collective-permute-start(bf16[256,768]{0,1:T(8,128)(2,1)} %get-tuple-element.97), channel_id=1, source_target_pairs={{0,4},{1,2},{2,6},{3,0},{4,5},{5,3},{6,7},{7,1},{8,12},{9,10},{10,... | collective-permute-start | bytes 1179656 | tf_op jit(solution)/shard_map/ppermute | solution.py:54
  89.9 26.7 %collective-permute-start.41 = (bf16[256,768]{0,1:T(8,128)(2,1)}, bf16[256,768]{0,1:T(8,128)(2,1)}, u32[]{:S(2)}, u32[]{:S(2)}) collective-permute-start(bf16[256,768]{0,1:T(8,128)(2,1)} %get-tuple-element.98), channel_id=1, source_target_pairs={{0,0},{1,4},{2,2},{3,6},{4,1},{5,5},{6,3},{7,7},{8,8},{9,12},{10,1... | collective-permute-start | bytes 1179656 | tf_op jit(solution)/shard_map/ppermute | solution.py:54
  119.7 25.5 %collective-permute-start.10 = (bf16[4,104,768]{2,1,0:T(8,128)(2,1)}, bf16[4,104,768]{2,1,0:T(8,128)(2,1)}, u32[]{:S(2)}, u32[]{:S(2)}) collective-permute-start(bf16[4,104,768]{2,1,0:T(8,128)(2,1)} %collective-permute-done.9.refs_2_), channel_id=1, source_target_pairs={{0,4},{1,5},{2,6},{3,7},{4,0},{5,1},{6,2},{7,3},{8,12},{9,13},{10,... | collective-permute-start | bytes 1916936 | tf_op jit(solution)/shard_map/ppermute | solution.py:54
  119.9 26.8 %collective-permute-start.14 = (bf16[4,104,768]{2,1,0:T(8,128)(2,1)}, bf16[4,104,768]{2,1,0:T(8,128)(2,1)}, u32[]{:S(2)}, u32[]{:S(2)}) collective-permute-start(bf16[4,104,768]{2,1,0:T(8,128)(2,1)} %collective-permute-done.13.refs_6_), channel_id=1, source_target_pairs={{0,4},{1,5},{2,6},{3,7},{4,0},{5,1},{6,2},{7,3},{8,12},{9,13},{10,... | collective-permute-start | bytes 1916936 | tf_op jit(solution)/shard_map/ppermute | solution.py:54
  133.4 170.8 %collective-permute-start.33 = (bf16[4,96,768]{2,1,0:T(8,128)(2,1)S(1)}, bf16[4,96,768]{2,1,0:T(8,128)(2,1)}, u32[]{:S(2)}, u32[]{:S(2)}) collective-permute-start(bf16[4,96,768]{2,1,0:T(8,128)(2,1)S(1)} %pad_maximum_fusion.6.refs_0_), channel_id=1, source_target_pairs={{0,16},{1,17},{2,18},{3,19},{4,20},{5,21},{6,22},{7,23},{8,24},{9,... | collective-permute-start | bytes 1769480 | tf_op jit(solution)/shard_map/ppermute | solution.py:54
  135.0 169.3 %collective-permute-start.30 = (bf16[4,96,768]{2,1,0:T(8,128)(2,1)S(1)}, bf16[4,96,768]{2,1,0:T(8,128)(2,1)S(1)}, u32[]{:S(2)}, u32[]{:S(2)}) collective-permute-start(bf16[4,96,768]{2,1,0:T(8,128)(2,1)S(1)} %pad_maximum_fusion.6.refs_0_), channel_id=1, source_target_pairs={{0,4},{1,5},{2,6},{3,7},{4,0},{5,1},{6,2},{7,3},{8,12},{9,13},{10,... | collective-permute-start | bytes 1769480 | tf_op jit(solution)/shard_map/ppermute | solution.py:54
  139.9 165.0 %collective-permute-start.23 = (bf16[4,96,768]{2,1,0:T(8,128)(2,1)S(1)}, bf16[4,96,768]{2,1,0:T(8,128)(2,1)}, u32[]{:S(2)}, u32[]{:S(2)}) collective-permute-start(bf16[4,96,768]{2,1,0:T(8,128)(2,1)S(1)} %pad_maximum_fusion.5.refs_0_), channel_id=1, source_target_pairs={{0,16},{1,17},{2,18},{3,19},{4,20},{5,21},{6,22},{7,23},{8,24},{9,... | collective-permute-start | bytes 1769480 | tf_op jit(solution)/shard_map/ppermute | solution.py:54
  145.2 166.0 %collective-permute-start.21 = (bf16[4,96,768]{2,1,0:T(8,128)(2,1)S(1)}, bf16[4,96,768]{2,1,0:T(8,128)(2,1)}, u32[]{:S(2)}, u32[]{:S(2)}) collective-permute-start(bf16[4,96,768]{2,1,0:T(8,128)(2,1)S(1)} %pad_maximum_fusion.5.refs_0_), channel_id=1, source_target_pairs={{0,8},{1,9},{2,10},{3,11},{4,12},{5,13},{6,14},{7,15},{8,0},{9,1},... | collective-permute-start | bytes 1769480 | tf_op jit(solution)/shard_map/ppermute | solution.py:54
  146.7 164.7 %collective-permute-start.35 = (bf16[4,96,768]{2,1,0:T(8,128)(2,1)}, bf16[4,96,768]{2,1,0:T(8,128)(2,1)}, u32[]{:S(2)}, u32[]{:S(2)}) collective-permute-start(bf16[4,96,768]{2,1,0:T(8,128)(2,1)} %collective-permute-done.31.refs_2_), channel_id=1, source_target_pairs={{0,16},{1,17},{2,18},{3,19},{4,20},{5,21},{6,22},{7,23},{8,24},{9,... | collective-permute-start | bytes 1769480 | tf_op jit(solution)/shard_map/ppermute | solution.py:54
  315.5 166.1 %collective-permute-start.24 = (bf16[4,96,768]{2,1,0:T(8,128)(2,1)}, bf16[4,96,768]{2,1,0:T(8,128)(2,1)}, u32[]{:S(2)}, u32[]{:S(2)}) collective-permute-start(bf16[4,96,768]{2,1,0:T(8,128)(2,1)} %collective-permute-done.23.refs_4_), channel_id=1, source_target_pairs={{0,4},{1,5},{2,6},{3,7},{4,0},{5,1},{6,2},{7,3},{8,12},{9,13},{10,... | collective-permute-start | bytes 1769480 | tf_op jit(solution)/shard_map/ppermute | solution.py:54
  315.8 165.9 %collective-permute-start.22 = (bf16[4,96,768]{2,1,0:T(8,128)(2,1)}, bf16[4,96,768]{2,1,0:T(8,128)(2,1)}, u32[]{:S(2)}, u32[]{:S(2)}) collective-permute-start(bf16[4,96,768]{2,1,0:T(8,128)(2,1)} %collective-permute-done.21.refs_2_), channel_id=1, source_target_pairs={{0,4},{1,5},{2,6},{3,7},{4,0},{5,1},{6,2},{7,3},{8,12},{9,13},{10,... | collective-permute-start | bytes 1769480 | tf_op jit(solution)/shard_map/ppermute | solution.py:54
  321.2 160.4 %collective-permute-start.26 = (bf16[4,96,768]{2,1,0:T(8,128)(2,1)}, bf16[4,96,768]{2,1,0:T(8,128)(2,1)}, u32[]{:S(2)}, u32[]{:S(2)}) collective-permute-start(bf16[4,96,768]{2,1,0:T(8,128)(2,1)} %collective-permute-done.25.refs_6_), channel_id=1, source_target_pairs={{0,4},{1,5},{2,6},{3,7},{4,0},{5,1},{6,2},{7,3},{8,12},{9,13},{10,... | collective-permute-start | bytes 1769480 | tf_op jit(solution)/shard_map/ppermute | solution.py:54
  329.8 307.9 %collective-permute-start.15 = (bf16[8,128,768]{2,1,0:T(8,128)(2,1)S(1)}, bf16[8,128,768]{2,1,0:T(8,128)(2,1)}, u32[]{:S(2)}, u32[]{:S(2)}) collective-permute-start(bf16[8,128,768]{2,1,0:T(8,128)(2,1)S(1)} %gather_fusion.1), channel_id=1, source_target_pairs={{0,4},{1,5},{2,6},{3,7},{4,0},{5,1},{6,2},{7,3},{8,12},{9,13},{10,... | collective-permute-start | bytes 4718600 | tf_op jit(solution)/shard_map/ppermute | solution.py:54
  330.4 307.3 %collective-permute-start.16 = (bf16[8,128,768]{2,1,0:T(8,128)(2,1)S(1)}, bf16[8,128,768]{2,1,0:T(8,128)(2,1)}, u32[]{:S(2)}, u32[]{:S(2)}) collective-permute-start(bf16[8,128,768]{2,1,0:T(8,128)(2,1)S(1)} %gather_fusion.2), channel_id=1, source_target_pairs={{0,4},{1,5},{2,6},{3,7},{4,0},{5,1},{6,2},{7,3},{8,12},{9,13},{10,... | collective-permute-start | bytes 4718600 | tf_op jit(solution)/shard_map/ppermute | solution.py:54
  899.0 44.2 %collective-permute-start.40 = (bf16[256,768]{0,1:T(8,128)(2,1)}, bf16[256,768]{0,1:T(8,128)(2,1)}, u32[]{:S(2)}, u32[]{:S(2)}) collective-permute-start(bf16[256,768]{0,1:T(8,128)(2,1)} %get-tuple-element.91), channel_id=1, source_target_pairs={{0,1},{1,5},{2,3},{3,7},{4,2},{5,6},{6,0},{7,4},{8,9},{9,13},{10,1... | collective-permute-start | bytes 1179656 | tf_op jit(solution)/shard_map/ppermute | solution.py:54
  905.8 36.1 %collective-permute-start.39 = (bf16[256,768]{0,1:T(8,128)(2,1)}, bf16[256,768]{0,1:T(8,128)(2,1)}, u32[]{:S(2)}, u32[]{:S(2)}) collective-permute-start(bf16[256,768]{0,1:T(8,128)(2,1)} %get-tuple-element.92), channel_id=1, source_target_pairs={{0,2},{1,6},{2,0},{3,4},{4,3},{5,7},{6,1},{7,5},{8,10},{9,14},{10,... | collective-permute-start | bytes 1179656 | tf_op jit(solution)/shard_map/ppermute | solution.py:54
  910.0 30.6 %collective-permute-start.38 = (bf16[256,768]{0,1:T(8,128)(2,1)}, bf16[256,768]{0,1:T(8,128)(2,1)}, u32[]{:S(2)}, u32[]{:S(2)}) collective-permute-start(bf16[256,768]{0,1:T(8,128)(2,1)} %get-tuple-element.93), channel_id=1, source_target_pairs={{0,3},{1,7},{2,1},{3,5},{4,0},{5,4},{6,2},{7,6},{8,11},{9,15},{10,... | collective-permute-start | bytes 1179656 | tf_op jit(solution)/shard_map/ppermute | solution.py:54
  913.5 25.0 %collective-permute-start.37 = (bf16[256,768]{0,1:T(8,128)(2,1)}, bf16[256,768]{0,1:T(8,128)(2,1)}, u32[]{:S(2)}, u32[]{:S(2)}) collective-permute-start(bf16[256,768]{0,1:T(8,128)(2,1)} %get-tuple-element.94), channel_id=1, source_target_pairs={{0,0},{1,4},{2,2},{3,6},{4,1},{5,5},{6,3},{7,7},{8,8},{9,12},{10,1... | collective-permute-start | bytes 1179656 | tf_op jit(solution)/shard_map/ppermute | solution.py:54
  940.5 116.7 %collective-permute-start.57 = (bf16[4,2,2,96,768]{4,3,0,1,2:T(8,128)(2,1)}, bf16[4,2,2,96,768]{4,3,0,1,2:T(8,128)(2,1)}, u32[]{:S(2)}, u32[]{:S(2)}) collective-permute-start(bf16[4,2,2,96,768]{4,3,0,1,2:T(8,128)(2,1)} %bitcast.278), channel_id=1, source_target_pairs={{0,4},{1,5},{2,6},{3,7},{4,0},{5,1},{6,2},{7,3},{8,12},{9,13},{10,... | collective-permute-start | bytes 7077896 | tf_op jit(solution)/shard_map/ppermute | solution.py:54
  941.9 120.3 %collective-permute-start.63 = (bf16[4,2,2,96,768]{4,3,0,2,1:T(8,128)(2,1)}, bf16[4,2,2,96,768]{4,3,0,2,1:T(8,128)(2,1)}, u32[]{:S(2)}, u32[]{:S(2)}) collective-permute-start(bf16[4,2,2,96,768]{4,3,0,2,1:T(8,128)(2,1)} %bitcast.277), channel_id=1, source_target_pairs={{0,4},{1,5},{2,6},{3,7},{4,0},{5,1},{6,2},{7,3},{8,12},{9,13},{10,... | collective-permute-start | bytes 7077896 | tf_op jit(solution)/shard_map/ppermute | solution.py:54
  1019.3 37.8 %collective-permute-start.50 = (bf16[256,768]{0,1:T(8,128)(2,1)S(1)}, bf16[256,768]{0,1:T(8,128)(2,1)S(1)}, u32[]{:S(2)}, u32[]{:S(2)}) collective-permute-start(bf16[256,768]{0,1:T(8,128)(2,1)S(1)} %get-tuple-element.87), channel_id=1, source_target_pairs={{0,1},{1,5},{2,3},{3,7},{4,2},{5,6},{6,0},{7,4},{8,9},{9,13},{10,1... | collective-permute-start | bytes 1179656 | tf_op jit(solution)/shard_map/ppermute | solution.py:54
  1026.4 30.7 %collective-permute-start.49 = (bf16[256,768]{0,1:T(8,128)(2,1)S(1)}, bf16[256,768]{0,1:T(8,128)(2,1)S(1)}, u32[]{:S(2)}, u32[]{:S(2)}) collective-permute-start(bf16[256,768]{0,1:T(8,128)(2,1)S(1)} %copy-done.68), channel_id=1, source_target_pairs={{0,2},{1,6},{2,0},{3,4},{4,3},{5,7},{6,1},{7,5},{8,10},{9,14},{10,... | collective-permute-start | bytes 1179656 | tf_op jit(solution)/shard_map/ppermute | solution.py:54
  1039.8 27.5 %collective-permute-start.51 = (bf16[4,2,2,4,24,768]{5,4,3,2,1,0:T(8,128)(2,1)S(1)}, bf16[4,2,2,4,24,768]{5,4,3,2,1,0:T(8,128)(2,1)S(1)}, u32[]{:S(2)}, u32[]{:S(2)}) collective-permute-start(bf16[4,2,2,4,24,768]{5,4,3,2,1,0:T(8,128)(2,1)S(1)} %dynamic-slice_bitcast_fusion), channel_id=1, source_target_pairs={{0,4},{1,5},{2,6},{3,7},{4,0},{5,1},{6,2},{7,3},{8,12},{9,13},{10,... | collective-permute-start | bytes 7077896 | tf_op jit(solution)/shard_map/ppermute | solution.py:54
  1059.9 29.1 %collective-permute-start.58 = (bf16[4,2,96,768]{3,2,0,1:T(8,128)(2,1)S(1)}, bf16[4,2,96,768]{3,2,0,1:T(8,128)(2,1)S(1)}, u32[]{:S(2)}, u32[]{:S(2)}) collective-permute-start(bf16[4,2,96,768]{3,2,0,1:T(8,128)(2,1)S(1)} %dynamic-slice_bitcast_fusion.2), channel_id=1, source_target_pairs={{0,8},{1,9},{2,10},{3,11},{4,12},{5,13},{6,14},{7,15},{8,0},{9,1},... | collective-permute-start | bytes 3538952 | tf_op jit(solution)/shard_map/ppermute | solution.py:54
  1065.8 42.7 %collective-permute-start.64 = (bf16[4,2,96,768]{3,2,0,1:T(8,128)(2,1)}, bf16[4,2,96,768]{3,2,0,1:T(8,128)(2,1)}, u32[]{:S(2)}, u32[]{:S(2)}) collective-permute-start(bf16[4,2,96,768]{3,2,0,1:T(8,128)(2,1)} %dynamic-slice_bitcast_fusion.1), channel_id=1, source_target_pairs={{0,16},{1,17},{2,18},{3,19},{4,20},{5,21},{6,22},{7,23},{8,24},{9,... | collective-permute-start | bytes 3538952 | tf_op jit(solution)/shard_map/ppermute | solution.py:54
  1069.2 47.4 %collective-permute-start.52 = (bf16[4,2,4,24,768]{4,3,2,1,0:T(8,128)(2,1)}, bf16[4,2,4,24,768]{4,3,2,1,0:T(8,128)(2,1)}, u32[]{:S(2)}, u32[]{:S(2)}) collective-permute-start(bf16[4,2,4,24,768]{4,3,2,1,0:T(8,128)(2,1)} %dynamic-slice_bitcast_fusion.3), channel_id=1, source_target_pairs={{0,8},{1,9},{2,10},{3,11},{4,12},{5,13},{6,14},{7,15},{8,0},{9,1},... | collective-permute-start | bytes 3538952 | tf_op jit(solution)/shard_map/ppermute | solution.py:54
  (132 other events, 3300.6 us)

commit v2 on v1

v2 whole, which is shorter than its diff:
```python
import functools

import jax
import jax.numpy as jnp
from jax import lax
from jax.experimental import pallas as pl
from jax.experimental.pallas import tpu as pltpu
from jax.sharding import PartitionSpec as P

F32 = jnp.float32
BF16 = jnp.bfloat16
BLOCK = 128
TILE = 2 * BLOCK
AXES = ("dp", "tensor")


def matmul(left, right):
    return jnp.dot(left, right, preferred_element_type=F32)


def right_t(left, right):
    return lax.dot_general(left, right, (((1,), (1,)), ((), ())), preferred_element_type=F32)


def left_t(left, right):
    return lax.dot_general(left, right, (((0,), (0,)), ((), ())), preferred_element_type=F32)


def rms_scale(values):
    return lax.rsqrt(jnp.mean(values * values, axis=-1, keepdims=True) + 1e-06)


def rms_back(grad_norm, normed, scale, gain):
    scaled = grad_norm * gain
    return scale * (scaled - normed * jnp.mean(scaled * normed, axis=-1, keepdims=True))


def gelu_exact(values):
    return jax.nn.gelu(values, approximate=False)


def gelu_back(upper, grad):
    unused, pull = jax.vjp(gelu_exact, upper)
    return pull(grad)[0]


def send(x, to):
    nd, nt = lax.axis_size("dp"), lax.axis_size("tensor")
    pairs = []
    for d in range(nd):
        for t in range(nt):
            d2, t2 = to(d, t)
            pairs.append((d * nt + t, d2 * nt + t2))
    return lax.ppermute(x, AXES, pairs)


def by_shift(shift):
    nt = lax.axis_size("tensor")
    return lambda d, t: (d, (t + shift) % nt)


def by_bit(bit):
    return lambda d, t: (d ^ bit, t)


def gather(piece, bits):
    nt = lax.axis_size("tensor")
    have = {0: jnp.stack([piece] + [send(piece, by_shift(s)) for s in range(1, nt)])}
    for bit in bits:
        have.update({mask | bit: send(block, by_bit(bit)) for mask, block in have.items()})
    return [have[mask] for mask in range(len(have))]


def place_kernel(slot_of, *refs):
    pieces, out, sem = refs[:-2], refs[-2], refs[-1]
    copies = []
    for mask, piece in enumerate(pieces):
        for shift in range(piece.shape[0]):
            copies.append(
                pltpu.make_async_copy(piece.at[shift], out.at[slot_of(mask, shift)], sem)
            )
    for copy in copies:
        copy.start()
    for copy in copies:
        copy.wait()


def placed(pieces, tensor_first):
    nd, nt = len(pieces), pieces[0].shape[0]

    def slot_of(mask, shift):
        d = lax.axis_index("dp") ^ mask
        t = lax.rem(lax.axis_index("tensor") + (nt - shift), nt)
        return t * nd + d if tensor_first else d * nt + t

    return pl.pallas_call(
        functools.partial(place_kernel, slot_of),
        out_shape=jax.ShapeDtypeStruct((nd * nt,) + pieces[0].shape[1:], pieces[0].dtype),
        in_specs=[pl.BlockSpec(memory_space=pl.ANY)] * nd,
        out_specs=pl.BlockSpec(memory_space=pl.ANY),
        scratch_shapes=[pltpu.SemaphoreType.DMA],
        name="place",
    )(*pieces)


def pick(x, index, axis):
    return lax.dynamic_index_in_dim(x, index, axis, keepdims=False)


def sum_to_owner(x, bits):
    nt, nd = x.shape[:2]
    d, t = lax.axis_index("dp"), lax.axis_index("tensor")
    rest = x.shape[2:]
    names = [1 << k for k in range(nd.bit_length() - 1)][::-1]
    x = x.reshape((nt,) + (2,) * len(names) + rest)
    for bit in bits:
        axis = 1 + names.index(bit)
        names.remove(bit)
        mine = (d // bit) % 2
        got = send(pick(x, 1 - mine, axis), by_bit(bit))
        x = pick(x, mine, axis).astype(F32) + got.astype(F32)
        if names or nt > 1:
            x = x.astype(BF16)
    total = pick(x, t, 0).astype(F32)
    for shift in range(1, nt):
        total = total + send(pick(x, lax.rem(t + shift, nt), 0), by_shift(shift)).astype(F32)
    return total


def seat(turn):
    nt = lax.axis_size("tensor")
    t, core = lax.axis_index("tensor"), lax.axis_index("dp") % 2
    block = lax.rem(turn + t, nt)
    source = lax.rem(2 * (t // 2) + core + nt - turn, nt)
    return block, source


def turn_to(turn):
    nt = lax.axis_size("tensor")

    def to(d, t):
        block = (turn + t) % nt
        return d - d % 2 + block % 2, 2 * (block // 2) + d % 2

    return to


def turn_back(turn):
    nt = lax.axis_size("tensor")

    def to(d, t):
        return d - d % 2 + t % 2, (2 * (t // 2) + d % 2 + nt - turn) % nt

    return to


def split_kernel(x_ref, *outs):
    for turn, out in enumerate(outs):
        block = seat(turn)[0]
        out[...] = x_ref[block // 2, :, block % 2].reshape(out.shape)


def join_kernel(*refs):
    out = refs[-1]
    for turn, piece in enumerate(refs[:-1]):
        block = seat(turn)[0]
        out[block // 2, :, block % 2] = piece[...].reshape(out.shape[1], BLOCK, out.shape[4])


def to_sequences(x):
    micro, _, rows, width = x.shape
    nt = lax.axis_size("tensor")
    pieces = pl.pallas_call(
        split_kernel, out_shape=[jax.ShapeDtypeStruct((rows // 2, width), x.dtype)] * nt, name="split"
    )(x.reshape(micro, rows // TILE, 2, BLOCK, width))
    return [send(piece, turn_to(turn)) for turn, piece in enumerate(pieces)]


def from_sequences(pieces, micro):
    half, width = pieces[0].shape
    back = [send(piece, turn_back(turn)) for turn, piece in enumerate(pieces)]
    out = pl.pallas_call(
        join_kernel,
        out_shape=jax.ShapeDtypeStruct((micro, half // BLOCK, 2, BLOCK, width), pieces[0].dtype),
        name="join",
    )(*back)
    return out.reshape(micro, 1, 2 * half, width)


def load_rows(rows, scratch, sem):
    return pltpu.make_async_copy(rows, scratch.at[pl.ds(1, rows.shape[0])], sem)


def reach(block, seg_low):
    first = seg_low[block, 0]
    before = 0
    for k in range(seg_low.shape[0]):
        before += (seg_low[k, BLOCK - 1] < first).astype(jnp.int32)
    return (block + 2 - before) // 2


def rows_of(block, seg_s):
    return jnp.broadcast_to(seg_s[block + 1], (BLOCK, BLOCK)).T


def row_mask(row_seg, first, block, seg_s):
    row = lax.broadcasted_iota(jnp.int32, (BLOCK, BLOCK), 0)
    col = lax.broadcasted_iota(jnp.int32, (BLOCK, BLOCK), 1)
    masks = []
    for k in range(2):
        ahead = (first + k - 1 - block) * BLOCK
        allowed = (row_seg == seg_s[first + k]) & (col + ahead <= row)
        masks.append(jnp.where(allowed, 0.0, -1e30).astype(F32))
    return jnp.concatenate(masks, axis=1)


def forward_kernel(
    heads, groups, q_ref, k_all, v_all, seg_low, seg_ref, pre_ref, post_ref,
    att_ref, u_ref, lse_ref, k_s, v_s, seg_s, qp_s, s_s, m_s, l_s, u_s, sems,
):
    step = pl.program_id(0)
    core = lax.axis_index("dp") % 2

    @pl.when(step == 0)
    def _():
        copies = [load_rows(k_all, k_s, sems.at[0]), load_rows(v_all, v_s, sems.at[1])]
        for copy in copies:
            copy.start()
        seg_s[0] = jnp.full((1, BLOCK), -1, jnp.int32)
        seg_s[1:] = seg_ref[...]
        k_s[0] = jnp.zeros(k_s.shape[1:], BF16)
        v_s[0] = jnp.zeros(v_s.shape[1:], BF16)
        for copy in copies:
            copy.wait()

    block = 2 * step + core
    tiles = reach(block, seg_low)
    query = q_ref[...].astype(F32)
    for h in range(heads):
        qp_s[h * BLOCK : (h + 1) * BLOCK, :] = (query * pre_ref[h : h + 1, :]).astype(BF16)
    row_seg = rows_of(block, seg_s)
    m_s[...] = jnp.full(m_s.shape, -3e38, F32)
    l_s[...] = jnp.zeros(l_s.shape, F32)
    u_s[...] = jnp.zeros(u_s.shape, F32)
    size = heads // groups * BLOCK

    def scores(tile, carry):
        first = block + 2 - 2 * (tile + 1)
        keys = k_s[pl.ds(first, 2)].reshape(TILE, -1)
        mask = row_mask(row_seg, first, block, seg_s)
        for g in range(groups):
            rows = pl.ds(g * size, size)
            s = right_t(qp_s[rows, :], keys)
            s = (s.reshape(heads // groups, BLOCK, TILE) + mask[None]).reshape(size, TILE)
            s_s[tile, rows, :] = s
            m_s[rows, :] = jnp.maximum(m_s[rows, :], jnp.maximum(s[:, :BLOCK], s[:, BLOCK:]))
        return carry

    lax.fori_loop(0, tiles, scores, 0)
    m_s[...] = jnp.broadcast_to(jnp.max(m_s[...], axis=-1, keepdims=True), m_s.shape)

    def weigh(tile, carry):
        first = block + 2 - 2 * (tile + 1)
        values = v_s[pl.ds(first, 2)].reshape(TILE, -1)
        for g in range(groups):
            rows = pl.ds(g * size, size)
            top = m_s[rows, :]
            p = jnp.exp(s_s[tile, rows, :] - jnp.concatenate([top, top], axis=1))
            l_s[rows, :] += p[:, :BLOCK] + p[:, BLOCK:]
            u_s[rows, :] += matmul(p.astype(BF16), values)
        return carry

    lax.fori_loop(0, tiles, weigh, 0)
    att = jnp.zeros((BLOCK, att_ref.shape[1]), F32)
    for h in range(heads):
        rows = slice(h * BLOCK, (h + 1) * BLOCK)
        total = jnp.sum(l_s[rows, :], axis=-1, keepdims=True)
        lse_ref[0, rows, :] = m_s[rows, :] + jnp.log(total)
        u = u_s[rows, :] * (1.0 / total)
        u_ref[0, h] = u.astype(BF16)
        att = att + u * post_ref[h : h + 1, :]
    att_ref[...] = att.astype(BF16)


def whole(shape):
    return pl.BlockSpec(shape, lambda i: (0,) * len(shape), pipeline_mode=pl.Buffered(1))


def cost(flops, moved):
    return pl.CostEstimate(flops=int(flops), bytes_accessed=int(moved), transcendentals=0)


ANY = pl.BlockSpec(memory_space=pl.ANY)
SCALARS = pl.BlockSpec(memory_space=pltpu.SMEM)


def attend(query, k_all, v_all, segs, pre, post):
    heads, width = pre.shape
    rows, stack = query.shape[0], heads * BLOCK
    blocks = rows // BLOCK
    most = (1024 // BLOCK + 2) // 2
    groups = 4
    by_block = pl.BlockSpec((BLOCK, width), lambda i: (i, 0))
    return pl.pallas_call(
        functools.partial(forward_kernel, heads, groups),
        grid=(blocks,),
        in_specs=[
            by_block, ANY, ANY, SCALARS, whole((2 * blocks, 1, BLOCK)), whole(pre.shape), whole(post.shape),
        ],
        out_specs=[
            by_block,
            pl.BlockSpec((1, heads, BLOCK, width), lambda i: (i, 0, 0, 0)),
            pl.BlockSpec((1, stack, BLOCK), lambda i: (i, 0, 0)),
        ],
        scratch_shapes=[
            pltpu.VMEM((2 * blocks + 1, BLOCK, width), BF16),
            pltpu.VMEM((2 * blocks + 1, BLOCK, width), BF16),
            pltpu.VMEM((2 * blocks + 1, 1, BLOCK), jnp.int32),
            pltpu.VMEM((stack, width), BF16),
            pltpu.VMEM((most, stack, TILE), F32),
            pltpu.VMEM((stack, BLOCK), F32),
            pltpu.VMEM((stack, BLOCK), F32),
            pltpu.VMEM((stack, width), F32),
            pltpu.SemaphoreType.DMA((2,)),
        ],
        out_shape=[
            jax.ShapeDtypeStruct((rows, width), BF16),
            jax.ShapeDtypeStruct((blocks, heads, BLOCK, width), BF16),
            jax.ShapeDtypeStruct((blocks, stack, BLOCK), F32),
        ],
        compiler_params=pltpu.CompilerParams(vmem_limit_bytes=60 << 20),
        cost_estimate=cost(4 * rows * 1024 * stack // BLOCK * width, 4 * rows * stack // BLOCK * width),
        name="attend",
    )(query, k_all, v_all, segs, segs[:, None, :], pre, post)


def backward_kernel(
    heads, groups, q_ref, g_ref, u_ref, lse_ref, k_all, v_all, seg_low, seg_ref, pre_ref, post_ref,
    dq_ref, dk_ref, dv_ref, dpre_ref, dpost_ref,
    k_s, v_s, seg_s, dk_s, dv_s, qp_s, gp_s, d_s, t_s, sems,
):
    step = pl.program_id(0)
    core = lax.axis_index("dp") % 2

    @pl.when(step == 0)
    def _():
        copies = [load_rows(k_all, k_s, sems.at[0]), load_rows(v_all, v_s, sems.at[1])]
        for copy in copies:
            copy.start()
        seg_s[0] = jnp.full((1, BLOCK), -1, jnp.int32)
        seg_s[1:] = seg_ref[...]
        k_s[0] = jnp.zeros(k_s.shape[1:], BF16)
        v_s[0] = jnp.zeros(v_s.shape[1:], BF16)
        dk_s[...] = jnp.zeros(dk_s.shape, F32)
        dv_s[...] = jnp.zeros(dv_s.shape, F32)
        dpre_ref[...] = jnp.zeros(dpre_ref.shape, F32)
        dpost_ref[...] = jnp.zeros(dpost_ref.shape, F32)
        for copy in copies:
            copy.wait()

    block = 2 * step + core
    tiles = reach(block, seg_low)
    query = q_ref[...].astype(F32)
    grad = g_ref[...].astype(F32)
    for h in range(heads):
        rows = slice(h * BLOCK, (h + 1) * BLOCK)
        qp_s[rows, :] = (query * pre_ref[h : h + 1, :]).astype(BF16)
        gain = post_ref[h : h + 1, :]
        gp_s[rows, :] = (grad * gain).astype(BF16)
        both = grad * u_ref[0, h].astype(F32)
        d_s[rows, :] = jnp.broadcast_to(jnp.sum(both * gain, axis=-1, keepdims=True), (BLOCK, BLOCK))
        dpost_ref[h] += jnp.sum(both.reshape(BLOCK // 8, 8, -1), axis=0)
    row_seg = rows_of(block, seg_s)
    t_s[...] = jnp.zeros(t_s.shape, F32)
    size = heads // groups * BLOCK

    def tile_step(tile, carry):
        first = block + 2 - 2 * (tile + 1)
        keys = k_s[pl.ds(first, 2)].reshape(TILE, -1)
        values = v_s[pl.ds(first, 2)].reshape(TILE, -1)
        mask = row_mask(row_seg, first, block, seg_s)
        dk = jnp.zeros((TILE, keys.shape[1]), F32)
        dv = jnp.zeros((TILE, keys.shape[1]), F32)
        for g in range(groups):
            rows = pl.ds(g * size, size)
            s = right_t(qp_s[rows, :], keys)
            s = (s.reshape(heads // groups, BLOCK, TILE) + mask[None]).reshape(size, TILE)
            top = lse_ref[0, rows, :]
            p = jnp.exp(s - jnp.concatenate([top, top], axis=1))
            dw = right_t(gp_s[rows, :], values)
            term = d_s[rows, :]
            ds = (p * (dw - jnp.concatenate([term, term], axis=1))).astype(BF16)
            t_s[rows, :] += matmul(ds, keys)
            dv = dv + left_t(p.astype(BF16), gp_s[rows, :])
            dk = dk + left_t(ds, qp_s[rows, :])
        dk_s[pl.ds(first, 2)] += dk.reshape(2, BLOCK, -1)
        dv_s[pl.ds(first, 2)] += dv.reshape(2, BLOCK, -1)
        return carry

    lax.fori_loop(0, tiles, tile_step, 0)
    dq = jnp.zeros(query.shape, F32)
    for h in range(heads):
        part = t_s[h * BLOCK : (h + 1) * BLOCK, :]
        dq = dq + part * pre_ref[h : h + 1, :]
        dpre_ref[h] += jnp.sum((query * part).reshape(BLOCK // 8, 8, -1), axis=0)
    dq_ref[...] = dq.astype(BF16)

    @pl.when(step == pl.num_programs(0) - 1)
    def _():
        for k in range(dk_ref.shape[0]):
            dk_ref[k] = dk_s[k + 1].astype(BF16)
            dv_ref[k] = dv_s[k + 1].astype(BF16)


def attend_back(query, grad, u, lse, k_all, v_all, segs, pre, post):
    heads, width = pre.shape
    rows, stack = query.shape[0], heads * BLOCK
    blocks = rows // BLOCK
    groups = 4
    by_block = pl.BlockSpec((BLOCK, width), lambda i: (i, 0))
    return pl.pallas_call(
        functools.partial(backward_kernel, heads, groups),
        grid=(blocks,),
        in_specs=[
            by_block,
            by_block,
            pl.BlockSpec((1, heads, BLOCK, width), lambda i: (i, 0, 0, 0)),
            pl.BlockSpec((1, stack, BLOCK), lambda i: (i, 0, 0)),
            ANY, ANY, SCALARS, whole((2 * blocks, 1, BLOCK)), whole(pre.shape), whole(post.shape),
        ],
        out_specs=[
            by_block,
            whole((2 * blocks, BLOCK, width)),
            whole((2 * blocks, BLOCK, width)),
            whole((heads, 8, width)),
            whole((heads, 8, width)),
        ],
        scratch_shapes=[
            pltpu.VMEM((2 * blocks + 1, BLOCK, width), BF16),
            pltpu.VMEM((2 * blocks + 1, BLOCK, width), BF16),
            pltpu.VMEM((2 * blocks + 1, 1, BLOCK), jnp.int32),
            pltpu.VMEM((2 * blocks + 1, BLOCK, width), F32),
            pltpu.VMEM((2 * blocks + 1, BLOCK, width), F32),
            pltpu.VMEM((stack, width), BF16),
            pltpu.VMEM((stack, width), BF16),
            pltpu.VMEM((stack, BLOCK), F32),
            pltpu.VMEM((stack, width), F32),
            pltpu.SemaphoreType.DMA((2,)),
        ],
        out_shape=[
            jax.ShapeDtypeStruct((rows, width), BF16),
            jax.ShapeDtypeStruct((2 * blocks, BLOCK, width), BF16),
            jax.ShapeDtypeStruct((2 * blocks, BLOCK, width), BF16),
            jax.ShapeDtypeStruct((heads, 8, width), F32),
            jax.ShapeDtypeStruct((heads, 8, width), F32),
        ],
        compiler_params=pltpu.CompilerParams(vmem_limit_bytes=62 << 20),
        cost_estimate=cost(10 * rows * 1024 * stack // BLOCK * width, 4 * rows * stack // BLOCK * width),
        name="attend_back",
    )(query, grad, u, lse, k_all, v_all, segs, segs[:, None, :], pre, post)


MESH = pl.DeviceIdType.MESH


def flip(index, bit):
    return index + bit - 2 * bit * ((index // bit) % 2)


def greet(nd, nt, d, t):
    barrier = pltpu.get_barrier_semaphore()
    core = d % 2
    partners = [(d, lax.rem(t + s, nt)) for s in range(1, nt)]
    partners += [(flip(d, 1), lax.rem(t + s, nt)) for s in range(nt)]
    bit = 2
    while bit < nd:
        partners.append((flip(d, bit), t))
        bit *= 2
    for partner in partners:
        pl.semaphore_signal(barrier, inc=1, device_id=partner, device_id_type=MESH)
    pl.semaphore_wait(barrier, len(partners))


def remote(src, dst, send_sem, recv_sem, to):
    return pltpu.make_async_remote_copy(
        src_ref=src, dst_ref=dst, send_sem=send_sem, recv_sem=recv_sem, device_id=to, device_id_type=MESH
    )


def start_kernel(
    nd, nt, share, halves, *refs,
):
    if halves:
        tokens, segments, bundle, later = refs[:4]
        x_out, q_out, k_out, v_out, seg_out, w_out, gain_out, later_out = refs[4:12]
        wg_s, w_send, w_recv, w_self = refs[12:16]
    else:
        tokens, segments, w_out, gain_out, later = refs[:5]
        x_out, q_out, k_out, v_out, seg_out, later_out = refs[5:11]
    (l_send, l_recv, l_self, x_s, kv_s, x_send, x_recv, x_self, kv_send, kv_recv, kv_self, seg_send, seg_recv, seg_self) = refs[-14:]
    d, t = lax.axis_index("dp"), lax.axis_index("tensor")
    core = d % 2
    width = x_out.shape[1]
    micro = tokens.shape[0]
    per = tokens.shape[1]
    greet(nd, nt, d, t)

    if halves:
        own = pltpu.make_async_copy(bundle, wg_s.at[d, t], w_self)
        own.start()
        z_copies = []
        for s in range(1, nt):
            copy = remote(bundle, wg_s.at[d, t], w_send.at[0, 0, s], w_recv.at[0, 0, s], (d, lax.rem(t + s, nt)))
            copy.start()
            z_copies.append(copy)
        own.wait()
        for copy in z_copies:
            copy.wait()

    sends = []
    for m in range(micro):
        for c in range(2):
            to = (d - core + c, 2 * m + core)
            here = (to[0] == d) & (to[1] == t)
            src, dst = tokens.at[m, :, c], x_s.at[pl.ds(per * t, per)]
            far = remote(src, dst, x_send.at[2 * m + c], x_recv.at[t], to)
            near = pltpu.make_async_copy(src, dst, x_self)
            pl.when(jnp.logical_not(here))(far.start)
            pl.when(here)(near.start)
            sends.append((here, far, near))

    holder = t % 2 == core
    seg_here = pltpu.make_async_copy(segments.at[t // 2], seg_out, seg_self)
    seg_there = remote(segments.at[t // 2], seg_out, seg_send, seg_recv, (flip(d, 1), t))

    @pl.when(holder)
    def _():
        seg_here.start()
        seg_there.start()

    l_copies = [pltpu.make_async_copy(later, later_out.at[t], l_self)]
    for s in range(1, nt):
        l_copies.append(remote(later, later_out.at[t], l_send.at[s], l_recv.at[s], (d, lax.rem(t + s, nt))))
    for copy in l_copies:
        copy.start()

    if halves:
        bits = [1 << k for k in range(1, nd.bit_length() - 1)]
        routes = [bits + [1], bits[::-1] + [1]]
        have = [[0] for _ in halves]
        for stage in range(len(bits) + 1):
            copies = []
            for h, (lo, hi) in enumerate(halves):
                bit = routes[h][stage]
                for k, mask in enumerate(have[h]):
                    slab = d
                    for b in [1 << j for j in range(nd.bit_length() - 1)]:
                        if mask & b:
                            slab = flip(slab, b)
                    ref = wg_s.at[slab, :, pl.ds(lo, hi - lo)]
                    copies.append(
                        remote(ref, ref, w_send.at[1 + h, stage, k], w_recv.at[1 + h, stage, k], (flip(d, bit), t))
                    )
                have[h] = have[h] + [mask | bit for mask in have[h]]
            for copy in copies:
                copy.start()
            for copy in copies:
                copy.wait()

        gains = jnp.zeros((8, width), F32)
        for pair in range(nd * nt // 2):
            slabs = [wg_s[(2 * pair + e) // nt, (2 * pair + e) % nt].astype(F32) for e in range(2)]
            for k in range(3):
                both = jnp.concatenate([slab[k * share : (k + 1) * share] for slab in slabs])
                w_out[2 * pair * share : 2 * (pair + 1) * share, k * width : (k + 1) * width] = both.astype(BF16)
            gains = gains + (slabs[0] + slabs[1])[3 * share : 3 * share + 8]
        gain_out[...] = gains

    kv_copies = []
    gain = gain_out[:1]
    for s in range(nt):
        source = lax.rem(t + s, nt)
        here = (source == t) & holder
        arrival = remote(
            x_s.at[pl.ds(per * source, per)], x_s.at[pl.ds(per * source, per)], x_send.at[0], x_recv.at[source], (flip(d, 1), t)
        )
        local = pltpu.make_async_copy(tokens.at[0, :, 0], x_s.at[pl.ds(per * source, per)], x_self)
        pl.when(jnp.logical_not(here))(arrival.wait_recv)
        pl.when(here)(local.wait)
        x = x_s[pl.ds(per * source, per)].reshape(per * BLOCK, width)
        rows = pl.ds(pl.multiple_of(source * per * BLOCK, per * BLOCK), per * BLOCK)
        x_out[rows, :] = x
        x = x.astype(F32)
        h = (x * rms_scale(x) * gain).astype(BF16)
        q_out[rows, :] = matmul(h, w_out[:, :width]).astype(BF16)
        for k, out in enumerate((k_out, v_out)):
            value = matmul(h, w_out[:, (k + 1) * width : (k + 2) * width]).astype(BF16)
            kv_s[k, s] = value.reshape(per, BLOCK, width)
            dst = out.at[pl.ds(per * source, per), core]
            near = pltpu.make_async_copy(kv_s.at[k, s], dst, kv_self.at[k, s])
            far = remote(kv_s.at[k, s], dst, kv_send.at[k, s], kv_recv.at[k, s], (flip(d, 1), t))
            near.start()
            far.start()
            kv_copies += [near, far]
    for copy in kv_copies + l_copies:
        copy.wait()
    for here, far, near in sends:
        pl.when(jnp.logical_not(here))(far.wait_send)

    @pl.when(holder)
    def _():
        seg_here.wait()
        seg_there.wait_send()

    @pl.when(jnp.logical_not(holder))
    def _():
        seg_there.wait_recv()


def start(tokens, segments, bundle, later, share):
    micro, _, rows, width = tokens.shape
    nd, nt = lax.axis_size("dp"), lax.axis_size("tensor")
    count = rows * nt // 2
    blocks = count // BLOCK
    per = blocks // nt
    length = bundle.shape[0]
    dma = pltpu.SemaphoreType.DMA
    vmem = pl.BlockSpec(memory_space=pltpu.VMEM)
    shaped = jax.ShapeDtypeStruct
    most = max(nd // 2, nt)
    inside = 2 * share % 16 == 0 and length >= 32
    middle = length // 32 * 16
    if inside:
        halves, given = [(0, middle), (middle, length)], [bundle]
        gathered_specs = [vmem, vmem]
        gathered = [shaped((width, 3 * width), BF16), shaped((8, width), F32)]
        scratch = [
            pltpu.VMEM((nd, nt, length, width), BF16),
            dma((3, nd.bit_length(), most)), dma((3, nd.bit_length(), most)), dma,
        ]
    else:
        slabs = lax.all_gather(bundle, AXES, axis=0, tiled=False)
        w_qkv = slabs[:, : 3 * share].reshape(nd * nt, 3, share, width).transpose(0, 2, 1, 3)
        w_qkv = w_qkv.reshape(width, 3 * width)
        gains = jnp.sum(slabs[:, 3 * share : 3 * share + 8].astype(F32), axis=0)
        halves, given, gathered_specs, gathered, scratch = [], [w_qkv, gains], [], [], []
    results = pl.pallas_call(
        functools.partial(start_kernel, nd, nt, share, halves),
        in_specs=[ANY, ANY] + ([ANY] if inside else [vmem, vmem]) + [ANY],
        out_specs=[vmem, vmem, ANY, ANY, ANY] + gathered_specs + [ANY],
        out_shape=[
            shaped((count, width), BF16),
            shaped((count, width), BF16),
            shaped((blocks, 2, BLOCK, width), BF16),
            shaped((blocks, 2, BLOCK, width), BF16),
            shaped((2 * blocks, BLOCK), jnp.int32),
            *gathered,
            shaped((nt,) + later.shape, BF16),
        ],
        scratch_shapes=scratch + [
            dma((nt,)), dma((nt,)), dma,
            pltpu.VMEM((blocks, BLOCK, width), BF16),
            pltpu.VMEM((2, nt, per, BLOCK, width), BF16),
            dma((nt,)), dma((nt,)), dma,
            dma((2, nt)), dma((2, nt)), dma((2, nt)),
            dma, dma, dma,
        ],
        compiler_params=pltpu.CompilerParams(
            collective_id=0, has_side_effects=True, vmem_limit_bytes=56 << 20
        ),
        name="start",
    )(
        tokens.reshape(micro, rows // TILE, 2, BLOCK, width),
        segments.reshape(micro, 2 * blocks, BLOCK),
        *given,
        later,
    )
    return results if inside else (*results[:5], w_qkv, gains, results[5])


def gelu_parts(v):
    t = 1.0 / (1.0 + 0.23164189 * jnp.abs(v))
    bell = jnp.exp(-0.5 * v * v)
    series = t * (0.127414796 + t * (-0.142248368 + t * (0.7107068705 + t * (-0.7265760135 + t * 0.5307027145))))
    tail = series * bell
    return jnp.where(v < 0.0, tail, 1.0 - tail), 0.3989422804 * bell


def middle_kernel(
    rb, nt, *refs,
):
    x_ref, att_ref, w_out, gain_ref, up_ref, down_ref = refs[:6]
    dys, refs = refs[6 : 6 + nt], refs[6 + nt :]
    outs, refs = refs[:nt], refs[nt:]
    after_ref, datt_ref, dwo_ref, dgain_ref, grads_ref = refs[:5]
    dy_ref, a_s, h_s, ht_s, dyt_s, o_s, dh_s, hid_s, dhid_s, sems = refs[5:]
    step = pl.program_id(0)
    count, width = x_ref.shape
    parts = range(0, count, rb)

    @pl.when(step == 0)
    def _():
        copies = []
        for turn, dy in enumerate(dys):
            rows = pl.ds(pl.multiple_of(seat(turn)[1] * (count // nt), count // nt), count // nt)
            copies.append(pltpu.make_async_copy(dy, dy_ref.at[rows], sems.at[turn]))
        for copy in copies:
            copy.start()
        for copy in copies:
            copy.wait()
        for r in parts:
            rows = slice(r, r + rb)
            after = x_ref[rows, :].astype(F32) + matmul(att_ref[rows, :], w_out[...])
            a_s[rows, :] = after
            o_s[rows, :] = after
            h = (after * rms_scale(after) * gain_ref[...]).astype(BF16)
            h_s[rows, :] = h
            ht_s[:, rows] = h.T
            dyt_s[:, rows] = dy_ref[rows, :].T
            dh_s[rows, :] = jnp.zeros((rb, width), F32)

    up = up_ref[:, 0, 0].reshape(width, -1)
    down = down_ref[:, 0, 0].reshape(width, -1)
    for r in parts:
        rows = slice(r, r + rb)
        v = matmul(h_s[rows, :], up)
        cumulative, density = gelu_parts(v)
        hidden = (v * cumulative).astype(BF16)
        hid_s[rows, :] = hidden
        o_s[rows, :] += right_t(hidden, down)
        d_hidden = (matmul(dy_ref[rows, :], down) * (cumulative + v * density)).astype(BF16)
        dhid_s[rows, :] = d_hidden
        dh_s[rows, :] += right_t(d_hidden, up)
    share = grads_ref.shape[3]
    for r in range(0, width, 2 * share):
        rows = slice(r, r + 2 * share)
        k = r // share
        grads_ref[k : k + 2, 0, 0] = matmul(ht_s[rows, :], dhid_s[...]).astype(BF16).reshape(2, share, -1)
        grads_ref[k : k + 2, 0, 1] = matmul(dyt_s[rows, :], hid_s[...]).astype(BF16).reshape(2, share, -1)

    @pl.when(step == pl.num_programs(0) - 1)
    def _():
        gain = gain_ref[...]
        total = jnp.zeros((8, width), F32)
        for r in parts:
            rows = slice(r, r + rb)
            after = a_s[rows, :]
            scale = rms_scale(after)
            normed = after * scale
            dh = dh_s[rows, :]
            total = total + jnp.sum((dh * normed).reshape(rb // 8, 8, width), axis=0)
            d_after = dy_ref[rows, :].astype(F32) + rms_back(dh, normed, scale, gain)
            after_ref[rows, :] = d_after
            branch = d_after.astype(BF16)
            hid_s[rows, :] = branch
            datt_ref[rows, :] = right_t(branch, w_out[...]).astype(BF16)
        for turn, out in enumerate(outs):
            rows = pl.ds(pl.multiple_of(seat(turn)[1] * (count // nt), count // nt), count // nt)
            out[...] = o_s[rows, :].astype(BF16)
        dgain_ref[...] = total
        dwo_ref[...] = left_t(att_ref[...], hid_s[...]).astype(BF16)


def feed_forward(x, attended, dys, w_out, gain, both):
    count, width = x.shape
    nd, nt, _, share, units = both.shape
    rb = 256
    rows, part = whole((count, width)), whole((count // nt, width))
    return pl.pallas_call(
        functools.partial(middle_kernel, rb, nt),
        grid=(nt,),
        in_specs=[
            rows, rows, whole((width, width)), whole((1, width)),
            pl.BlockSpec((nd, 1, 1, share, units), lambda t: (0, t, 0, 0, 0)),
            pl.BlockSpec((nd, 1, 1, share, units), lambda t: (0, t, 1, 0, 0)),
        ] + [ANY] * nt,
        out_specs=[part] * nt + [
            rows, rows, whole((width, width)), whole((8, width)),
            pl.BlockSpec((nd, 1, 2, share, units), lambda t: (0, t, 0, 0, 0)),
        ],
        out_shape=[jax.ShapeDtypeStruct((count // nt, width), BF16)] * nt + [
            jax.ShapeDtypeStruct((count, width), F32),
            jax.ShapeDtypeStruct((count, width), BF16),
            jax.ShapeDtypeStruct((width, width), BF16),
            jax.ShapeDtypeStruct((8, width), F32),
            jax.ShapeDtypeStruct(both.shape, BF16),
        ],
        scratch_shapes=[
            pltpu.VMEM((count, width), BF16),
            pltpu.VMEM((count, width), F32),
            pltpu.VMEM((count, width), BF16),
            pltpu.VMEM((width, count), BF16),
            pltpu.VMEM((width, count), BF16),
            pltpu.VMEM((count, width), F32),
            pltpu.VMEM((count, width), F32),
            pltpu.VMEM((count, units), BF16),
            pltpu.VMEM((count, units), BF16),
            pltpu.SemaphoreType.DMA((nt,)),
        ],
        compiler_params=pltpu.CompilerParams(vmem_limit_bytes=62 << 20),
        cost_estimate=cost(12 * count * width * nt * units, 4 * nd * nt * share * units),
        name="feed_forward",
    )(x, attended, w_out, gain, both, both, *dys)


def masks_of(bits):
    masks = [0]
    for bit in bits:
        masks = masks + [mask | bit for mask in masks]
    return masks


def flips(index, mask):
    bit = 1
    while bit <= mask:
        if mask & bit:
            index = flip(index, bit)
        bit *= 2
    return index


def finish_kernel(
    nd, nt, share, inside, x_ref, dq_ref, dk_all, dv_all, after_ref, w_ref, gain_ref, dwo_ref, small_ref, *refs,
):
    if inside:
        tok_out, owned_out, small_out = refs[:3]
    else:
        tok_out, dw_out, small_out = refs[:3]
    (own_s, other_s, grads_s, ht_s, tok_s, own_sems, kv_send, kv_recv, tok_send, tok_recv, tok_self) = refs[3:14]
    d, t = lax.axis_index("dp"), lax.axis_index("tensor")
    core = d % 2
    count, width = x_ref.shape
    per = tok_out.shape[1]
    rows_in = per * BLOCK
    holder = t % 2 == core
    greet(nd, nt, d, t)

    order = [lax.rem(t + s, nt) for s in list(range(1, nt)) + [0]]
    own = [pltpu.make_async_copy(a.at[:, core], own_s.at[k], own_sems.at[k]) for k, a in enumerate((dk_all, dv_all))]
    for copy in own:
        copy.start()
    exchanged = []
    for s, source in enumerate(order):
        pair = []
        for k, a in enumerate((dk_all, dv_all)):
            pair.append(
                remote(
                    a.at[pl.ds(per * source, per), 1 - core], other_s.at[k, pl.ds(per * source, per)],
                    kv_send.at[k, s], kv_recv.at[k, s], (flip(d, 1), t),
                )
            )
            pair[-1].start()
        exchanged.append(pair)
    gain = gain_ref[:1]

    def norms(rows):
        x = x_ref[rows, :].astype(F32)
        scale = rms_scale(x)
        return x * scale, scale

    for r in range(0, count, rows_in):
        rows = slice(r, r + rows_in)
        normed, scale = norms(rows)
        ht_s[:, rows] = (normed * gain).astype(BF16).T
        grads_s[rows, :width] = dq_ref[rows, :]
    for copy in own:
        copy.wait()

    d_gain = jnp.zeros((8, width), F32)
    sends = []
    to_core = d - core + t % 2
    for s, source in enumerate(order):
        for copy in exchanged[s]:
            copy.wait()
        rows = pl.ds(pl.multiple_of(source * rows_in, rows_in), rows_in)
        for k in range(2):
            total = own_s[k, pl.ds(per * source, per)].astype(F32) + other_s[k, pl.ds(per * source, per)].astype(F32)
            grads_s[rows, (k + 1) * width : (k + 2) * width] = total.reshape(rows_in, width).astype(BF16)
        dh = right_t(grads_s[rows, :], w_ref[...])
        normed, scale = norms(rows)
        d_gain = d_gain + jnp.sum((dh * normed).reshape(rows_in // 8, 8, width), axis=0)
        tok = after_ref[rows, :] + rms_back(dh, normed, scale, gain)
        tok_s[s] = tok.astype(BF16).reshape(per, BLOCK, width)
        here = (source == t) & holder
        dst = tok_out.at[t // 2, :, core]
        far = remote(tok_s.at[s], dst, tok_send.at[s], tok_recv.at[2 * (t // 2) + core], (to_core, source))
        near = pltpu.make_async_copy(tok_s.at[s], dst, tok_self)
        pl.when(jnp.logical_not(here))(far.start)
        pl.when(here)(near.start)
        sends.append((here, far, near))

    small = small_ref[...]
    line = lax.broadcasted_iota(jnp.int32, small.shape, 0)
    small = small + jnp.where(line == 0, jnp.sum(d_gain, axis=0, keepdims=True), 0.0)
    rows_at = min(width, 8 * share if inside else 256)
    if inside:
        slab_s, core_s, plane_s, z_s, sm_s, sm_in, g_send, g_recv, s_send, s_recv = refs[14:]
    for r in range(0, width, rows_at):
        dw = matmul(ht_s[r : r + rows_at, :], grads_s[...])
        if not inside:
            dw_out[r : r + rows_at, : 3 * width] = dw.astype(BF16)
            dw_out[r : r + rows_at, 3 * width :] = dwo_ref[r : r + rows_at, :]
            continue
        dwo = dwo_ref[r : r + rows_at, :].astype(F32)
        for k in range(rows_at // share):
            lines = slice(k * share, (k + 1) * share)
            parts = [dw[lines, m * width : (m + 1) * width] for m in range(3)] + [dwo[lines]]
            slab = r // share + k
            slab_s[slab // nt, slab % nt] = jnp.concatenate(parts).astype(BF16)
    if not inside:
        small_out[...] = small
    else:
        length = slab_s.shape[2]
        middle = length // 32 * 16
        halves = [(0, middle), (middle, length)]
        bits = [1 << k for k in range(1, nd.bit_length() - 1)]
        routes = [[1] + bits, [1] + bits[::-1]]
        left = [bits + [1], bits + [1]]
        sm_s[...] = small
        for stage in range(len(bits) + 1):
            copies, adds = [], []
            for h, (lo, hi) in enumerate(halves):
                bit = routes[h][stage]
                left[h] = [b for b in left[h] if b != bit]
                for k, mask in enumerate(masks_of(left[h])):
                    away, mine = flips(flip(d, bit), mask), flips(d, mask)
                    buffer = core_s if stage == 0 else plane_s.at[stage - 1]
                    there = buffer.at[k, :, pl.ds(lo, hi - lo)]
                    copies.append(
                        remote(
                            slab_s.at[away, :, pl.ds(lo, hi - lo)], there,
                            g_send.at[h, stage, k], g_recv.at[h, stage, k], (flip(d, bit), t),
                        )
                    )
                    adds.append((mine, lo, hi, buffer, k))
            bit = routes[0][stage]
            tiny = remote(sm_s, sm_in.at[stage], s_send.at[stage], s_recv.at[stage], (flip(d, bit), t))
            for copy in copies + [tiny]:
                copy.start()
            for copy in copies + [tiny]:
                copy.wait()
            for mine, lo, hi, buffer, k in adds:
                both = slab_s[mine, :, lo:hi].astype(F32) + buffer[k, :, lo:hi].astype(F32)
                slab_s[mine, :, lo:hi] = both.astype(BF16)
            sm_s[...] += sm_in[stage]
        copies = []
        for s in range(1, nt):
            to = lax.rem(t + s, nt)
            copies.append(remote(slab_s.at[d, to], z_s.at[s], g_send.at[2, 0, s], g_recv.at[2, 0, s], (d, to)))
            copies.append(
                remote(sm_s, sm_in.at[len(bits) + s], s_send.at[len(bits) + s], s_recv.at[len(bits) + s], (d, to))
            )
        for copy in copies:
            copy.start()
        for copy in copies:
            copy.wait()
        total = slab_s[d, t].astype(F32)
        for s in range(1, nt):
            total = total + z_s[s].astype(F32)
        owned_out[...] = total
        small_out[...] = sm_s[...] + sum(sm_in[len(bits) + s] for s in range(1, nt))

    for here, far, near in sends:
        pl.when(jnp.logical_not(here))(far.wait_send)
        pl.when(here)(near.wait)
    for m in range(tok_out.shape[0]):
        for c in range(2):
            here = (2 * m + core == t) & (c == core)
            dst = tok_out.at[m, :, c]
            back = remote(dst, dst, tok_send.at[0], tok_recv.at[2 * m + c], (flip(d, 1), t))
            pl.when(jnp.logical_not(here))(back.wait_recv)


def finish(x, dq, dk_all, dv_all, after, w_qkv, gains, dwo, small, share, micro):
    count, width = x.shape
    nd, nt = lax.axis_size("dp"), lax.axis_size("tensor")
    inside = 2 * share % 16 == 0
    blocks = count // BLOCK
    per = blocks // nt
    dma = pltpu.SemaphoreType.DMA
    vmem = pl.BlockSpec(memory_space=pltpu.VMEM)
    shaped = jax.ShapeDtypeStruct
    scratch = [
        pltpu.VMEM((2, blocks, BLOCK, width), BF16),
        pltpu.VMEM((2, blocks, BLOCK, width), BF16),
        pltpu.VMEM((count, 3 * width), BF16),
        pltpu.VMEM((width, count), BF16),
        pltpu.VMEM((nt, per, BLOCK, width), BF16),
        dma((2,)), dma((2, nt)), dma((2, nt)), dma((nt,)), dma((nt,)), dma,
    ]
    if inside:
        most = max(nd // 2, nt)
        stages = nd.bit_length() - 1
        scratch += [
            pltpu.VMEM((nd, nt, 4 * share, width), BF16),
            pltpu.VMEM((nd // 2, nt, 4 * share, width), BF16),
            pltpu.VMEM((stages - 1, nd // 4, nt, 4 * share, width), BF16),
            pltpu.VMEM((nt, 4 * share, width), BF16),
            pltpu.VMEM(small.shape, F32),
            pltpu.VMEM((stages + nt,) + small.shape, F32),
            dma((3, stages, most)), dma((3, stages, most)), dma((stages + nt,)), dma((stages + nt,)),
        ]
    return pl.pallas_call(
        functools.partial(finish_kernel, nd, nt, share, inside),
        in_specs=[vmem, vmem, ANY, ANY, vmem, vmem, vmem, vmem, vmem],
        out_specs=[vmem, vmem, vmem],
        out_shape=[
            shaped((micro, per, 2, BLOCK, width), BF16),
            shaped((4 * share, width), F32) if inside else shaped((width, 4 * width), BF16),
            shaped(small.shape, F32),
        ],
        scratch_shapes=scratch,
        compiler_params=pltpu.CompilerParams(
            collective_id=1, has_side_effects=True, vmem_limit_bytes=60 << 20
        ),
        cost_estimate=cost(24 * count * width * width, 16 * count * width),
        name="finish",
    )(x, dq, dk_all, dv_all, after, w_qkv, gains, dwo, small)


def per_device(
    tokens, segments, w_query, w_key, w_value, w_out, norm_attn, norm_ffn, pre_mix, post_mix, w_up, w_down, out_grad,
):
    micro, _, rows, width = tokens.shape
    nd, nt = lax.axis_size("dp"), lax.axis_size("tensor")
    heads = pre_mix.shape[0]
    head_width = width // heads
    length = rows * nt
    count = length // 2
    blocks = count // BLOCK
    share = w_query.shape[0]
    bits = [1 << k for k in range(nd.bit_length() - 1)]
    d, t = lax.axis_index("dp"), lax.axis_index("tensor")
    core = d % 2

    place = (d * nt + t) * share
    gains = lax.dynamic_update_slice(jnp.zeros((8, width), BF16), jnp.stack([norm_attn, norm_ffn]), (0, place))
    fill = jnp.zeros((-(3 * share + 8) % 16, width), BF16)
    bundle = jnp.concatenate([w_query, w_key, w_value, gains, fill])
    units = 2 * w_up.shape[0]
    fill = jnp.zeros((-(units + share) % 16, width), BF16)
    later = jnp.concatenate([w_up, w_down, w_out, fill])
    x, query, k_all, v_all, segs, w_qkv, gains, later = start(tokens, segments, bundle, later, share)
    k_all, v_all = (a.reshape(2 * blocks, BLOCK, width) for a in (k_all, v_all))
    x, out_grad = lax.optimization_barrier((x, out_grad))
    grad_turns = to_sequences(out_grad)
    gathered = lax.all_gather(later, "dp", axis=0, tiled=False)
    all_out = gathered[:, :, units : units + share].reshape(width, width)
    both = gathered[:, :, :units].reshape((nd, nt, 2) + w_up.shape)

    def by_lane(mix):
        return jnp.repeat(mix.astype(F32), head_width, axis=1)

    pre = by_lane(pre_mix.T) * head_width ** (-0.5)
    post = by_lane(post_mix)

    attended, u, lse = attend(query, k_all, v_all, segs, pre, post)
    *out_turns, grad_after, grad_attended, grad_w_out, grad_gain_ffn, grad_both = feed_forward(
        x, attended, grad_turns, all_out, gains[1:2], both
    )
    grad_gain_ffn = jnp.sum(grad_gain_ffn, axis=0)
    out = from_sequences(out_turns, micro)
    part_both = lax.psum_scatter(
        grad_both.reshape((nd * nt,) + grad_both.shape[2:]), AXES, scatter_dimension=0, tiled=False
    ).astype(F32)

    grad_query, grad_key, grad_value, d_pre, d_post = attend_back(
        query, grad_attended, u, lse, k_all, v_all, segs, pre, post
    )

    def spread(d_mix):
        total = d_mix.reshape(heads, 8, heads, head_width).sum((1, 3)).reshape(-1)
        return jnp.pad(total, (0, width - total.shape[0]))

    small = jnp.zeros((8, width), F32).at[1].set(grad_gain_ffn)
    small = small.at[2].set(spread(d_pre)).at[3].set(spread(d_post))
    x, out = lax.optimization_barrier((x, out))
    d_tokens, owned, small = finish(
        x, grad_query, grad_key.reshape(blocks, 2, BLOCK, width), grad_value.reshape(blocks, 2, BLOCK, width),
        grad_after, w_qkv, gains, grad_w_out, small, share, micro,
    )
    d_tokens = d_tokens.reshape(tokens.shape).astype(F32)
    if owned.dtype == BF16:
        owned = lax.psum_scatter(owned, AXES, scatter_dimension=0, tiled=True).astype(F32)
        owned = [owned[:, k * width : (k + 1) * width] for k in range(4)]
        small = lax.psum(small, AXES)
    else:
        owned = [owned[k * share : (k + 1) * share] for k in range(4)]
    gain_grads = lax.dynamic_slice_in_dim(small, place, share, 1)
    pairs = heads * heads
    return (
        out,
        d_tokens,
        owned[0],
        owned[1],
        owned[2],
        owned[3],
        gain_grads[0],
        gain_grads[1],
        small[2, :pairs].reshape(heads, heads).T * head_width ** (-0.5),
        small[3, :pairs].reshape(heads, heads),
        part_both[0],
        part_both[1],
    )


def solution(mesh):
    both = P(("dp", "tensor"), None)
    gain = P(("dp", "tensor"))
    data = P(None, "dp", "tensor", None)
    ffn = P("dp", "tensor")
    return jax.shard_map(
        per_device,
        mesh=mesh,
        in_specs=(data, P(None, "dp", None), both, both, both, both, gain, gain, P(), P(), ffn, ffn, data),
        out_specs=(data, data, both, both, both, both, gain, gain, P(), P(), ffn, ffn),
        check_vma=False,
    )
```

time: 1160 us -> 438 us (0.38)
  Pallas kernels: 599 us -> 354 us
  matrix products: 129 us -> 0 us
  starting transfers between devices: 132 us -> 18.5 us
  waiting for transfers between devices: 108 us -> 10 us
  local copies, waits for them, and re-layouts: 104 us -> 21.7 us
  blocking collectives: 36.9 us -> 0 us
  other arithmetic: 40.9 us -> 11.3 us
  between operations: 2.59 us -> 14.8 us
    pallas_call x5 -> x7, Pallas kernels: 599 us -> 354 us  [the longest x1 87.9 us: attend_back(): pl.pallas_call(functools.partial(backward_kernel, heads, groups), grid=(b...]
    dot_general x36 -> x0, matrix products: 129 us -> none  [the longest x12 60 us: matmul(): return jnp.dot(left, right, preferred_element_type=F32)]
    ppermute x69 -> x8, starting transfers between devices: 132 us -> 18.5 us  [send(): return lax.ppermute(x, AXES, pairs)]
    ppermute x69 -> x8, waiting for transfers between devices: 108 us -> 0.02 us  [send(): return lax.ppermute(x, AXES, pairs)]
    psum x1 -> x0, blocking collectives: 36.9 us -> none  [per_device(): small = lax.psum(small, AXES)]
    unnamed x208 -> x28, local copies, waits for them, and re-layouts: 26.3 us -> 2.86 us
    convert_element_type x19 -> x1, other arithmetic: 23.3 us -> 1 us  [per_device(): part_both = lax.psum_scatter(grad_both.reshape((nd * nt,) + grad_both.sha...]
  transfers between devices with their start and end apart: 69 -> 10, of which waited for: 12 -> 1; matrix products, arithmetic and copies ran while one was open for 14% -> 6% of each run, Pallas kernels for 39% -> 52%
where the time goes in v2:
time: 438 us; the launch traced here: 430 us
  Pallas kernels  354 us (81%)
  local copies, waits for them, and re-layouts  21.7 us (5%)
  starting transfers between devices  18.5 us (4%)
  between operations  14.8 us (3%)
  other arithmetic  11.3 us (3%)
  waiting for transfers between devices  10 us (2%)
    pallas_call x1, Pallas kernels, attend_back(): pl.pallas_call(functools.partial(backward_kernel, heads, groups), grid=(b...  87.9 us
    pallas_call x1, Pallas kernels, finish(): pl.pallas_call(functools.partial(finish_kernel, nd, nt, share, inside), i...  85.4 us
    pallas_call x1, Pallas kernels, start(): pl.pallas_call(functools.partial(start_kernel, nd, nt, share, halves), in...  79.1 us
    pallas_call x1, Pallas kernels, feed_forward(): pl.pallas_call(functools.partial(middle_kernel, rb, nt), grid=(nt,), in_s...  51.5 us
    pallas_call x1, Pallas kernels, attend(): pl.pallas_call(functools.partial(forward_kernel, heads, groups), grid=(bl...  44.7 us
    ppermute x8, starting transfers between devices, send(): return lax.ppermute(x, AXES, pairs)  18.5 us
    all_gather x1, waiting for transfers between devices, per_device(): gathered = lax.all_gather(later, 'dp', axis=0, tiled=False)  9.98 us
  transfers between devices with their start and end apart: 10, of which 1 were waited for; matrix products, arithmetic and copies ran while one was open for 6% of the time, Pallas kernels for 52%

profile of v2, /device:TPU:0, one launch (start us, length us, event | category | flops | bytes accessed | tf_op | source)
XLA Modules:
  0.0 430.3 jit_solution(14547934993097952590)
XLA Ops:
  8.2 1.5 pad_maximum_fusion.1.refs_2_
  9.7 1.8 pad_maximum_fusion.refs_3_
  11.5 79.1 %start.1 = (bf16[1024,768]{1,0:T(8,128)(2,1)}, bf16[1024,768]{1,0:T(8,128)(2,1)}, bf16[8,2,128,768]{3,2,1,0:T(8,128)(2,1)}, bf16[8,2,128,768]{3,2,1,0:T(8,128)(2...) custom-call(bf16[2,2,2,128,768]{4,3,2,1,0:T(8,128)(2,1)} %bitcast.39, ...), custom_call_target="tpu_custom_call" | custom-call | tf_op jit(solution)/shard_map/start/pallas_call | solution.py:647
  90.7 2.7 split.1
  93.3 1.6 collective-permute-start
  95.0 7.4 %collective-permute-start.1 = (bf16[256,768]{1,0:T(8,128)(2,1)}, bf16[256,768]{1,0:T(8,128)(2,1)S(1)}, u32[]{:S(2)}, u32[]{:S(2)}) collective-permute-start(bf16[256,768]{1,0:T(8,128)(2,1)} %get-tuple-element.95), channel_id=1, source_target_pairs={{0,4},{1,2},{2,6},{3,0},{4,5},{5,3},{6,7},{7,1},{8,12},{9,10},{10,... | collective-permute-start | bytes 1179656 | tf_op jit(solution)/shard_map/ppermute | solution.py:54
  102.4 3.0 collective-permute-start.2
  105.7 0.7 mul.33.pre_ref
  106.5 0.7 reshape.175.post_ref
  107.2 44.7 %attend.1 = (bf16[1024,768]{1,0:T(8,128)(2,1)}, bf16[8,12,128,768]{3,2,1,0:T(8,128)(2,1)}, f32[8,1536,128]{2,1,0:T(8,128)}) custom-call(bf16[1024,768]{1,0:T(8,128)(2,1)} %get-tuple-element.86.q_ref, bf16[16,128,768]{2,1,0:T(8,128)(2,1)} %bitcast.44, bf16[16,128,768]{2,1,0:T(8,128)(2,1)} %bitcast.46, s32[16,128]{1,0:T(8,128)} %get-tuple-element.89.seg_low, ...), custom_call_target="tpu_custom_call" | custom-call | flops 38654705664 | bytes 37748736 | tf_op jit(solution)/shard_map/attend/pallas_call | solution.py:304
  151.9 1.3 slice.86.refs_3_
  153.2 10.0 %all-gather.3.cloned.1.call-done = bf16[32,224,768]{2,1,0:T(8,128)(2,1)} async-done(((bf16[4,224,768]{2,1,0:T(8,128)(2,1)}), bf16[32,224,768]{2,1,0:T(8,128)(2,1)}) %all-gather.3.cloned.1.call-update) | async-done | bytes 11010064 | tf_op jit(solution)/shard_map/all_gather | solution.py:1047
  163.2 2.4 slice.98
  165.6 8.3 %slice.99 = bf16[8,4,192,768]{3,2,1,0:T(8,128)(2,1)} slice(bf16[8,4,224,768]{3,2,1,0:T(8,128)(2,1)} %bitcast.33), slice={[0:8], [0:4], [0:192], [0:768]} | slice | bytes 18874368 | tf_op jit(solution)/shard_map/slice | solution.py:1049
  175.0 51.5 %feed_forward.1 = (bf16[256,768]{1,0:T(8,128)(2,1)}, bf16[256,768]{1,0:T(8,128)(2,1)}, bf16[256,768]{1,0:T(8,128)(2,1)}, bf16[256,768]{1,0:T(8,128)(2,1)}, f32[1...) custom-call(bf16[1024,768]{1,0:T(8,128)(2,1)} %get-tuple-element.103, ...), custom_call_target="tpu_custom_call" | custom-call | flops 28991029248 | bytes 9437184 | tf_op jit(solution)/shard_map/feed_forward/pallas_call | solution.py:769
  226.6 1.8 collective-permute-start.4
  228.4 4.1 collective-permute-start.5
  232.9 87.9 %attend_back.1 = (bf16[1024,768]{1,0:T(8,128)(2,1)}, bf16[16,128,768]{2,1,0:T(8,128)(2,1)}, bf16[16,128,768]{2,1,0:T(8,128)(2,1)}, f32[12,8,768]{2,1,0:T(8,128)}, f32[12,8,768]{2,1,0:T(8,128)}) custom-call(bf16[1024,768]{1,0:T(8,128)(2,1)} %get-tuple-element.86.q_ref, bf16[1024,768]{1,0:T(8,128)(2,1)} %get-tuple-element.104.g_ref, ...), custom_call_target="tpu_custom_call" | custom-call | flops 96636764160 | bytes 37748736 | tf_op jit(solution)/shard_map/attend_back/pallas_call | solution.py:421
  320.9 1.0 reduce_sum.32
  322.2 1.0 reduce_sum.45
  323.8 0.7 copy-done
  324.8 0.8 copy-done.3
  325.5 2.6 join.1
  328.2 85.4 %finish.1 = (bf16[2,2,2,128,768]{4,3,2,1,0:T(8,128)(2,1)}, f32[96,768]{1,0:T(8,128)}, f32[8,768]{1,0:T(8,128)}) custom-call(bf16[1024,768]{1,0:T(8,128)(2,1)} %get-tuple-element.103.refs_0_.x_ref, bf16[1024,768]{1,0:T(8,128)(2,1)} %get-tuple-element.107.dq_ref, bf16[8,2,128,768]{3,2,1,0:T(8,128)(2,1)} %bitcast.52, bf16[8,2,128,768]{3,2,1,0:T(8,128)(2,1)} %bitcast.53, ...), custom_call_target="tpu_custom_call" | custom-call | flops 14495514624 | bytes 12582912 | tf_op jit(solution)/shard_map/finish/pallas_call | solution.py:1003
  413.6 0.8 slice_reduce_fusion
  414.4 0.7 reshape_squeeze.4
  415.2 0.7 copy.34
  415.9 3.3 convert.2
  419.2 0.8 constant_dynamic-slice_fusion
  420.4 0.7 fusion
  421.2 1.0 convert_element_type.32
  422.2 0.8 slice_bitcast_fusion
  (67 shorter events, 4.6 us)
Async XLA Ops:
  7.2 98.3 %copy-start.7 = (bf16[12,12]{1,0:T(8,128)(2,1)S(1)}, bf16[12,12]{1,0:T(8,128)(2,1)}, u32[]{:S(2)}) copy-start(bf16[12,12]{1,0:T(8,128)(2,1)} %param.27) | copy-start | bytes 868
  7.2 156.0 %all-gather.3.cloned.1.call-start = ((), (), s32[]{:S(2)}) async-start(), calls=%async_computation.2 | async-start | bytes 12386304 | tf_op jit(solution)/shard_map/all_gather | solution.py:1047
  7.2 99.1 %copy-start.8 = (bf16[12,12]{1,0:T(8,128)(2,1)S(1)}, bf16[12,12]{1,0:T(8,128)(2,1)}, u32[]{:S(2)}) copy-start(bf16[12,12]{1,0:T(8,128)(2,1)} %param.28) | copy-start | bytes 868
  90.6 330.5 %reduce-scatter.2.cloned.1.call-start = ((), (), s32[]{:S(2)}) async-start(), calls=%async_computation.1 | async-start | bytes 9732096 | tf_op jit(solution)/shard_map/reduce_scatter | solution.py:1063
  93.3 80.5 %collective-permute-start = (bf16[256,768]{1,0:T(8,128)(2,1)}, bf16[256,768]{1,0:T(8,128)(2,1)S(1)}, u32[]{:S(2)}, u32[]{:S(2)}) collective-permute-start(bf16[256,768]{1,0:T(8,128)(2,1)} %get-tuple-element.94), channel_id=1, source_target_pairs={{0,0},{1,4},{2,2},{3,6},{4,1},{5,5},{6,3},{7,7},{8,8},{9,12},{10,1... | collective-permute-start | bytes 1179656 | tf_op jit(solution)/shard_map/ppermute | solution.py:54
  95.0 78.9 %collective-permute-start.1 = (bf16[256,768]{1,0:T(8,128)(2,1)}, bf16[256,768]{1,0:T(8,128)(2,1)S(1)}, u32[]{:S(2)}, u32[]{:S(2)}) collective-permute-start(bf16[256,768]{1,0:T(8,128)(2,1)} %get-tuple-element.95), channel_id=1, source_target_pairs={{0,4},{1,2},{2,6},{3,0},{4,5},{5,3},{6,7},{7,1},{8,12},{9,10},{10,... | collective-permute-start | bytes 1179656 | tf_op jit(solution)/shard_map/ppermute | solution.py:54
  102.4 71.5 %collective-permute-start.2 = (bf16[256,768]{1,0:T(8,128)(2,1)}, bf16[256,768]{1,0:T(8,128)(2,1)S(1)}, u32[]{:S(2)}, u32[]{:S(2)}) collective-permute-start(bf16[256,768]{1,0:T(8,128)(2,1)} %get-tuple-element.96), channel_id=1, source_target_pairs={{0,2},{1,6},{2,0},{3,4},{4,3},{5,7},{6,1},{7,5},{8,10},{9,14},{10,... | collective-permute-start | bytes 1179656 | tf_op jit(solution)/shard_map/ppermute | solution.py:54
  105.5 68.4 %collective-permute-start.3 = (bf16[256,768]{1,0:T(8,128)(2,1)}, bf16[256,768]{1,0:T(8,128)(2,1)S(1)}, u32[]{:S(2)}, u32[]{:S(2)}) collective-permute-start(bf16[256,768]{1,0:T(8,128)(2,1)} %get-tuple-element.97), channel_id=1, source_target_pairs={{0,6},{1,0},{2,4},{3,2},{4,7},{5,1},{6,5},{7,3},{8,14},{9,8},{10,1... | collective-permute-start | bytes 1179656 | tf_op jit(solution)/shard_map/ppermute | solution.py:54
  173.9 0.7 copy-start.10
  173.9 0.9 copy-start.11
  173.9 1.0 copy-start.12
  173.9 1.1 copy-start.13
  226.6 5.9 %copy-start.9 = (bf16[256,768]{1,0:T(8,128)(2,1)S(1)}, bf16[256,768]{1,0:T(8,128)(2,1)}, u32[]{:S(2)}) copy-start(bf16[256,768]{1,0:T(8,128)(2,1)} %get-tuple-element.101) | copy-start | bytes 1179652
  226.6 97.2 %collective-permute-start.4 = (bf16[256,768]{1,0:T(8,128)(2,1)}, bf16[256,768]{1,0:T(8,128)(2,1)S(1)}, u32[]{:S(2)}, u32[]{:S(2)}) collective-permute-start(bf16[256,768]{1,0:T(8,128)(2,1)} %get-tuple-element.98), channel_id=1, source_target_pairs={{0,0},{1,4},{2,2},{3,6},{4,1},{5,5},{6,3},{7,7},{8,8},{9,12},{10,1... | collective-permute-start | bytes 1179656 | tf_op jit(solution)/shard_map/ppermute | solution.py:54
  228.4 95.4 %collective-permute-start.5 = (bf16[256,768]{1,0:T(8,128)(2,1)}, bf16[256,768]{1,0:T(8,128)(2,1)S(1)}, u32[]{:S(2)}, u32[]{:S(2)}) collective-permute-start(bf16[256,768]{1,0:T(8,128)(2,1)} %get-tuple-element.99), channel_id=1, source_target_pairs={{0,3},{1,7},{2,1},{3,5},{4,0},{5,4},{6,2},{7,6},{8,11},{9,15},{10,... | collective-permute-start | bytes 1179656 | tf_op jit(solution)/shard_map/ppermute | solution.py:54
  232.4 91.4 %collective-permute-start.6 = (bf16[256,768]{1,0:T(8,128)(2,1)}, bf16[256,768]{1,0:T(8,128)(2,1)S(1)}, u32[]{:S(2)}, u32[]{:S(2)}) collective-permute-start(bf16[256,768]{1,0:T(8,128)(2,1)} %get-tuple-element.100), channel_id=1, source_target_pairs={{0,2},{1,6},{2,0},{3,4},{4,3},{5,7},{6,1},{7,5},{8,10},{9,14},{10,... | collective-permute-start | bytes 1179656 | tf_op jit(solution)/shard_map/ppermute | solution.py:54
  232.5 91.4 %collective-permute-start.7 = (bf16[256,768]{1,0:T(8,128)(2,1)S(1)}, bf16[256,768]{1,0:T(8,128)(2,1)S(1)}, u32[]{:S(2)}, u32[]{:S(2)}) collective-permute-start(bf16[256,768]{1,0:T(8,128)(2,1)S(1)} %copy-done.9), channel_id=1, source_target_pairs={{0,1},{1,5},{2,3},{3,7},{4,2},{5,6},{6,0},{7,4},{8,9},{9,13},{10,1... | collective-permute-start | bytes 1179656 | tf_op jit(solution)/shard_map/ppermute | solution.py:54
  232.9 87.9 %copy-start.5 = (f32[8,768]{1,0:T(8,128)S(1)}, f32[8,768]{1,0:T(8,128)}, u32[]{:S(2)}) copy-start(f32[8,768]{1,0:T(8,128)} %get-tuple-element.113) | copy-start | bytes 73732
  323.8 4.4 %copy-start.6 = (f32[8,768]{1,0:T(8,128)}, f32[8,768]{1,0:T(8,128)S(1)}, u32[]{:S(2)}) copy-start(f32[8,768]{1,0:T(8,128)S(1)} %scatter.14.small_ref) | copy-start | bytes 73732
  323.8 0.8 copy-start
  323.8 0.9 copy-start.1
  323.8 1.0 copy-start.2
  324.8 0.8 copy-start.3
  413.6 6.9 %copy-start.4 = (f32[96,768]{1,0:T(8,128)S(1)}, f32[96,768]{1,0:T(8,128)}, u32[]{:S(2)}) copy-start(f32[96,768]{1,0:T(8,128)} %get-tuple-element.117) | copy-start | bytes 884740
Sparse Core Ops, SparseCore 0:
  90.7 72.4 all-gather.2
  226.7 152.3 reduce-scatter.1

commit v3 on v2

v3 whole, which is shorter than its diff:
```python
import functools

import jax
import jax.numpy as jnp
from jax import lax
from jax.experimental import pallas as pl
from jax.experimental.pallas import tpu as pltpu
from jax.sharding import PartitionSpec as P

F32 = jnp.float32
BF16 = jnp.bfloat16
BLOCK = 128
TILE = 2 * BLOCK
FORWARD_GROUPS = 6
BACKWARD_GROUPS = 2
AXES = ("plane", "core", "tensor")


def matmul(left, right):
    return jnp.dot(left, right, preferred_element_type=F32)


def right_t(left, right):
    return lax.dot_general(left, right, (((1,), (1,)), ((), ())), preferred_element_type=F32)


def left_t(left, right):
    return lax.dot_general(left, right, (((0,), (0,)), ((), ())), preferred_element_type=F32)


def rms_scale(values):
    return lax.rsqrt(jnp.mean(values * values, axis=-1, keepdims=True) + 1e-06)


def rms_back(grad_norm, normed, scale, gain):
    scaled = grad_norm * gain
    return scale * (scaled - normed * jnp.mean(scaled * normed, axis=-1, keepdims=True))


def gelu_exact(values):
    return jax.nn.gelu(values, approximate=False)


def gelu_back(upper, grad):
    unused, pull = jax.vjp(gelu_exact, upper)
    return pull(grad)[0]


def send(x, to):
    nd, nt = 2 * lax.axis_size("plane"), lax.axis_size("tensor")
    pairs = []
    for d in range(nd):
        for t in range(nt):
            d2, t2 = to(d, t)
            pairs.append((d * nt + t, d2 * nt + t2))
    return lax.ppermute(x, AXES, pairs)


def by_shift(shift):
    nt = lax.axis_size("tensor")
    return lambda d, t: (d, (t + shift) % nt)


def by_bit(bit):
    return lambda d, t: (d ^ bit, t)


def gather(piece, bits):
    nt = lax.axis_size("tensor")
    have = {0: jnp.stack([piece] + [send(piece, by_shift(s)) for s in range(1, nt)])}
    for bit in bits:
        have.update({mask | bit: send(block, by_bit(bit)) for mask, block in have.items()})
    return [have[mask] for mask in range(len(have))]


def pick(x, index, axis):
    return lax.dynamic_index_in_dim(x, index, axis, keepdims=False)


def sum_to_owner(x, bits):
    nt, nd = x.shape[:2]
    d, t = 2 * lax.axis_index("plane") + lax.axis_index("core"), lax.axis_index("tensor")
    rest = x.shape[2:]
    names = [1 << k for k in range(nd.bit_length() - 1)][::-1]
    x = x.reshape((nt,) + (2,) * len(names) + rest)
    for bit in bits:
        axis = 1 + names.index(bit)
        names.remove(bit)
        mine = (d // bit) % 2
        got = send(pick(x, 1 - mine, axis), by_bit(bit))
        x = pick(x, mine, axis).astype(F32) + got.astype(F32)
        if names or nt > 1:
            x = x.astype(BF16)
    total = pick(x, t, 0).astype(F32)
    for shift in range(1, nt):
        total = total + send(pick(x, lax.rem(t + shift, nt), 0), by_shift(shift)).astype(F32)
    return total


def seat(turn):
    nt = lax.axis_size("tensor")
    t, core = lax.axis_index("tensor"), lax.axis_index("core")
    block = lax.rem(turn + t, nt)
    source = lax.rem(2 * (t // 2) + core + nt - turn, nt)
    return block, source


def turn_to(turn):
    nt = lax.axis_size("tensor")

    def to(d, t):
        block = (turn + t) % nt
        return d - d % 2 + block % 2, 2 * (block // 2) + d % 2

    return to


def turn_back(turn):
    nt = lax.axis_size("tensor")

    def to(d, t):
        return d - d % 2 + t % 2, (2 * (t // 2) + d % 2 + nt - turn) % nt

    return to


def split_kernel(x_ref, *outs):
    for turn, out in enumerate(outs):
        block = seat(turn)[0]
        out[...] = x_ref[block // 2, :, block % 2].reshape(out.shape)


def join_kernel(*refs):
    out = refs[-1]
    for turn, piece in enumerate(refs[:-1]):
        block = seat(turn)[0]
        out[block // 2, :, block % 2] = piece[...].reshape(out.shape[1], BLOCK, out.shape[4])


def to_sequences(x):
    micro, _, rows, width = x.shape
    nt = lax.axis_size("tensor")
    pieces = pl.pallas_call(
        split_kernel, out_shape=[jax.ShapeDtypeStruct((rows // 2, width), x.dtype)] * nt, name="split"
    )(x.reshape(micro, rows // TILE, 2, BLOCK, width))
    return [send(piece, turn_to(turn)) for turn, piece in enumerate(pieces)]


def from_sequences(pieces, micro):
    half, width = pieces[0].shape
    back = [send(piece, turn_back(turn)) for turn, piece in enumerate(pieces)]
    out = pl.pallas_call(
        join_kernel,
        out_shape=jax.ShapeDtypeStruct((micro, half // BLOCK, 2, BLOCK, width), pieces[0].dtype),
        name="join",
    )(*back)
    return out.reshape(micro, 1, 2 * half, width)


def arrive(step, sources, scratches, sems, seg_ref, seg_s):
    blocks = sources[0].shape[0]
    copies = []
    for k, (source, scratch) in enumerate(zip(sources, scratches)):
        for part in range(blocks // 2):
            rows = pl.ds(2 * part, 2)
            there = scratch.at[pl.ds(2 * part + 1, 2)]
            copies.append((part, pltpu.make_async_copy(source.at[rows], there, sems.at[k, part])))

    @pl.when(step == 0)
    def _():
        for _, copy in copies:
            copy.start()
        seg_s[0] = jnp.full((1, BLOCK), -1, jnp.int32)
        seg_s[1:] = seg_ref[...]
        for scratch in scratches:
            scratch[0] = jnp.zeros(scratch.shape[1:], BF16)

    for part, copy in copies:
        pl.when(step == part)(copy.wait)


def reach(block, seg_low):
    first = seg_low[block, 0]
    before = 0
    for k in range(seg_low.shape[0]):
        before += (seg_low[k, BLOCK - 1] < first).astype(jnp.int32)
    return (block + 2 - before) // 2


def rows_of(block, seg_s):
    return jnp.broadcast_to(seg_s[block + 1], (BLOCK, BLOCK)).T


def row_mask(row_seg, first, block, seg_s):
    row = lax.broadcasted_iota(jnp.int32, (BLOCK, BLOCK), 0)
    col = lax.broadcasted_iota(jnp.int32, (BLOCK, BLOCK), 1)
    masks = []
    for k in range(2):
        ahead = (first + k - 1 - block) * BLOCK
        allowed = (row_seg == seg_s[first + k]) & (col + ahead <= row)
        masks.append(jnp.where(allowed, 0.0, -1e30).astype(F32))
    return jnp.concatenate(masks, axis=1)


def forward_kernel(
    heads, groups, most, q_ref, k_all, v_all, seg_low, seg_ref, pre_ref, post_ref,
    att_ref, u_ref, lse_ref, k_s, v_s, seg_s, qp_s, m_s, s_s, sems,
):
    step = pl.program_id(0)
    core = lax.axis_index("core")
    block = 2 * step + core
    width = q_ref.shape[1]
    arrive(step, [k_all, v_all], [k_s, v_s], sems, seg_ref, seg_s)
    tiles = reach(block, seg_low)
    row_seg = rows_of(block, seg_s)

    def scores(left, first, mask):
        keys = k_s[pl.ds(first, 2)].reshape(TILE, -1)
        s = right_t(left, keys).reshape(left.shape[0] // BLOCK, BLOCK, TILE)
        return (s + mask[None]).reshape(left.shape[0], TILE)

    def close(g, per, top, total, u, att):
        size = per * BLOCK
        lse_ref[0, g * size : (g + 1) * size, :] = jnp.broadcast_to(top + jnp.log(total), (size, BLOCK))
        for k in range(per):
            h = g * per + k
            part = u[k * BLOCK : (k + 1) * BLOCK]
            u_ref[0, h] = part.astype(BF16)
            att = att + part * post_ref[h : h + 1, :]
        return att

    @pl.when(tiles == 1)
    def _():
        per = heads // groups
        query = q_ref[...]
        mask = row_mask(row_seg, block, block, seg_s)
        att = jnp.zeros((BLOCK, width), F32)
        values = v_s[pl.ds(block, 2)].reshape(TILE, -1)
        for g in range(groups):
            left = jnp.concatenate([query * pre_ref[h : h + 1, :] for h in range(g * per, (g + 1) * per)])
            s = scores(left, block, mask)
            top = jnp.max(s, axis=-1, keepdims=True)
            p = jnp.exp(s - top)
            total = jnp.sum(p, axis=-1, keepdims=True)
            u = matmul((p * (1.0 / total)).astype(BF16), values)
            att = close(g, per, top, total, u, att)
        att_ref[...] = att.astype(BF16)

    @pl.when(tiles > 1)
    def _():
        query = q_ref[...]
        for h in range(heads):
            qp_s[h * BLOCK : (h + 1) * BLOCK, :] = query * pre_ref[h : h + 1, :]
        m_s[...] = jnp.full(m_s.shape, -3e38, F32)
        split = 2
        size = heads // split * BLOCK

        def meet(tile, carry):
            first = block - 2 * tile
            mask = row_mask(row_seg, first, block, seg_s)
            for g in range(split):
                rows = slice(g * size, (g + 1) * size)
                s = scores(qp_s[rows, :], first, mask)
                s_s[tile, rows, :] = s
                m_s[rows, :] = jnp.maximum(m_s[rows, :], jnp.maximum(s[:, :BLOCK], s[:, BLOCK:]))
            return carry

        lax.fori_loop(0, tiles, meet, 0)

    for n in range(2, most + 1):

        @pl.when(tiles == n)
        def _(n=n):
            per = heads // groups
            size = per * BLOCK
            values = v_s[pl.ds(block - 2 * n + 2, 2 * n)].reshape(n * TILE, -1)
            att = jnp.zeros((BLOCK, width), F32)
            for g in range(groups):
                rows = slice(g * size, (g + 1) * size)
                top = jnp.max(m_s[rows, :], axis=-1, keepdims=True)
                parts = [jnp.exp(s_s[tile, rows, :] - top) for tile in range(n)]
                total = jnp.sum(sum(p[:, :BLOCK] + p[:, BLOCK:] for p in parts), axis=-1, keepdims=True)
                p = jnp.concatenate([part.astype(BF16) for part in parts[::-1]], axis=1)
                u = matmul(p, values) * (1.0 / total)
                att = close(g, per, top, total, u, att)
            att_ref[...] = att.astype(BF16)


def whole(shape):
    return pl.BlockSpec(shape, lambda i: (0,) * len(shape), pipeline_mode=pl.Buffered(1))


def cost(flops, moved):
    return pl.CostEstimate(flops=int(flops), bytes_accessed=int(moved), transcendentals=0)


ANY = pl.BlockSpec(memory_space=pl.ANY)
SCALARS = pl.BlockSpec(memory_space=pltpu.SMEM)


def attend(query, k_all, v_all, segs, pre, post):
    heads, width = pre.shape
    rows, stack = query.shape[0], heads * BLOCK
    blocks = rows // BLOCK
    groups = FORWARD_GROUPS
    most = (1024 // BLOCK + 2) // 2
    by_block = pl.BlockSpec((BLOCK, width), lambda i: (i, 0))
    return pl.pallas_call(
        functools.partial(forward_kernel, heads, groups, most),
        grid=(blocks,),
        in_specs=[
            by_block, ANY, ANY, SCALARS, whole((2 * blocks, 1, BLOCK)), whole(pre.shape), whole(post.shape),
        ],
        out_specs=[
            by_block,
            pl.BlockSpec((1, heads, BLOCK, width), lambda i: (i, 0, 0, 0)),
            pl.BlockSpec((1, stack, BLOCK), lambda i: (i, 0, 0)),
        ],
        scratch_shapes=[
            pltpu.VMEM((2 * blocks + 1, BLOCK, width), BF16),
            pltpu.VMEM((2 * blocks + 1, BLOCK, width), BF16),
            pltpu.VMEM((2 * blocks + 1, 1, BLOCK), jnp.int32),
            pltpu.VMEM((stack, width), BF16),
            pltpu.VMEM((stack, BLOCK), F32),
            pltpu.VMEM((most, stack, TILE), F32),
            pltpu.SemaphoreType.DMA((2, blocks)),
        ],
        out_shape=[
            jax.ShapeDtypeStruct((rows, width), BF16),
            jax.ShapeDtypeStruct((blocks, heads, BLOCK, width), BF16),
            jax.ShapeDtypeStruct((blocks, stack, BLOCK), F32),
        ],
        compiler_params=pltpu.CompilerParams(vmem_limit_bytes=60 << 20),
        cost_estimate=cost(4 * rows * 1024 * stack // BLOCK * width, 4 * rows * stack // BLOCK * width),
        name="attend",
    )(query, k_all, v_all, segs, segs[:, None, :], pre, post)


def backward_kernel(
    heads, groups, q_ref, g_ref, u_ref, lse_ref, k_all, v_all, seg_low, seg_ref, pre_ref, post_ref,
    dq_ref, dk_ref, dv_ref, dpre_ref, dpost_ref,
    k_s, v_s, seg_s, dk_s, dv_s, qp_s, gp_s, d_s, t_s, sems,
):
    step = pl.program_id(0)
    core = lax.axis_index("core")
    block = 2 * step + core
    per = heads // groups
    size = per * BLOCK
    width = q_ref.shape[1]
    arrive(step, [k_all, v_all], [k_s, v_s], sems, seg_ref, seg_s)

    @pl.when(step == 0)
    def _():
        dk_s[...] = jnp.zeros(dk_s.shape, F32)
        dv_s[...] = jnp.zeros(dv_s.shape, F32)
        dpre_ref[...] = jnp.zeros(dpre_ref.shape, F32)
        dpost_ref[...] = jnp.zeros(dpost_ref.shape, F32)

    tiles = reach(block, seg_low)
    row_seg = rows_of(block, seg_s)

    def opening(g):
        query, grad_low = q_ref[...], g_ref[...]
        grad = grad_low.astype(F32)
        left, right, terms = [], [], []
        for h in range(g * per, (g + 1) * per):
            gain = post_ref[h : h + 1, :]
            left.append(query * pre_ref[h : h + 1, :])
            right.append(grad_low * gain.astype(BF16))
            both = grad * u_ref[0, h].astype(F32)
            terms.append(jnp.sum(both * gain, axis=-1, keepdims=True))
            dpost_ref[h] += jnp.sum(both.reshape(BLOCK // 8, 8, -1), axis=0)
        return jnp.concatenate(left), jnp.concatenate(right), jnp.concatenate(terms)

    def closing(h, part, dq):
        dpre_ref[h] += jnp.sum((q_ref[...].astype(F32) * part).reshape(BLOCK // 8, 8, -1), axis=0)
        return dq + part * pre_ref[h : h + 1, :].astype(F32)

    def tile_part(first, mask, g, left, right, term):
        keys = k_s[pl.ds(first, 2)].reshape(TILE, -1)
        values = v_s[pl.ds(first, 2)].reshape(TILE, -1)
        s = (right_t(left, keys).reshape(per, BLOCK, TILE) + mask[None]).reshape(size, TILE)
        top = lse_ref[0, g * size : (g + 1) * size, :]
        p = jnp.exp(s - jnp.concatenate([top, top], axis=1))
        dw = right_t(right, values)
        ds = (p * (dw - term)).astype(BF16)
        return matmul(ds, keys), left_t(ds, left), left_t(p.astype(BF16), right)

    def add_up(first, dk, dv):
        dk_s[pl.ds(first, 2)] += dk.reshape(2, BLOCK, -1)
        dv_s[pl.ds(first, 2)] += dv.reshape(2, BLOCK, -1)

    @pl.when(tiles == 1)
    def _():
        mask = row_mask(row_seg, block, block, seg_s)
        dk = dv = jnp.zeros((TILE, width), F32)
        dq = jnp.zeros((BLOCK, width), F32)
        for g in range(groups):
            part, a, b = tile_part(block, mask, g, *opening(g))
            dk, dv = dk + a, dv + b
            for k in range(per):
                dq = closing(g * per + k, part[k * BLOCK : (k + 1) * BLOCK], dq)
        add_up(block, dk, dv)
        dq_ref[...] = dq.astype(BF16)

    @pl.when(tiles > 1)
    def _():
        mask = row_mask(row_seg, block, block, seg_s)
        dk = dv = jnp.zeros((TILE, width), F32)
        for g in range(groups):
            rows = slice(g * size, (g + 1) * size)
            left, right, term = opening(g)
            qp_s[rows, :], gp_s[rows, :] = left, right
            d_s[rows, :] = jnp.broadcast_to(term, (size, BLOCK))
            t_s[rows, :], a, b = tile_part(block, mask, g, left, right, term)
            dk, dv = dk + a, dv + b
        add_up(block, dk, dv)

        def more(tile, carry):
            first = block - 2 * tile
            mask = row_mask(row_seg, first, block, seg_s)
            dk = dv = jnp.zeros((TILE, width), F32)
            for g in range(groups):
                rows = slice(g * size, (g + 1) * size)
                term = jnp.concatenate([d_s[rows, :]] * 2, axis=1)
                part, a, b = tile_part(first, mask, g, qp_s[rows, :], gp_s[rows, :], term)
                t_s[rows, :] += part
                dk, dv = dk + a, dv + b
            add_up(first, dk, dv)
            return carry

        lax.fori_loop(1, tiles, more, 0)
        dq = jnp.zeros((BLOCK, width), F32)
        for h in range(heads):
            dq = closing(h, t_s[h * BLOCK : (h + 1) * BLOCK, :], dq)
        dq_ref[...] = dq.astype(BF16)

    @pl.when(step == pl.num_programs(0) - 1)
    def _():
        for k in range(dk_ref.shape[0]):
            dk_ref[k] = dk_s[k + 1].astype(BF16)
            dv_ref[k] = dv_s[k + 1].astype(BF16)


def attend_back(query, grad, u, lse, k_all, v_all, segs, pre, post):
    heads, width = pre.shape
    rows, stack = query.shape[0], heads * BLOCK
    blocks = rows // BLOCK
    groups = BACKWARD_GROUPS
    by_block = pl.BlockSpec((BLOCK, width), lambda i: (i, 0))
    return pl.pallas_call(
        functools.partial(backward_kernel, heads, groups),
        grid=(blocks,),
        in_specs=[
            by_block,
            by_block,
            pl.BlockSpec((1, heads, BLOCK, width), lambda i: (i, 0, 0, 0)),
            pl.BlockSpec((1, stack, BLOCK), lambda i: (i, 0, 0)),
            ANY, ANY, SCALARS, whole((2 * blocks, 1, BLOCK)), whole(pre.shape), whole(post.shape),
        ],
        out_specs=[
            by_block,
            whole((2 * blocks, BLOCK, width)),
            whole((2 * blocks, BLOCK, width)),
            whole((heads, 8, width)),
            whole((heads, 8, width)),
        ],
        scratch_shapes=[
            pltpu.VMEM((2 * blocks + 1, BLOCK, width), BF16),
            pltpu.VMEM((2 * blocks + 1, BLOCK, width), BF16),
            pltpu.VMEM((2 * blocks + 1, 1, BLOCK), jnp.int32),
            pltpu.VMEM((2 * blocks + 1, BLOCK, width), F32),
            pltpu.VMEM((2 * blocks + 1, BLOCK, width), F32),
            pltpu.VMEM((stack, width), BF16),
            pltpu.VMEM((stack, width), BF16),
            pltpu.VMEM((stack, BLOCK), F32),
            pltpu.VMEM((stack, width), F32),
            pltpu.SemaphoreType.DMA((2, blocks)),
        ],
        out_shape=[
            jax.ShapeDtypeStruct((rows, width), BF16),
            jax.ShapeDtypeStruct((2 * blocks, BLOCK, width), BF16),
            jax.ShapeDtypeStruct((2 * blocks, BLOCK, width), BF16),
            jax.ShapeDtypeStruct((heads, 8, width), F32),
            jax.ShapeDtypeStruct((heads, 8, width), F32),
        ],
        compiler_params=pltpu.CompilerParams(vmem_limit_bytes=62 << 20),
        cost_estimate=cost(10 * rows * 1024 * stack // BLOCK * width, 4 * rows * stack // BLOCK * width),
        name="attend_back",
    )(query, grad, u, lse, k_all, v_all, segs, segs[:, None, :], pre, post)


MESH = pl.DeviceIdType.MESH


def device(place):
    d, t = place
    return d // 2, d % 2, t


def flip(index, bit):
    return index + bit - 2 * bit * ((index // bit) % 2)


def greet(nd, nt, d, t):
    barrier = pltpu.get_barrier_semaphore()
    core = d % 2
    partners = [(d, lax.rem(t + s, nt)) for s in range(1, nt)]
    partners += [(flip(d, 1), lax.rem(t + s, nt)) for s in range(nt)]
    bit = 2
    while bit < nd:
        partners.append((flip(d, bit), t))
        bit *= 2
    for partner in partners:
        pl.semaphore_signal(barrier, inc=1, device_id=device(partner), device_id_type=MESH)
    pl.semaphore_wait(barrier, len(partners))


def remote(src, dst, send_sem, recv_sem, to):
    return pltpu.make_async_remote_copy(
        src_ref=src, dst_ref=dst, send_sem=send_sem, recv_sem=recv_sem, device_id=device(to), device_id_type=MESH
    )


def start_kernel(
    nd, nt, share, halves, *refs,
):
    if halves:
        tokens, segments, bundle, later = refs[:4]
        x_out, q_out, k_out, v_out, seg_out, w_out, o_out, gain_out, later_out = refs[4:13]
        wg_s, w_send, w_recv, w_self = refs[13:17]
    else:
        tokens, segments, w_out, gain_out, later = refs[:5]
        x_out, q_out, k_out, v_out, seg_out, later_out = refs[5:11]
    (l_send, l_recv, x_s, kv_s, x_send, x_recv, x_self, kv_send, kv_recv, kv_self, seg_send, seg_recv, seg_self) = refs[-13:]
    d, t = 2 * lax.axis_index("plane") + lax.axis_index("core"), lax.axis_index("tensor")
    core = d % 2
    width = x_out.shape[1]
    micro = tokens.shape[0]
    per = tokens.shape[1]
    greet(nd, nt, d, t)

    if halves:
        own = pltpu.make_async_copy(bundle, wg_s.at[d, t], w_self)
        own.start()
        z_copies = []
        for s in range(1, nt):
            copy = remote(bundle, wg_s.at[d, t], w_send.at[0, 0, s], w_recv.at[0, 0, s], (d, lax.rem(t + s, nt)))
            copy.start()
            z_copies.append(copy)
        own.wait()
        for copy in z_copies:
            copy.wait()

    sends = []
    for m in range(micro):
        for c in range(2):
            to = (d - core + c, 2 * m + core)
            here = (to[0] == d) & (to[1] == t)
            src, dst = tokens.at[m, :, c], x_s.at[pl.ds(per * t, per)]
            far = remote(src, dst, x_send.at[2 * m + c], x_recv.at[t], to)
            near = pltpu.make_async_copy(src, dst, x_self)
            pl.when(jnp.logical_not(here))(far.start)
            pl.when(here)(near.start)
            sends.append((here, far, near))

    holder = t % 2 == core
    seg_here = pltpu.make_async_copy(segments.at[t // 2], seg_out, seg_self)
    seg_there = remote(segments.at[t // 2], seg_out, seg_send, seg_recv, (flip(d, 1), t))

    @pl.when(holder)
    def _():
        seg_here.start()
        seg_there.start()

    l_copies = []
    for s in range(1, nt):
        l_copies.append(remote(later, later_out.at[s - 1], l_send.at[s], l_recv.at[s], (d, lax.rem(t + s, nt))))
    for copy in l_copies:
        copy.start()

    if halves:
        bits = [1 << k for k in range(1, nd.bit_length() - 1)]
        routes = [bits + [1], bits[::-1] + [1]]
        have = [[0] for _ in halves]
        for stage in range(len(bits) + 1):
            copies = []
            for h, (lo, hi) in enumerate(halves):
                bit = routes[h][stage]
                for k, mask in enumerate(have[h]):
                    slab = d
                    for b in [1 << j for j in range(nd.bit_length() - 1)]:
                        if mask & b:
                            slab = flip(slab, b)
                    ref = wg_s.at[slab, :, pl.ds(lo, hi - lo)]
                    copies.append(
                        remote(ref, ref, w_send.at[1 + h, stage, k], w_recv.at[1 + h, stage, k], (flip(d, bit), t))
                    )
                have[h] = have[h] + [mask | bit for mask in have[h]]
            for copy in copies:
                copy.start()
            for copy in copies:
                copy.wait()

        gains = jnp.zeros((8, width), F32)
        for pair in range(nd * nt // 2):
            slabs = [wg_s[(2 * pair + e) // nt, (2 * pair + e) % nt].astype(F32) for e in range(2)]
            for k in range(3):
                both = jnp.concatenate([slab[k * share : (k + 1) * share] for slab in slabs])
                w_out[2 * pair * share : 2 * (pair + 1) * share, k * width : (k + 1) * width] = both.astype(BF16)
            both = jnp.concatenate([slab[3 * share : 4 * share] for slab in slabs])
            o_out[2 * pair * share : 2 * (pair + 1) * share, :] = both.astype(BF16)
            gains = gains + (slabs[0] + slabs[1])[4 * share : 4 * share + 8]
        gain_out[...] = gains

    kv_copies = []
    gain = gain_out[:1]
    for s in range(nt):
        source = lax.rem(t + s, nt)
        here = (source == t) & holder
        arrival = remote(
            x_s.at[pl.ds(per * source, per)], x_s.at[pl.ds(per * source, per)], x_send.at[0], x_recv.at[source], (flip(d, 1), t)
        )
        local = pltpu.make_async_copy(tokens.at[0, :, 0], x_s.at[pl.ds(per * source, per)], x_self)
        pl.when(jnp.logical_not(here))(arrival.wait_recv)
        pl.when(here)(local.wait)
        x = x_s[pl.ds(per * source, per)].reshape(per * BLOCK, width)
        rows = pl.ds(pl.multiple_of(source * per * BLOCK, per * BLOCK), per * BLOCK)
        x_out[rows, :] = x
        x = x.astype(F32)
        h = (x * rms_scale(x) * gain).astype(BF16)
        q_out[rows, :] = matmul(h, w_out[:, :width]).astype(BF16)
        for k, out in enumerate((k_out, v_out)):
            value = matmul(h, w_out[:, (k + 1) * width : (k + 2) * width]).astype(BF16)
            kv_s[k, s] = value.reshape(per, BLOCK, width)
            dst = out.at[pl.ds(per * source, per), core]
            near = pltpu.make_async_copy(kv_s.at[k, s], dst, kv_self.at[k, s])
            far = remote(kv_s.at[k, s], dst, kv_send.at[k, s], kv_recv.at[k, s], (flip(d, 1), t))
            near.start()
            far.start()
            kv_copies += [near, far]
    for copy in kv_copies + l_copies:
        copy.wait()
    for here, far, near in sends:
        pl.when(jnp.logical_not(here))(far.wait_send)

    @pl.when(holder)
    def _():
        seg_here.wait()
        seg_there.wait_send()

    @pl.when(jnp.logical_not(holder))
    def _():
        seg_there.wait_recv()


def start(tokens, segments, bundle, later, share):
    micro, _, rows, width = tokens.shape
    nd, nt = 2 * lax.axis_size("plane"), lax.axis_size("tensor")
    count = rows * nt // 2
    blocks = count // BLOCK
    per = blocks // nt
    length = bundle.shape[0]
    dma = pltpu.SemaphoreType.DMA
    vmem = pl.BlockSpec(memory_space=pltpu.VMEM)
    shaped = jax.ShapeDtypeStruct
    most = max(nd // 2, nt)
    inside = 2 * share % 16 == 0 and length >= 32
    middle = length // 32 * 16
    if inside:
        halves, given = [(0, middle), (middle, length)], [bundle]
        gathered_specs = [vmem, vmem, vmem]
        gathered = [shaped((width, 3 * width), BF16), shaped((width, width), BF16), shaped((8, width), F32)]
        scratch = [
            pltpu.VMEM((nd, nt, length, width), BF16),
            dma((3, nd.bit_length(), most)), dma((3, nd.bit_length(), most)), dma,
        ]
    else:
        slabs = lax.all_gather(bundle, AXES, axis=0, tiled=False)
        w_qkv = slabs[:, : 3 * share].reshape(nd * nt, 3, share, width).transpose(0, 2, 1, 3)
        w_qkv = w_qkv.reshape(width, 3 * width)
        w_out = slabs[:, 3 * share : 4 * share].reshape(width, width)
        gains = jnp.sum(slabs[:, 4 * share : 4 * share + 8].astype(F32), axis=0)
        halves, given, gathered_specs, gathered, scratch = [], [w_qkv, gains], [], [], []
    results = pl.pallas_call(
        functools.partial(start_kernel, nd, nt, share, halves),
        in_specs=[ANY, ANY] + ([ANY] if inside else [vmem, vmem]) + [ANY],
        out_specs=[vmem, vmem, ANY, ANY, ANY] + gathered_specs + [ANY],
        out_shape=[
            shaped((count, width), BF16),
            shaped((count, width), BF16),
            shaped((blocks, 2, BLOCK, width), BF16),
            shaped((blocks, 2, BLOCK, width), BF16),
            shaped((2 * blocks, BLOCK), jnp.int32),
            *gathered,
            shaped((nt - 1,) + later.shape, BF16),
        ],
        scratch_shapes=scratch + [
            dma((nt,)), dma((nt,)),
            pltpu.VMEM((blocks, BLOCK, width), BF16),
            pltpu.VMEM((2, nt, per, BLOCK, width), BF16),
            dma((nt,)), dma((nt,)), dma,
            dma((2, nt)), dma((2, nt)), dma((2, nt)),
            dma, dma, dma,
        ],
        compiler_params=pltpu.CompilerParams(
            collective_id=0, has_side_effects=True, vmem_limit_bytes=56 << 20
        ),
        name="start",
    )(
        tokens.reshape(micro, rows // TILE, 2, BLOCK, width),
        segments.reshape(micro, 2 * blocks, BLOCK),
        *given,
        later,
    )
    return results if inside else (*results[:5], w_qkv, w_out, gains, results[5])


def gelu_parts(v):
    t = 1.0 / (1.0 + 0.23164189 * jnp.abs(v))
    bell = jnp.exp(-0.5 * v * v)
    series = t * (0.127414796 + t * (-0.142248368 + t * (0.7107068705 + t * (-0.7265760135 + t * 0.5307027145))))
    tail = series * bell
    return jnp.where(v < 0.0, tail, 1.0 - tail), 0.3989422804 * bell


def middle_kernel(rb, nd, nt, share, inside, *refs):
    x_ref, att_ref, w_out, gain_ref, own_ref, rest_ref = refs[:6]
    dys, refs = refs[6 : 6 + nt], refs[6 + nt :]
    outs, refs = refs[:nt], refs[nt:]
    after_ref, datt_ref, dwo_ref, dgain_ref, part_ref = refs[:5]
    dy_ref, h_s, ht_s, dyt_s, o_s, dh_s, hid_s, dhid_s, w_s, sems = refs[5:15]
    if inside:
        g_s, core_s, plane_s, c_send, c_recv, p_send, p_recv = refs[15:]
    step = pl.program_id(0)
    d, t = 2 * lax.axis_index("plane") + lax.axis_index("core"), lax.axis_index("tensor")
    count, width = x_ref.shape
    parts = range(0, count, rb)
    bits = [1 << k for k in range(1, nd.bit_length() - 1)]
    routes = [bits, bits[::-1]]

    @pl.when(step == 0)
    def _():
        if inside:
            greet(nd, nt, d, t)
        copies = []
        for turn, dy in enumerate(dys):
            rows = pl.ds(pl.multiple_of(seat(turn)[1] * (count // nt), count // nt), count // nt)
            copies.append(pltpu.make_async_copy(dy, dy_ref.at[rows], sems.at[turn]))
        for copy in copies:
            copy.start()
        for r in parts:
            rows = slice(r, r + rb)
            after = x_ref[rows, :].astype(F32) + matmul(att_ref[rows, :], w_out[...])
            after_ref[rows, :] = after
            o_s[rows, :] = after
            h = (after * rms_scale(after) * gain_ref[...]).astype(BF16)
            h_s[rows, :] = h
            ht_s[:, rows] = h.T
            dh_s[rows, :] = jnp.zeros((rb, width), F32)
        for k in range(2):
            w_s[k] = own_ref[:, k * share : (k + 1) * share]
        for copy in copies:
            copy.wait()
        for r in parts:
            rows = slice(r, r + rb)
            dyt_s[:, rows] = dy_ref[rows, :].T

    @pl.when((step > 0) & (step < nt))
    def _():
        for k in range(2):
            w_s[k] = rest_ref[:, 0, k * share : (k + 1) * share]

    def core_copies(slot):
        return [
            remote(
                g_s.at[slot, flips(flip(d, 1), mask)], core_s.at[slot, j],
                c_send.at[slot, j], c_recv.at[slot, j], (flip(d, 1), t),
            )
            for j, mask in enumerate(masks_of(bits))
        ]

    def plane_copies(slot, stage):
        copies = []
        for h in range(2):
            bit, rows = routes[h][stage], pl.ds(h * share, share)
            for j, mask in enumerate(masks_of(routes[h][stage + 1 :])):
                copies.append(
                    remote(
                        g_s.at[slot, flips(flip(d, bit), mask), rows], plane_s.at[slot, stage, j, rows],
                        p_send.at[slot, stage, h, j], p_recv.at[slot, stage, h, j], (flip(d, bit), t),
                    )
                )
        return copies

    def core_done(k):
        slot = lax.rem(k, 2)
        for copy in core_copies(slot):
            copy.wait()
        for j, mask in enumerate(masks_of(bits)):
            mine = flips(d, mask)
            g_s[slot, mine] = (g_s[slot, mine].astype(F32) + core_s[slot, j].astype(F32)).astype(BF16)
        for copy in plane_copies(slot, 0):
            copy.start()

    def plane_done(k, stage):
        slot = lax.rem(k, 2)
        for copy in plane_copies(slot, stage):
            copy.wait()
        for h in range(2):
            rows = slice(h * share, (h + 1) * share)
            for j, mask in enumerate(masks_of(routes[h][stage + 1 :])):
                mine = flips(d, mask)
                total = g_s[slot, mine, rows].astype(F32) + plane_s[slot, stage, j, rows].astype(F32)
                g_s[slot, mine, rows] = total.astype(BF16)
        if stage + 1 < len(bits):
            for copy in plane_copies(slot, stage + 1):
                copy.start()
        else:
            part_ref[lax.rem(t + nt - k, nt)] = g_s[slot, d]

    def when(condition, stage, *args):
        if inside:
            pl.when(condition)(functools.partial(stage, *args))

    @pl.when(step < nt)
    def _():
        up, down = (w_s[k].reshape(width, -1) for k in range(2))
        for point, r in enumerate(parts):
            rows = slice(r, r + rb)
            v = matmul(h_s[rows, :], up)
            cumulative, density = gelu_parts(v)
            hid_s[rows, :] = (v * cumulative).astype(BF16)
            d_hidden = matmul(dy_ref[rows, :], down) * (cumulative + v * density)
            dhid_s[rows, :] = d_hidden.astype(BF16)
            if point == 1:
                when(step >= 1, core_done, step - 1)
        when(step >= 2, plane_done, step - 2, len(bits) - 1)
        slot = lax.rem(step, 2)
        for r in range(0, width, 2 * share):
            rows = slice(r, r + 2 * share)
            for k, (left, right) in enumerate(((ht_s, dhid_s), (dyt_s, hid_s))):
                both = matmul(left[rows, :], right[...]).astype(BF16)
                for e in range(2):
                    grad = both[e * share : (e + 1) * share]
                    if inside:
                        g_s[slot, r // share + e, k * share : (k + 1) * share] = grad
                    else:
                        part_ref[r // share + e, 0, k] = grad
        if inside:
            for copy in core_copies(slot):
                copy.start()
        for r in parts:
            rows = slice(r, r + rb)
            o_s[rows, :] += right_t(hid_s[rows, :], down)
            dh_s[rows, :] += right_t(dhid_s[rows, :], up)
        for stage in range(len(bits) - 1):
            when(step >= 1, plane_done, step - 1, stage)

    @pl.when(step == nt)
    def _():
        gain = gain_ref[...]
        total = jnp.zeros((8, width), F32)
        for turn, out in enumerate(outs):
            rows = pl.ds(pl.multiple_of(seat(turn)[1] * (count // nt), count // nt), count // nt)
            out[...] = o_s[rows, :].astype(BF16)
        for point, r in enumerate(parts):
            rows = slice(r, r + rb)
            after = after_ref[rows, :]
            scale = rms_scale(after)
            normed = after * scale
            dh = dh_s[rows, :]
            total = total + jnp.sum((dh * normed).reshape(rb // 8, 8, width), axis=0)
            d_after = dy_ref[rows, :].astype(F32) + rms_back(dh, normed, scale, gain)
            after_ref[rows, :] = d_after
            branch = d_after.astype(BF16)
            hid_s[rows, :] = branch
            datt_ref[rows, :] = right_t(branch, w_out[...]).astype(BF16)
            if inside and point == 0:
                core_done(nt - 1)
        if inside:
            plane_done(step - 2, len(bits) - 1)
        dgain_ref[...] = total
        if inside:
            for stage in range(len(bits) - 1):
                plane_done(nt - 1, stage)
        dwo_ref[...] = left_t(att_ref[...], hid_s[...]).astype(BF16)
        if inside:
            plane_done(nt - 1, len(bits) - 1)


def feed_forward(x, attended, dys, w_out, gain, own, rest):
    count, width = x.shape
    nd, nt, units = own.shape[0], rest.shape[1] + 1, own.shape[2]
    share = own.shape[1] // 2
    inside = share % 16 == 0 and nd >= 8
    rb = 256
    rows, part = whole((count, width)), whole((count // nt, width))
    dma = pltpu.SemaphoreType.DMA
    scratch = [
        pltpu.VMEM((count, width), BF16),
        pltpu.VMEM((count, width), BF16),
        pltpu.VMEM((width, count), BF16),
        pltpu.VMEM((width, count), BF16),
        pltpu.VMEM((count, width), F32),
        pltpu.VMEM((count, width), F32),
        pltpu.VMEM((count, units), BF16),
        pltpu.VMEM((count, units), BF16),
        pltpu.VMEM((2, nd, share, units), BF16),
        dma((nt,)),
    ]
    if inside:
        stages = nd.bit_length() - 2
        grads, grads_spec = jax.ShapeDtypeStruct((nt, 2 * share, units), BF16), whole((nt, 2 * share, units))
        scratch += [
            pltpu.VMEM((2, nd, 2 * share, units), BF16),
            pltpu.VMEM((2, nd // 2, 2 * share, units), BF16),
            pltpu.VMEM((2, stages, nd // 4, 2 * share, units), BF16),
            dma((2, nd // 2)), dma((2, nd // 2)),
            dma((2, stages, 2, nd // 4)), dma((2, stages, 2, nd // 4)),
        ]
        params = dict(collective_id=2, has_side_effects=True)
    else:
        grads = jax.ShapeDtypeStruct((nd, nt, 2, share, units), BF16)
        grads_spec = pl.BlockSpec((nd, 1, 2, share, units), lambda s: (0, jnp.minimum(s, nt - 1), 0, 0, 0))
        params = {}
    return pl.pallas_call(
        functools.partial(middle_kernel, rb, nd, nt, share, inside),
        grid=(nt + 1,),
        in_specs=[
            rows, rows, whole((width, width)), whole((1, width)), whole(own.shape),
            pl.BlockSpec((nd, 1, 2 * share, units), lambda s: (0, jnp.clip(s - 1, 0, nt - 2), 0, 0)),
        ] + [ANY] * nt,
        out_specs=[part] * nt + [rows, rows, whole((width, width)), whole((8, width)), grads_spec],
        out_shape=[jax.ShapeDtypeStruct((count // nt, width), BF16)] * nt + [
            jax.ShapeDtypeStruct((count, width), F32),
            jax.ShapeDtypeStruct((count, width), BF16),
            jax.ShapeDtypeStruct((width, width), BF16),
            jax.ShapeDtypeStruct((8, width), F32),
            grads,
        ],
        scratch_shapes=scratch,
        compiler_params=pltpu.CompilerParams(vmem_limit_bytes=62 << 20, **params),
        cost_estimate=cost(12 * count * width * nt * units, 4 * nd * nt * share * units),
        name="feed_forward",
    )(x, attended, w_out, gain, own, rest, *dys)


def masks_of(bits):
    masks = [0]
    for bit in bits:
        masks = masks + [mask | bit for mask in masks]
    return masks


def flips(index, mask):
    bit = 1
    while bit <= mask:
        if mask & bit:
            index = flip(index, bit)
        bit *= 2
    return index


def finish_kernel(
    nd, nt, share, inside, x_ref, dq_ref, dk_all, dv_all, after_ref, w_ref, gain_ref, dwo_ref, small_ref,
    *refs,
):
    tok_out, dw_out, small_out = refs[:3]
    own_s, other_s, grads_s, ht_s, tok_s, own_sems, kv_send, kv_recv, tok_send, tok_recv, tok_self = refs[3:14]
    if inside:
        slab_s, core_s, plane_s, z_s, sm_s, sm_in, g_send, g_recv, s_send, s_recv = refs[14:]
    d, t = 2 * lax.axis_index("plane") + lax.axis_index("core"), lax.axis_index("tensor")
    core = d % 2
    count, width = x_ref.shape
    per = tok_out.shape[1]
    rows_in = per * BLOCK
    holder = t % 2 == core
    bits = [1 << k for k in range(1, nd.bit_length() - 1)]
    greet(nd, nt, d, t)

    order = [lax.rem(t + s, nt) for s in list(range(1, nt)) + [0]]
    own = [pltpu.make_async_copy(a.at[:, core], own_s.at[k], own_sems.at[k]) for k, a in enumerate((dk_all, dv_all))]
    for copy in own:
        copy.start()
    exchanged = []
    for s, source in enumerate(order):
        pair = []
        for k, a in enumerate((dk_all, dv_all)):
            pair.append(
                remote(
                    a.at[pl.ds(per * source, per), 1 - core], other_s.at[k, pl.ds(per * source, per)],
                    kv_send.at[k, s], kv_recv.at[k, s], (flip(d, 1), t),
                )
            )
            pair[-1].start()
        exchanged.append(pair)
    gain = gain_ref[:1]

    def norms(rows):
        x = x_ref[rows, :].astype(F32)
        scale = rms_scale(x)
        return x * scale, scale

    def fill(bundle, at, source, first):
        lines = source.shape[0] // share
        for k in range(lines):
            slab = first // share + k
            slab_s[bundle, slab // nt, slab % nt, at : at + source.shape[1] // width * share] = jnp.concatenate(
                [
                    source[k * share : (k + 1) * share, m * width : (m + 1) * width]
                    for m in range(source.shape[1] // width)
                ]
            ).astype(BF16)

    halves = [(0, nt // 2), (nt // 2, nt)]
    routes = [[1] + bits, [1] + bits[::-1]]

    def stage_copies(bundle, stage):
        copies, adds = [], []
        for h, (lo, hi) in enumerate(halves):
            bit, part = routes[h][stage], pl.ds(lo, hi - lo)
            for k, mask in enumerate(masks_of(routes[h][stage + 1 :])):
                buffer = core_s.at[bundle] if stage == 0 else plane_s.at[bundle, stage - 1]
                copies.append(
                    remote(
                        slab_s.at[bundle, flips(flip(d, bit), mask), part], buffer.at[k, part],
                        g_send.at[bundle, h, stage, k], g_recv.at[bundle, h, stage, k], (flip(d, bit), t),
                    )
                )
                adds.append((flips(d, mask), lo, hi, buffer, k))
        return copies, adds

    def stage_start(bundle, stage):
        for copy in stage_copies(bundle, stage)[0]:
            copy.start()

    def stage_done(bundle, stage):
        copies, adds = stage_copies(bundle, stage)
        for copy in copies:
            copy.wait()
        for mine, lo, hi, buffer, k in adds:
            both = slab_s[bundle, mine, lo:hi].astype(F32) + buffer[k, lo:hi].astype(F32)
            slab_s[bundle, mine, lo:hi] = both.astype(BF16)

    def z_copies(bundle):
        copies = []
        for s in range(1, nt):
            to = lax.rem(t + s, nt)
            copies.append(
                remote(
                    slab_s.at[bundle, d, to], z_s.at[bundle, s],
                    g_send.at[bundle, 2, 0, s], g_recv.at[bundle, 2, 0, s], (d, to),
                )
            )
        return copies

    def small_copies(stage):
        if stage <= len(bits):
            return [remote(sm_s, sm_in.at[stage], s_send.at[stage], s_recv.at[stage], (flip(d, routes[0][stage]), t))]
        copies = []
        for s in range(1, nt):
            k = len(bits) + s
            copies.append(remote(sm_s, sm_in.at[k], s_send.at[k], s_recv.at[k], (d, lax.rem(t + s, nt))))
        return copies

    d_gain = jnp.zeros((8, width), F32)
    sends = []
    to_core = d - core + t % 2
    for s, source in enumerate(order):
        if s == 0:
            for copy in own:
                copy.wait()
        for copy in exchanged[s]:
            copy.wait()
        rows = pl.ds(pl.multiple_of(source * rows_in, rows_in), rows_in)
        grads_s[rows, :width] = dq_ref[rows, :]
        for k in range(2):
            total = own_s[k, pl.ds(per * source, per)].astype(F32) + other_s[k, pl.ds(per * source, per)].astype(F32)
            grads_s[rows, (k + 1) * width : (k + 2) * width] = total.reshape(rows_in, width).astype(BF16)
        dh = right_t(grads_s[rows, :], w_ref[...])
        normed, scale = norms(rows)
        d_gain = d_gain + jnp.sum((dh * normed).reshape(rows_in // 8, 8, width), axis=0)
        tok = after_ref[rows, :] + rms_back(dh, normed, scale, gain)
        tok_s[s] = tok.astype(BF16).reshape(per, BLOCK, width)
        here = (source == t) & holder
        dst = tok_out.at[t // 2, :, core]
        far = remote(tok_s.at[s], dst, tok_send.at[s], tok_recv.at[2 * (t // 2) + core], (to_core, source))
        near = pltpu.make_async_copy(tok_s.at[s], dst, tok_self)
        pl.when(jnp.logical_not(here))(far.start)
        pl.when(here)(near.start)
        sends.append((here, far, near))
        if s == 0:
            for r in range(0, count, rows_in):
                lines = slice(r, r + rows_in)
                normed, scale = norms(lines)
                ht_s[:, lines] = (normed * gain).astype(BF16).T
            if inside:
                for r in range(0, width, 8 * share):
                    lines = slice(r, r + 8 * share)
                    dwo = dwo_ref[lines, :].astype(F32)
                    fill(0, 0, jnp.concatenate([matmul(ht_s[lines, :], dq_ref[...]), dwo], axis=1), r)
                stage_start(0, 0)
        if s == 1 and inside:
            stage_done(0, 0)
            stage_start(0, 1)

    small = small_ref[...]
    line = lax.broadcasted_iota(jnp.int32, small.shape, 0)
    small = small + jnp.where(line == 0, jnp.sum(d_gain, axis=0, keepdims=True), 0.0)
    if inside:
        sm_s[...] = small
        tiny = small_copies(0)
        for copy in tiny:
            copy.start()
        for stage in range(1, len(bits)):
            stage_done(0, stage)
            stage_start(0, stage + 1)
        for r in range(0, width, 8 * share):
            fill(1, 0, matmul(ht_s[r : r + 8 * share, :], grads_s[:, width:]), r)
        stage_start(1, 0)
        stage_done(0, len(bits))
        first_z = z_copies(0)
        for copy in first_z:
            copy.start()
        for stage in range(len(bits) + 1):
            for copy in tiny:
                copy.wait()
            sm_s[...] += sm_in[stage]
            stage_done(1, stage)
            if stage < len(bits):
                stage_start(1, stage + 1)
            tiny = small_copies(stage + 1)
            for copy in tiny:
                copy.start()
        second_z = z_copies(1)
        for copy in second_z:
            copy.start()
        for copy in first_z + second_z + tiny:
            copy.wait()
        for bundle in range(2):
            total = slab_s[bundle, d, t].astype(F32)
            for s in range(1, nt):
                total = total + z_s[bundle, s].astype(F32)
            dw_out[bundle * 2 * share : (bundle + 1) * 2 * share] = total
        small_out[...] = sm_s[...] + sum(sm_in[len(bits) + s] for s in range(1, nt))
    else:
        small_out[...] = small
        for r in range(0, width, 256):
            lines = slice(r, r + 256)
            dw_out[lines, : 3 * width] = matmul(ht_s[lines, :], grads_s[...]).astype(BF16)
            dw_out[lines, 3 * width :] = dwo_ref[lines, :]

    for here, far, near in sends:
        pl.when(jnp.logical_not(here))(far.wait_send)
        pl.when(here)(near.wait)
    for m in range(tok_out.shape[0]):
        for c in range(2):
            here = (2 * m + core == t) & (c == core)
            dst = tok_out.at[m, :, c]
            back = remote(dst, dst, tok_send.at[0], tok_recv.at[2 * m + c], (flip(d, 1), t))
            pl.when(jnp.logical_not(here))(back.wait_recv)


def finish(x, dq, dk_all, dv_all, after, w_qkv, gains, dwo, small, share, micro):
    count, width = x.shape
    nd, nt = 2 * lax.axis_size("plane"), lax.axis_size("tensor")
    inside = 2 * share % 16 == 0 and nd >= 8
    blocks = count // BLOCK
    per = blocks // nt
    dma = pltpu.SemaphoreType.DMA
    vmem = pl.BlockSpec(memory_space=pltpu.VMEM)
    shaped = jax.ShapeDtypeStruct
    scratch = [
        pltpu.VMEM((2, blocks, BLOCK, width), BF16),
        pltpu.VMEM((2, blocks, BLOCK, width), BF16),
        pltpu.VMEM((count, 3 * width), BF16),
        pltpu.VMEM((width, count), BF16),
        pltpu.VMEM((nt, per, BLOCK, width), BF16),
        dma((2,)), dma((2, nt)), dma((2, nt)), dma((nt,)), dma((nt,)), dma,
    ]
    if inside:
        most = max(nd // 2, nt)
        stages = nd.bit_length() - 1
        scratch += [
            pltpu.VMEM((2, nd, nt, 2 * share, width), BF16),
            pltpu.VMEM((2, nd // 2, nt, 2 * share, width), BF16),
            pltpu.VMEM((2, stages - 1, nd // 4, nt, 2 * share, width), BF16),
            pltpu.VMEM((2, nt, 2 * share, width), BF16),
            pltpu.VMEM(small.shape, F32),
            pltpu.VMEM((stages + nt,) + small.shape, F32),
            dma((2, 3, stages, most)), dma((2, 3, stages, most)), dma((stages + nt,)), dma((stages + nt,)),
        ]
    return pl.pallas_call(
        functools.partial(finish_kernel, nd, nt, share, inside),
        in_specs=[vmem, vmem, ANY, ANY, vmem, vmem, vmem, vmem, vmem],
        out_specs=[vmem, vmem, vmem],
        out_shape=[
            shaped((micro, per, 2, BLOCK, width), BF16),
            shaped((4 * share, width), F32) if inside else shaped((width, 4 * width), BF16),
            shaped(small.shape, F32),
        ],
        scratch_shapes=scratch,
        compiler_params=pltpu.CompilerParams(
            collective_id=1, has_side_effects=True, vmem_limit_bytes=60 << 20
        ),
        cost_estimate=cost(24 * count * width * width, 16 * count * width),
        name="finish",
    )(x, dq, dk_all, dv_all, after, w_qkv, gains, dwo, small)


def per_device(
    tokens, segments, w_query, w_key, w_value, w_out, norm_attn, norm_ffn, pre_mix, post_mix, w_up, w_down, out_grad,
):
    micro, _, rows, width = tokens.shape
    nd, nt = 2 * lax.axis_size("plane"), lax.axis_size("tensor")
    heads = pre_mix.shape[0]
    head_width = width // heads
    length = rows * nt
    count = length // 2
    blocks = count // BLOCK
    share = w_query.shape[0]
    bits = [1 << k for k in range(nd.bit_length() - 1)]
    d, t = 2 * lax.axis_index("plane") + lax.axis_index("core"), lax.axis_index("tensor")
    core = d % 2

    place = (d * nt + t) * share
    gains = lax.dynamic_update_slice(jnp.zeros((8, width), BF16), jnp.stack([norm_attn, norm_ffn]), (0, place))
    fill = jnp.zeros((-(4 * share + 8) % 16, width), BF16)
    bundle = jnp.concatenate([w_query, w_key, w_value, w_out, gains, fill])
    later = jnp.concatenate([w_up, w_down])
    own_rows = lax.all_gather(later, ("plane", "core"), axis=0, tiled=False)
    x, query, k_all, v_all, segs, w_qkv, all_out, gains, later = start(tokens, segments, bundle, later, share)
    k_all, v_all = (a.reshape(2 * blocks, BLOCK, width) for a in (k_all, v_all))
    x, out_grad = lax.optimization_barrier((x, out_grad))
    grad_turns = to_sequences(out_grad)
    rest_rows = lax.all_gather(later, ("plane", "core"), axis=0, tiled=False)

    def by_lane(mix):
        return jnp.repeat(mix.astype(F32), head_width, axis=1)

    pre = (by_lane(pre_mix.T) * head_width ** (-0.5)).astype(BF16)
    post = by_lane(post_mix)

    attended, u, lse = attend(query, k_all, v_all, segs, pre, post)
    *out_turns, grad_after, grad_attended, grad_w_out, grad_gain_ffn, part_both = feed_forward(
        x, attended, grad_turns, all_out, gains[1:2], own_rows, rest_rows
    )
    grad_gain_ffn = jnp.sum(grad_gain_ffn, axis=0)
    out = from_sequences(out_turns, micro)
    if part_both.ndim > 3:
        part_both = lax.dynamic_slice_in_dim(jnp.concatenate([part_both[:, ::-1]] * 2, axis=1), nt - 1 - t, nt, 1)
        part_both = lax.psum_scatter(part_both, ("plane", "core"), scatter_dimension=0, tiled=False)
    part_both = lax.psum_scatter(part_both, "tensor", scatter_dimension=0, tiled=False).astype(F32)
    part_both = part_both.reshape((2,) + w_up.shape)

    grad_query, grad_key, grad_value, d_pre, d_post = attend_back(
        query, grad_attended, u, lse, k_all, v_all, segs, pre, post
    )

    def spread(d_mix):
        total = d_mix.reshape(heads, 8, heads, head_width).sum((1, 3)).reshape(-1)
        return jnp.pad(total, (0, width - total.shape[0]))

    small = jnp.zeros((8, width), F32).at[1].set(grad_gain_ffn)
    small = small.at[2].set(spread(d_pre)).at[3].set(spread(d_post))
    x, out = lax.optimization_barrier((x, out))
    d_tokens, owned, small = finish(
        x, grad_query, grad_key.reshape(blocks, 2, BLOCK, width), grad_value.reshape(blocks, 2, BLOCK, width),
        grad_after, w_qkv, gains, grad_w_out, small, share, micro,
    )
    d_tokens = d_tokens.reshape(tokens.shape).astype(F32)
    if owned.dtype == BF16:
        owned = lax.psum_scatter(owned, AXES, scatter_dimension=0, tiled=True).astype(F32)
        owned = [owned[:, k * width : (k + 1) * width] for k in range(4)]
        small = lax.psum(small, AXES)
    else:
        owned = [owned[k * share : (k + 1) * share] for k in (0, 2, 3, 1)]
    gain_grads = lax.dynamic_slice_in_dim(small, place, share, 1)
    pairs = heads * heads
    return (
        out,
        d_tokens,
        owned[0],
        owned[1],
        owned[2],
        owned[3],
        gain_grads[0],
        gain_grads[1],
        small[2, :pairs].reshape(heads, heads).T * head_width ** (-0.5),
        small[3, :pairs].reshape(heads, heads),
        part_both[0],
        part_both[1],
    )


def solution(mesh):
    devices = mesh.devices
    devices = devices.reshape(devices.shape[0] // 2, 2, devices.shape[1])
    dp = ("plane", "core")
    both = P(AXES, None)
    gain = P(AXES)
    data = P(None, dp, "tensor", None)
    ffn = P(dp, "tensor")
    return jax.shard_map(
        per_device,
        mesh=jax.sharding.Mesh(devices, AXES),
        in_specs=(data, P(None, dp, None), both, both, both, both, gain, gain, P(), P(), ffn, ffn, data),
        out_specs=(data, data, both, both, both, both, gain, gain, P(), P(), ffn, ffn),
        check_vma=False,
    )
```

time: 438 us -> 402 us (0.918)
  Pallas kernels: 354 us -> 338 us
  waiting for transfers between devices: 10 us -> 4.49 us
  local copies, waits for them, and re-layouts: 21.7 us -> 16.2 us
    pallas_call x1, Pallas kernels: 87.9 us -> 65.5 us  [attend_back(): pl.pallas_call(functools.partial(backward_kernel, heads, groups), grid=(b...]
    pallas_call x2, Pallas kernels: 96.2 us -> 108 us  [the longest x1 74.5 us: feed_forward(): pl.pallas_call(functools.partial(middle_kernel, rb, nd, nt, share, inside...]
    slice x3 -> x2, local copies, waits for them, and re-layouts: 11.4 us -> 1.56 us  [the longest x1 0.85 us: per_device(): part_both[1]]
    pallas_call x1, Pallas kernels: 85.4 us -> 79.1 us  [finish(): pl.pallas_call(functools.partial(finish_kernel, nd, nt, share, inside), i...]
    all_gather x1 -> x2, waiting for transfers between devices: 9.98 us -> 4.41 us  [the longest x1 4.39 us: per_device(): rest_rows = lax.all_gather(later, ('plane', 'core'), axis=0, tiled=False)]
  transfers between devices with their start and end apart: 10 -> 11, of which waited for: 1 -> 1; matrix products, arithmetic and copies ran while one was open for 6% -> 4% of each run, Pallas kernels for 52% -> 67%
where the time goes in v3:
time: 402 us; the launch traced here: 396 us
  Pallas kernels  338 us (84%)
  local copies, waits for them, and re-layouts  16.2 us (4%)
  starting transfers between devices  14.7 us (4%)
  between operations  14.4 us (4%)
  other arithmetic  8.12 us (2%)
  waiting for transfers between devices  4.49 us (1%)
    pallas_call x1, Pallas kernels, start(): pl.pallas_call(functools.partial(start_kernel, nd, nt, share, halves), in...  80.5 us
    pallas_call x1, Pallas kernels, finish(): pl.pallas_call(functools.partial(finish_kernel, nd, nt, share, inside), i...  79.1 us
    pallas_call x1, Pallas kernels, feed_forward(): pl.pallas_call(functools.partial(middle_kernel, rb, nd, nt, share, inside...  74.5 us
    pallas_call x1, Pallas kernels, attend_back(): pl.pallas_call(functools.partial(backward_kernel, heads, groups), grid=(b...  65.5 us
    pallas_call x1, Pallas kernels, attend(): pl.pallas_call(functools.partial(forward_kernel, heads, groups, most), gr...  33.6 us
    ppermute x8, starting transfers between devices, send(): return lax.ppermute(x, AXES, pairs)  14.6 us
  transfers between devices with their start and end apart: 11, of which 1 were waited for; matrix products, arithmetic and copies ran while one was open for 4% of the time, Pallas kernels for 67%

profile of v3, /device:TPU:0, one launch (start us, length us, event | category | flops | bytes accessed | tf_op | source)
XLA Modules:
  0.0 396.3 jit_solution(14944801283351236005)
XLA Ops:
  7.2 0.9 constant_dynamic-update-slice_fusion.7
  8.1 0.9 constant_dynamic-update-slice_fusion.6.refs_3_
  10.9 0.8 constant_dynamic-update-slice_fusion.5
  11.6 0.8 constant_dynamic-update-slice_fusion.4
  12.4 0.8 constant_dynamic-update-slice_fusion.3
  13.2 0.8 constant_dynamic-update-slice_fusion.2
  14.6 80.5 %start.1 = (bf16[1024,768]{1,0:T(8,128)(2,1)}, bf16[1024,768]{1,0:T(8,128)(2,1)}, bf16[8,2,128,768]{3,2,1,0:T(8,128)(2,1)}, bf16[8,2,128,768]{3,2,1,0:T(8,128)(2...) custom-call(bf16[2,2,2,128,768]{4,3,2,1,0:T(8,128)(2,1)} %bitcast.32, ...), custom_call_target="tpu_custom_call" | custom-call | tf_op jit(solution)/shard_map/start/pallas_call | solution.py:685
  95.2 2.6 split.1
  97.8 1.6 collective-permute-start
  99.5 6.4 %collective-permute-start.1 = (bf16[256,768]{1,0:T(8,128)(2,1)}, bf16[256,768]{1,0:T(8,128)(2,1)S(1)}, u32[]{:S(2)}, u32[]{:S(2)}) collective-permute-start(bf16[256,768]{1,0:T(8,128)(2,1)} %get-tuple-element.97), channel_id=1, source_target_pairs={{0,4},{1,2},{2,6},{3,0},{4,5},{5,3},{6,7},{7,1},{8,12},{9,10},{10,... | collective-permute-start | bytes 1179656 | tf_op jit(solution)/shard_map/ppermute | solution.py:56
  105.9 2.6 collective-permute-start.2
  108.7 0.7 convert_element_type.38.pre_ref
  109.5 0.7 reshape.170.post_ref
  110.2 33.6 %attend.1 = (bf16[1024,768]{1,0:T(8,128)(2,1)}, bf16[8,12,128,768]{3,2,1,0:T(8,128)(2,1)}, f32[8,1536,128]{2,1,0:T(8,128)}) custom-call(bf16[1024,768]{1,0:T(8,128)(2,1)} %get-tuple-element.87.q_ref, bf16[16,128,768]{2,1,0:T(8,128)(2,1)} %bitcast.37, bf16[16,128,768]{2,1,0:T(8,128)(2,1)} %bitcast.39, s32[16,128]{1,0:T(8,128)} %get-tuple-element.90.seg_low, ...), custom_call_target="tpu_custom_call" | custom-call | flops 38654705664 | bytes 37748736 | tf_op jit(solution)/shard_map/attend/pallas_call | solution.py:308
  143.8 1.3 slice.85.refs_3_
  145.2 4.4 %all-gather.7.cloned.1.call-done = bf16[24,192,768]{2,1,0:T(8,128)(2,1)} async-done(((bf16[3,192,768]{2,1,0:T(8,128)(2,1)}), bf16[24,192,768]{2,1,0:T(8,128)(2,1)}) %all-gather.7.cloned.1.call-update) | async-done | bytes 7077904 | tf_op jit(solution)/shard_map/all_gather | solution.py:1237
  149.6 74.5 %feed_forward.1 = (bf16[256,768]{1,0:T(8,128)(2,1)}, bf16[256,768]{1,0:T(8,128)(2,1)}, bf16[256,768]{1,0:T(8,128)(2,1)}, bf16[256,768]{1,0:T(8,128)(2,1)}, f32[1...) custom-call(bf16[1024,768]{1,0:T(8,128)(2,1)} %get-tuple-element.105, ...), custom_call_target="tpu_custom_call" | custom-call | flops 28991029248 | bytes 9437184 | tf_op jit(solution)/shard_map/feed_forward/pallas_call | solution.py:927
  224.1 1.7 collective-permute-start.4
  225.8 1.5 collective-permute-start.5
  227.4 0.8 collective-permute-start.7
  228.1 65.5 %attend_back.1 = (bf16[1024,768]{1,0:T(8,128)(2,1)}, bf16[16,128,768]{2,1,0:T(8,128)(2,1)}, bf16[16,128,768]{2,1,0:T(8,128)(2,1)}, f32[12,8,768]{2,1,0:T(8,128)}, f32[12,8,768]{2,1,0:T(8,128)}) custom-call(bf16[1024,768]{1,0:T(8,128)(2,1)} %get-tuple-element.87.q_ref, bf16[1024,768]{1,0:T(8,128)(2,1)} %get-tuple-element.106.g_ref, ...), custom_call_target="tpu_custom_call" | custom-call | flops 96636764160 | bytes 37748736 | tf_op jit(solution)/shard_map/attend_back/pallas_call | solution.py:451
  293.7 1.0 reduce_sum.32
  295.0 1.0 reduce_sum.45
  297.6 0.7 copy-done.4
  298.3 2.6 join.1
  301.0 79.1 %finish.1 = (bf16[2,2,2,128,768]{4,3,2,1,0:T(8,128)(2,1)}, f32[96,768]{1,0:T(8,128)}, f32[8,768]{1,0:T(8,128)}) custom-call(bf16[1024,768]{1,0:T(8,128)(2,1)} %get-tuple-element.105.refs_0_.x_ref, bf16[1024,768]{1,0:T(8,128)(2,1)} %get-tuple-element.109.dq_ref, bf16[8,2,128,768]{3,2,1,0:T(8,128)(2,1)} %bitcast.46, bf16[8,2,128,768]{3,2,1,0:T(8,128)(2,1)} %bitcast.47, ...), custom_call_target="tpu_custom_call" | custom-call | flops 14495514624 | bytes 12582912 | tf_op jit(solution)/shard_map/finish/pallas_call | solution.py:1194
  380.1 0.8 slice_reduce_fusion
  382.3 3.4 convert.2
  385.7 0.8 constant_dynamic-slice_fusion
  387.0 0.7 fusion.1
  387.7 1.0 convert_element_type.42
  388.7 0.8 slice_bitcast_fusion
  (75 shorter events, 6.7 us)
Async XLA Ops:
  7.2 138.0 %all-gather.5.cloned.1.call-start = ((), (), s32[]{:S(2)}) async-start(), calls=%async_computation.2 | async-start | bytes 2654208 | tf_op jit(solution)/shard_map/all_gather | solution.py:1232
  9.1 0.7 copy-start
  9.8 139.7 %all-gather.7.cloned.1.call-start = ((), (), s32[]{:S(2)}) async-start(), calls=%async_computation.3 | async-start | bytes 7962624 | tf_op jit(solution)/shard_map/all_gather | solution.py:1237
  14.0 0.7 copy-start.6
  95.1 13.3 %copy-start.10 = (bf16[12,12]{1,0:T(8,128)(2,1)S(1)}, bf16[12,12]{1,0:T(8,128)(2,1)}, u32[]{:S(2)}) copy-start(bf16[12,12]{1,0:T(8,128)(2,1)} %param.27) | copy-start | bytes 868
  95.1 14.3 %copy-start.9 = (bf16[12,12]{1,0:T(8,128)(2,1)S(1)}, bf16[12,12]{1,0:T(8,128)(2,1)}, u32[]{:S(2)}) copy-start(bf16[12,12]{1,0:T(8,128)(2,1)} %param.28) | copy-start | bytes 868
  95.1 292.5 %reduce-scatter.2.cloned.1.call-start = ((), (), s32[]{:S(2)}) async-start(), calls=%async_computation.1 | async-start | bytes 1474560 | tf_op jit(solution)/shard_map/reduce_scatter | solution.py:1254
  97.8 47.2 %collective-permute-start = (bf16[256,768]{1,0:T(8,128)(2,1)}, bf16[256,768]{1,0:T(8,128)(2,1)S(1)}, u32[]{:S(2)}, u32[]{:S(2)}) collective-permute-start(bf16[256,768]{1,0:T(8,128)(2,1)} %get-tuple-element.96), channel_id=1, source_target_pairs={{0,0},{1,4},{2,2},{3,6},{4,1},{5,5},{6,3},{7,7},{8,8},{9,12},{10,1... | collective-permute-start | bytes 1179656 | tf_op jit(solution)/shard_map/ppermute | solution.py:56
  99.5 45.6 %collective-permute-start.1 = (bf16[256,768]{1,0:T(8,128)(2,1)}, bf16[256,768]{1,0:T(8,128)(2,1)S(1)}, u32[]{:S(2)}, u32[]{:S(2)}) collective-permute-start(bf16[256,768]{1,0:T(8,128)(2,1)} %get-tuple-element.97), channel_id=1, source_target_pairs={{0,4},{1,2},{2,6},{3,0},{4,5},{5,3},{6,7},{7,1},{8,12},{9,10},{10,... | collective-permute-start | bytes 1179656 | tf_op jit(solution)/shard_map/ppermute | solution.py:56
  105.9 39.2 %collective-permute-start.2 = (bf16[256,768]{1,0:T(8,128)(2,1)}, bf16[256,768]{1,0:T(8,128)(2,1)S(1)}, u32[]{:S(2)}, u32[]{:S(2)}) collective-permute-start(bf16[256,768]{1,0:T(8,128)(2,1)} %get-tuple-element.98), channel_id=1, source_target_pairs={{0,2},{1,6},{2,0},{3,4},{4,3},{5,7},{6,1},{7,5},{8,10},{9,14},{10,... | collective-permute-start | bytes 1179656 | tf_op jit(solution)/shard_map/ppermute | solution.py:56
  108.4 36.7 %collective-permute-start.3 = (bf16[256,768]{1,0:T(8,128)(2,1)}, bf16[256,768]{1,0:T(8,128)(2,1)S(1)}, u32[]{:S(2)}, u32[]{:S(2)}) collective-permute-start(bf16[256,768]{1,0:T(8,128)(2,1)} %get-tuple-element.99), channel_id=1, source_target_pairs={{0,6},{1,0},{2,4},{3,2},{4,7},{5,1},{6,5},{7,3},{8,14},{9,8},{10,1... | collective-permute-start | bytes 1179656 | tf_op jit(solution)/shard_map/ppermute | solution.py:56
  145.1 4.5 %copy-start.11 = (bf16[256,768]{1,0:T(8,128)(2,1)}, bf16[256,768]{1,0:T(8,128)(2,1)S(1)}, u32[]{:S(2)}) copy-start(bf16[256,768]{1,0:T(8,128)(2,1)S(1)} %collective-permute-done.refs_6_) | copy-start | bytes 1179652
  145.1 4.5 %copy-start.12 = (bf16[256,768]{1,0:T(8,128)(2,1)}, bf16[256,768]{1,0:T(8,128)(2,1)S(1)}, u32[]{:S(2)}) copy-start(bf16[256,768]{1,0:T(8,128)(2,1)S(1)} %collective-permute-done.1.refs_7_) | copy-start | bytes 1179652
  145.1 4.5 %copy-start.13 = (bf16[256,768]{1,0:T(8,128)(2,1)}, bf16[256,768]{1,0:T(8,128)(2,1)S(1)}, u32[]{:S(2)}) copy-start(bf16[256,768]{1,0:T(8,128)(2,1)S(1)} %collective-permute-done.2.refs_8_) | copy-start | bytes 1179652
  145.1 4.4 %copy-start.14 = (bf16[256,768]{1,0:T(8,128)(2,1)}, bf16[256,768]{1,0:T(8,128)(2,1)S(1)}, u32[]{:S(2)}) copy-start(bf16[256,768]{1,0:T(8,128)(2,1)S(1)} %collective-permute-done.3.refs_9_) | copy-start | bytes 1179652
  224.1 72.4 %collective-permute-start.4 = (bf16[256,768]{1,0:T(8,128)(2,1)}, bf16[256,768]{1,0:T(8,128)(2,1)S(1)}, u32[]{:S(2)}, u32[]{:S(2)}) collective-permute-start(bf16[256,768]{1,0:T(8,128)(2,1)} %get-tuple-element.100), channel_id=1, source_target_pairs={{0,0},{1,4},{2,2},{3,6},{4,1},{5,5},{6,3},{7,7},{8,8},{9,12},{10,1... | collective-permute-start | bytes 1179656 | tf_op jit(solution)/shard_map/ppermute | solution.py:56
  225.8 70.8 %collective-permute-start.5 = (bf16[256,768]{1,0:T(8,128)(2,1)}, bf16[256,768]{1,0:T(8,128)(2,1)S(1)}, u32[]{:S(2)}, u32[]{:S(2)}) collective-permute-start(bf16[256,768]{1,0:T(8,128)(2,1)} %get-tuple-element.101), channel_id=1, source_target_pairs={{0,3},{1,7},{2,1},{3,5},{4,0},{5,4},{6,2},{7,6},{8,11},{9,15},{10,... | collective-permute-start | bytes 1179656 | tf_op jit(solution)/shard_map/ppermute | solution.py:56
  227.2 69.4 %collective-permute-start.6 = (bf16[256,768]{1,0:T(8,128)(2,1)}, bf16[256,768]{1,0:T(8,128)(2,1)S(1)}, u32[]{:S(2)}, u32[]{:S(2)}) collective-permute-start(bf16[256,768]{1,0:T(8,128)(2,1)} %get-tuple-element.102), channel_id=1, source_target_pairs={{0,2},{1,6},{2,0},{3,4},{4,3},{5,7},{6,1},{7,5},{8,10},{9,14},{10,... | collective-permute-start | bytes 1179656 | tf_op jit(solution)/shard_map/ppermute | solution.py:56
  227.4 69.3 %collective-permute-start.7 = (bf16[256,768]{1,0:T(8,128)(2,1)}, bf16[256,768]{1,0:T(8,128)(2,1)S(1)}, u32[]{:S(2)}, u32[]{:S(2)}) collective-permute-start(bf16[256,768]{1,0:T(8,128)(2,1)} %get-tuple-element.103), channel_id=1, source_target_pairs={{0,1},{1,5},{2,3},{3,7},{4,2},{5,6},{6,0},{7,4},{8,9},{9,13},{10,1... | collective-permute-start | bytes 1179656 | tf_op jit(solution)/shard_map/ppermute | solution.py:56
  228.1 65.5 %copy-start.7 = (f32[8,768]{1,0:T(8,128)S(1)}, f32[8,768]{1,0:T(8,128)}, u32[]{:S(2)}) copy-start(f32[8,768]{1,0:T(8,128)} %get-tuple-element.115) | copy-start | bytes 73732
  296.5 4.4 %copy-start.8 = (f32[8,768]{1,0:T(8,128)}, f32[8,768]{1,0:T(8,128)S(1)}, u32[]{:S(2)}) copy-start(f32[8,768]{1,0:T(8,128)S(1)} %scatter.14.small_ref) | copy-start | bytes 73732
  296.6 0.7 copy-start.1
  296.6 0.9 copy-start.2
  296.6 1.0 copy-start.3
  297.6 0.7 copy-start.4
  382.3 4.6 %copy-start.5 = (f32[96,768]{1,0:T(8,128)S(1)}, f32[96,768]{1,0:T(8,128)}, u32[]{:S(2)}) copy-start(f32[96,768]{1,0:T(8,128)} %get-tuple-element.119) | copy-start | bytes 884740
Sparse Core Ops, SparseCore 0:
  10.5 37.3 all-gather.4
  95.3 54.2 all-gather.6
  224.2 49.9 reduce-scatter.1

commit v4 on v3

--- a/solution.py
+++ b/solution.py
@@ -12,7 +12,7 @@
 BLOCK = 128
 TILE = 2 * BLOCK
 FORWARD_GROUPS = 6
-BACKWARD_GROUPS = 2
+BACKWARD_GROUPS = (2, 2, 2)
 AXES = ("plane", "core", "tensor")
 
 
@@ -95,66 +95,6 @@
     for shift in range(1, nt):
         total = total + send(pick(x, lax.rem(t + shift, nt), 0), by_shift(shift)).astype(F32)
     return total
-
-
-def seat(turn):
-    nt = lax.axis_size("tensor")
-    t, core = lax.axis_index("tensor"), lax.axis_index("core")
-    block = lax.rem(turn + t, nt)
-    source = lax.rem(2 * (t // 2) + core + nt - turn, nt)
-    return block, source
-
-
-def turn_to(turn):
-    nt = lax.axis_size("tensor")
-
-    def to(d, t):
-        block = (turn + t) % nt
-        return d - d % 2 + block % 2, 2 * (block // 2) + d % 2
-
-    return to
-
-
-def turn_back(turn):
-    nt = lax.axis_size("tensor")
-
-    def to(d, t):
-        return d - d % 2 + t % 2, (2 * (t // 2) + d % 2 + nt - turn) % nt
-
-    return to
-
-
-def split_kernel(x_ref, *outs):
-    for turn, out in enumerate(outs):
-        block = seat(turn)[0]
-        out[...] = x_ref[block // 2, :, block % 2].reshape(out.shape)
-
-
-def join_kernel(*refs):
-    out = refs[-1]
-    for turn, piece in enumerate(refs[:-1]):
-        block = seat(turn)[0]
-        out[block // 2, :, block % 2] = piece[...].reshape(out.shape[1], BLOCK, out.shape[4])
-
-
-def to_sequences(x):
-    micro, _, rows, width = x.shape
-    nt = lax.axis_size("tensor")
-    pieces = pl.pallas_call(
-        split_kernel, out_shape=[jax.ShapeDtypeStruct((rows // 2, width), x.dtype)] * nt, name="split"
-    )(x.reshape(micro, rows // TILE, 2, BLOCK, width))
-    return [send(piece, turn_to(turn)) for turn, piece in enumerate(pieces)]
-
-
-def from_sequences(pieces, micro):
-    half, width = pieces[0].shape
-    back = [send(piece, turn_back(turn)) for turn, piece in enumerate(pieces)]
-    out = pl.pallas_call(
-        join_kernel,
-        out_shape=jax.ShapeDtypeStruct((micro, half // BLOCK, 2, BLOCK, width), pieces[0].dtype),
-        name="join",
-    )(*back)
-    return out.reshape(micro, 1, 2 * half, width)
 
 
 def arrive(step, sources, scratches, sems, seg_ref, seg_s):
@@ -330,7 +270,7 @@
             jax.ShapeDtypeStruct((blocks, heads, BLOCK, width), BF16),
             jax.ShapeDtypeStruct((blocks, stack, BLOCK), F32),
         ],
-        compiler_params=pltpu.CompilerParams(vmem_limit_bytes=60 << 20),
+        compiler_params=pltpu.CompilerParams(vmem_limit_bytes=62 << 20),
         cost_estimate=cost(4 * rows * 1024 * stack // BLOCK * width, 4 * rows * stack // BLOCK * width),
         name="attend",
     )(query, k_all, v_all, segs, segs[:, None, :], pre, post)
@@ -338,14 +278,12 @@
 
 def backward_kernel(
     heads, groups, q_ref, g_ref, u_ref, lse_ref, k_all, v_all, seg_low, seg_ref, pre_ref, post_ref,
-    dq_ref, dk_ref, dv_ref, dpre_ref, dpost_ref,
-    k_s, v_s, seg_s, dk_s, dv_s, qp_s, gp_s, d_s, t_s, sems,
+    dq_ref, dk_ref, dv_ref, small_ref,
+    dpre_ref, dpost_ref, k_s, v_s, seg_s, dk_s, dv_s, qp_s, gp_s, d_s, t_s, sems,
 ):
     step = pl.program_id(0)
     core = lax.axis_index("core")
     block = 2 * step + core
-    per = heads // groups
-    size = per * BLOCK
     width = q_ref.shape[1]
     arrive(step, [k_all, v_all], [k_s, v_s], sems, seg_ref, seg_s)
 
@@ -359,7 +297,7 @@
     tiles = reach(block, seg_low)
     row_seg = rows_of(block, seg_s)
 
-    def opening(g):
+    def opening(g, per):
         query, grad_low = q_ref[...], g_ref[...]
         grad = grad_low.astype(F32)
         left, right, terms = [], [], []
@@ -377,6 +315,8 @@
         return dq + part * pre_ref[h : h + 1, :].astype(F32)
 
     def tile_part(first, mask, g, left, right, term):
+        size = left.shape[0]
+        per = size // BLOCK
         keys = k_s[pl.ds(first, 2)].reshape(TILE, -1)
         values = v_s[pl.ds(first, 2)].reshape(TILE, -1)
         s = (right_t(left, keys).reshape(per, BLOCK, TILE) + mask[None]).reshape(size, TILE)
@@ -395,8 +335,9 @@
         mask = row_mask(row_seg, block, block, seg_s)
         dk = dv = jnp.zeros((TILE, width), F32)
         dq = jnp.zeros((BLOCK, width), F32)
-        for g in range(groups):
-            part, a, b = tile_part(block, mask, g, *opening(g))
+        per = heads // groups[0]
+        for g in range(groups[0]):
+            part, a, b = tile_part(block, mask, g, *opening(g, per))
             dk, dv = dk + a, dv + b
             for k in range(per):
                 dq = closing(g * per + k, part[k * BLOCK : (k + 1) * BLOCK], dq)
@@ -407,9 +348,11 @@
     def _():
         mask = row_mask(row_seg, block, block, seg_s)
         dk = dv = jnp.zeros((TILE, width), F32)
-        for g in range(groups):
+        per = heads // groups[1]
+        size = per * BLOCK
+        for g in range(groups[1]):
             rows = slice(g * size, (g + 1) * size)
-            left, right, term = opening(g)
+            left, right, term = opening(g, per)
             qp_s[rows, :], gp_s[rows, :] = left, right
             d_s[rows, :] = jnp.broadcast_to(term, (size, BLOCK))
             t_s[rows, :], a, b = tile_part(block, mask, g, left, right, term)
@@ -420,7 +363,8 @@
             first = block - 2 * tile
             mask = row_mask(row_seg, first, block, seg_s)
             dk = dv = jnp.zeros((TILE, width), F32)
-            for g in range(groups):
+            size = heads // groups[2] * BLOCK
+            for g in range(groups[2]):
                 rows = slice(g * size, (g + 1) * size)
                 term = jnp.concatenate([d_s[rows, :]] * 2, axis=1)
                 part, a, b = tile_part(first, mask, g, qp_s[rows, :], gp_s[rows, :], term)
@@ -440,6 +384,18 @@
         for k in range(dk_ref.shape[0]):
             dk_ref[k] = dk_s[k + 1].astype(BF16)
             dv_ref[k] = dv_s[k + 1].astype(BF16)
+        sums = [jnp.sum(ref[h], axis=0, keepdims=True) for ref in (dpre_ref, dpost_ref) for h in range(heads)]
+        row = lax.broadcasted_iota(jnp.int32, (width, BLOCK), 0)
+        col = lax.broadcasted_iota(jnp.int32, (width, BLOCK), 1)
+        member = (row // (width // heads) == col).astype(F32)
+        mixes = jnp.dot(
+            jnp.concatenate(sums), member, preferred_element_type=F32, precision=lax.Precision.HIGHEST
+        )
+        lines = 2 * heads * BLOCK // width
+        small_ref[...] = jnp.zeros(small_ref.shape, F32)
+        small_ref[:lines, :] = jnp.concatenate(
+            [mixes[k * lines : (k + 1) * lines] for k in range(width // BLOCK)], axis=1
+        )
 
 
 def attend_back(query, grad, u, lse, k_all, v_all, segs, pre, post):
@@ -447,6 +403,8 @@
     rows, stack = query.shape[0], heads * BLOCK
     blocks = rows // BLOCK
     groups = BACKWARD_GROUPS
+    lines = 2 * heads * BLOCK // width + 2
+    lines += -lines % 8
     by_block = pl.BlockSpec((BLOCK, width), lambda i: (i, 0))
     return pl.pallas_call(
         functools.partial(backward_kernel, heads, groups),
@@ -462,10 +420,11 @@
             by_block,
             whole((2 * blocks, BLOCK, width)),
             whole((2 * blocks, BLOCK, width)),
-            whole((heads, 8, width)),
-            whole((heads, 8, width)),
+            whole((lines, width)),
         ],
         scratch_shapes=[
+            pltpu.VMEM((heads, 8, width), F32),
+            pltpu.VMEM((heads, 8, width), F32),
             pltpu.VMEM((2 * blocks + 1, BLOCK, width), BF16),
             pltpu.VMEM((2 * blocks + 1, BLOCK, width), BF16),
             pltpu.VMEM((2 * blocks + 1, 1, BLOCK), jnp.int32),
@@ -481,8 +440,7 @@
             jax.ShapeDtypeStruct((rows, width), BF16),
             jax.ShapeDtypeStruct((2 * blocks, BLOCK, width), BF16),
             jax.ShapeDtypeStruct((2 * blocks, BLOCK, width), BF16),
-            jax.ShapeDtypeStruct((heads, 8, width), F32),
-            jax.ShapeDtypeStruct((heads, 8, width), F32),
+            jax.ShapeDtypeStruct((lines, width), F32),
         ],
         compiler_params=pltpu.CompilerParams(vmem_limit_bytes=62 << 20),
         cost_estimate=cost(10 * rows * 1024 * stack // BLOCK * width, 4 * rows * stack // BLOCK * width),
@@ -525,14 +483,15 @@
 def start_kernel(
     nd, nt, share, halves, *refs,
 ):
+    tokens, grads, segments, later = refs[:4]
     if halves:
-        tokens, segments, bundle, later = refs[:4]
-        x_out, q_out, k_out, v_out, seg_out, w_out, o_out, gain_out, later_out = refs[4:13]
-        wg_s, w_send, w_recv, w_self = refs[13:17]
+        weights, norms = refs[4:8], refs[8]
+        x_out, q_out, k_out, v_out, seg_out, mail_out, later_out, w_out, o_out, gain_out = refs[9:19]
+        wg_s, w_send, w_recv = refs[19:22]
     else:
-        tokens, segments, w_out, gain_out, later = refs[:5]
-        x_out, q_out, k_out, v_out, seg_out, later_out = refs[5:11]
-    (l_send, l_recv, x_s, kv_s, x_send, x_recv, x_self, kv_send, kv_recv, kv_self, seg_send, seg_recv, seg_self) = refs[-13:]
+        w_out, gain_out = refs[4:6]
+        x_out, q_out, k_out, v_out, seg_out, mail_out, later_out = refs[6:13]
+    (g_send, g_recv, g_self, l_send, l_recv, x_s, kv_s, x_send, x_recv, x_self, kv_send, kv_recv, kv_self, seg_send, seg_recv, seg_self) = refs[-16:]
     d, t = 2 * lax.axis_index("plane") + lax.axis_index("core"), lax.axis_index("tensor")
     core = d % 2
     width = x_out.shape[1]
@@ -541,16 +500,33 @@
     greet(nd, nt, d, t)
 
     if halves:
-        own = pltpu.make_async_copy(bundle, wg_s.at[d, t], w_self)
-        own.start()
+        line = lax.broadcasted_iota(jnp.int32, (8, width), 0)
+        lane = lax.broadcasted_iota(jnp.int32, (8, width), 1)
+        gains = jnp.zeros((8, width), F32)
+        for n in range(2):
+            for k in range(share):
+                here = (line == n) & (lane == (d * nt + t) * share + k)
+                gains = jnp.where(here, norms[n, k], gains)
+        own = [weight[...].astype(F32) for weight in weights] + [gains]
+        rest = wg_s.shape[2] - 4 * share - 8
+        own = own + ([jnp.zeros((rest, width), F32)] if rest else [])
+        wg_s[d, t] = jnp.concatenate(own).astype(BF16)
         z_copies = []
         for s in range(1, nt):
-            copy = remote(bundle, wg_s.at[d, t], w_send.at[0, 0, s], w_recv.at[0, 0, s], (d, lax.rem(t + s, nt)))
+            slab = wg_s.at[d, t]
+            copy = remote(slab, slab, w_send.at[0, 0, s], w_recv.at[0, 0, s], (d, lax.rem(t + s, nt)))
             copy.start()
             z_copies.append(copy)
-        own.wait()
         for copy in z_copies:
             copy.wait()
+
+    g_copies = []
+    for m in range(micro):
+        there = mail_out.at[2 * m + core]
+        g_copies.append(pltpu.make_async_copy(grads.at[m, :, core], there, g_self.at[m]))
+        g_copies.append(remote(grads.at[m, :, 1 - core], there, g_send.at[m], g_recv.at[m], (flip(d, 1), t)))
+    for copy in g_copies:
+        copy.start()
 
     sends = []
     for m in range(micro):
@@ -639,7 +615,7 @@
             near.start()
             far.start()
             kv_copies += [near, far]
-    for copy in kv_copies + l_copies:
+    for copy in kv_copies + l_copies + g_copies:
         copy.wait()
     for here, far, near in sends:
         pl.when(jnp.logical_not(here))(far.wait_send)
@@ -654,13 +630,14 @@
         seg_there.wait_recv()
 
 
-def start(tokens, segments, bundle, later, share):
+def start(tokens, grads, segments, weights, norms, later):
     micro, _, rows, width = tokens.shape
     nd, nt = 2 * lax.axis_size("plane"), lax.axis_size("tensor")
     count = rows * nt // 2
     blocks = count // BLOCK
     per = blocks // nt
-    length = bundle.shape[0]
+    share = weights[0].shape[0]
+    length = 4 * share + 8 + -(4 * share + 8) % 16
     dma = pltpu.SemaphoreType.DMA
     vmem = pl.BlockSpec(memory_space=pltpu.VMEM)
     shaped = jax.ShapeDtypeStruct
@@ -668,34 +645,39 @@
     inside = 2 * share % 16 == 0 and length >= 32
     middle = length // 32 * 16
     if inside:
-        halves, given = [(0, middle), (middle, length)], [bundle]
+        halves, given = [(0, middle), (middle, length)], [*weights, jnp.stack(norms).astype(F32)]
+        given_specs = [vmem] * 4 + [SCALARS]
         gathered_specs = [vmem, vmem, vmem]
         gathered = [shaped((width, 3 * width), BF16), shaped((width, width), BF16), shaped((8, width), F32)]
         scratch = [
             pltpu.VMEM((nd, nt, length, width), BF16),
-            dma((3, nd.bit_length(), most)), dma((3, nd.bit_length(), most)), dma,
+            dma((3, nd.bit_length(), most)), dma((3, nd.bit_length(), most)),
         ]
     else:
-        slabs = lax.all_gather(bundle, AXES, axis=0, tiled=False)
+        place = (lax.axis_index("plane") * 2 * nt + lax.axis_index("core") * nt + lax.axis_index("tensor")) * share
+        gains = lax.dynamic_update_slice(jnp.zeros((8, width), BF16), jnp.stack(norms), (0, place))
+        slabs = lax.all_gather(jnp.concatenate([*weights, gains]), AXES, axis=0, tiled=False)
         w_qkv = slabs[:, : 3 * share].reshape(nd * nt, 3, share, width).transpose(0, 2, 1, 3)
         w_qkv = w_qkv.reshape(width, 3 * width)
         w_out = slabs[:, 3 * share : 4 * share].reshape(width, width)
         gains = jnp.sum(slabs[:, 4 * share : 4 * share + 8].astype(F32), axis=0)
-        halves, given, gathered_specs, gathered, scratch = [], [w_qkv, gains], [], [], []
+        halves, given, given_specs, gathered_specs, gathered, scratch = [], [w_qkv, gains], [vmem, vmem], [], [], []
     results = pl.pallas_call(
         functools.partial(start_kernel, nd, nt, share, halves),
-        in_specs=[ANY, ANY] + ([ANY] if inside else [vmem, vmem]) + [ANY],
-        out_specs=[vmem, vmem, ANY, ANY, ANY] + gathered_specs + [ANY],
+        in_specs=[ANY, ANY, ANY, ANY] + given_specs,
+        out_specs=[vmem, vmem, ANY, ANY, ANY, vmem, ANY] + gathered_specs,
         out_shape=[
             shaped((count, width), BF16),
             shaped((count, width), BF16),
             shaped((blocks, 2, BLOCK, width), BF16),
             shaped((blocks, 2, BLOCK, width), BF16),
             shaped((2 * blocks, BLOCK), jnp.int32),
+            shaped((nt, per, BLOCK, width), BF16),
+            shaped((nt - 1,) + later.shape, BF16),
             *gathered,
-            shaped((nt - 1,) + later.shape, BF16),
         ],
         scratch_shapes=scratch + [
+            dma((micro,)), dma((micro,)), dma((micro,)),
             dma((nt,)), dma((nt,)),
             pltpu.VMEM((blocks, BLOCK, width), BF16),
             pltpu.VMEM((2, nt, per, BLOCK, width), BF16),
@@ -704,16 +686,17 @@
             dma, dma, dma,
         ],
         compiler_params=pltpu.CompilerParams(
-            collective_id=0, has_side_effects=True, vmem_limit_bytes=56 << 20
+            collective_id=0, has_side_effects=True, vmem_limit_bytes=62 << 20
         ),
         name="start",
     )(
         tokens.reshape(micro, rows // TILE, 2, BLOCK, width),
+        grads.reshape(micro, rows // TILE, 2, BLOCK, width),
         segments.reshape(micro, 2 * blocks, BLOCK),
+        later,
         *given,
-        later,
     )
-    return results if inside else (*results[:5], w_qkv, w_out, gains, results[5])
+    return results if inside else (*results, w_qkv, w_out, gains)
 
 
 def gelu_parts(v):
@@ -725,13 +708,11 @@
 
 
 def middle_kernel(rb, nd, nt, share, inside, *refs):
-    x_ref, att_ref, w_out, gain_ref, own_ref, rest_ref = refs[:6]
-    dys, refs = refs[6 : 6 + nt], refs[6 + nt :]
-    outs, refs = refs[:nt], refs[nt:]
-    after_ref, datt_ref, dwo_ref, dgain_ref, part_ref = refs[:5]
-    dy_ref, h_s, ht_s, dyt_s, o_s, dh_s, hid_s, dhid_s, w_s, sems = refs[5:15]
+    x_ref, att_ref, w_out, gain_ref, own_ref, rest_ref, dy_all = refs[:7]
+    out_ref, after_ref, datt_ref, dwo_ref, dgain_ref, part_ref = refs[7:13]
+    dy_ref, h_s, ht_s, dyt_s, o_s, dh_s, hid_s, dhid_s, w_s, dy_sem = refs[13:23]
     if inside:
-        g_s, core_s, plane_s, c_send, c_recv, p_send, p_recv = refs[15:]
+        g_s, core_s, plane_s, c_send, c_recv, p_send, p_recv = refs[23:]
     step = pl.program_id(0)
     d, t = 2 * lax.axis_index("plane") + lax.axis_index("core"), lax.axis_index("tensor")
     count, width = x_ref.shape
@@ -743,12 +724,8 @@
     def _():
         if inside:
             greet(nd, nt, d, t)
-        copies = []
-        for turn, dy in enumerate(dys):
-            rows = pl.ds(pl.multiple_of(seat(turn)[1] * (count // nt), count // nt), count // nt)
-            copies.append(pltpu.make_async_copy(dy, dy_ref.at[rows], sems.at[turn]))
-        for copy in copies:
-            copy.start()
+        dy_copy = pltpu.make_async_copy(dy_all, dy_ref, dy_sem)
+        dy_copy.start()
         for r in parts:
             rows = slice(r, r + rb)
             after = x_ref[rows, :].astype(F32) + matmul(att_ref[rows, :], w_out[...])
@@ -760,8 +737,7 @@
             dh_s[rows, :] = jnp.zeros((rb, width), F32)
         for k in range(2):
             w_s[k] = own_ref[:, k * share : (k + 1) * share]
-        for copy in copies:
-            copy.wait()
+        dy_copy.wait()
         for r in parts:
             rows = slice(r, r + rb)
             dyt_s[:, rows] = dy_ref[rows, :].T
@@ -861,9 +837,7 @@
     def _():
         gain = gain_ref[...]
         total = jnp.zeros((8, width), F32)
-        for turn, out in enumerate(outs):
-            rows = pl.ds(pl.multiple_of(seat(turn)[1] * (count // nt), count // nt), count // nt)
-            out[...] = o_s[rows, :].astype(BF16)
+        out_ref[...] = o_s[...].astype(BF16)
         for point, r in enumerate(parts):
             rows = slice(r, r + rb)
             after = after_ref[rows, :]
@@ -889,13 +863,13 @@
             plane_done(nt - 1, len(bits) - 1)
 
 
-def feed_forward(x, attended, dys, w_out, gain, own, rest):
+def feed_forward(x, attended, dy, w_out, gain, own, rest):
     count, width = x.shape
     nd, nt, units = own.shape[0], rest.shape[1] + 1, own.shape[2]
     share = own.shape[1] // 2
     inside = share % 16 == 0 and nd >= 8
     rb = 256
-    rows, part = whole((count, width)), whole((count // nt, width))
+    rows = whole((count, width))
     dma = pltpu.SemaphoreType.DMA
     scratch = [
         pltpu.VMEM((count, width), BF16),
@@ -907,7 +881,7 @@
         pltpu.VMEM((count, units), BF16),
         pltpu.VMEM((count, units), BF16),
         pltpu.VMEM((2, nd, share, units), BF16),
-        dma((nt,)),
+        dma,
     ]
     if inside:
         stages = nd.bit_length() - 2
@@ -930,9 +904,11 @@
         in_specs=[
             rows, rows, whole((width, width)), whole((1, width)), whole(own.shape),
             pl.BlockSpec((nd, 1, 2 * share, units), lambda s: (0, jnp.clip(s - 1, 0, nt - 2), 0, 0)),
-        ] + [ANY] * nt,
-        out_specs=[part] * nt + [rows, rows, whole((width, width)), whole((8, width)), grads_spec],
-        out_shape=[jax.ShapeDtypeStruct((count // nt, width), BF16)] * nt + [
+            ANY,
+        ],
+        out_specs=[rows, rows, rows, whole((width, width)), whole((8, width)), grads_spec],
+        out_shape=[
+            jax.ShapeDtypeStruct((count, width), BF16),
             jax.ShapeDtypeStruct((count, width), F32),
             jax.ShapeDtypeStruct((count, width), BF16),
             jax.ShapeDtypeStruct((width, width), BF16),
@@ -943,7 +919,7 @@
         compiler_params=pltpu.CompilerParams(vmem_limit_bytes=62 << 20, **params),
         cost_estimate=cost(12 * count * width * nt * units, 4 * nd * nt * share * units),
         name="feed_forward",
-    )(x, attended, w_out, gain, own, rest, *dys)
+    )(x, attended, w_out, gain, own, rest, dy)
 
 
 def masks_of(bits):
@@ -963,26 +939,33 @@
 
 
 def finish_kernel(
-    nd, nt, share, inside, x_ref, dq_ref, dk_all, dv_all, after_ref, w_ref, gain_ref, dwo_ref, small_ref,
-    *refs,
+    nd, nt, share, inside, x_all, dq_all, dk_all, dv_all, after_all, w_all, gain_ref, dwo_all, small_ref,
+    ffn_ref, back, *refs,
 ):
-    tok_out, dw_out, small_out = refs[:3]
-    own_s, other_s, grads_s, ht_s, tok_s, own_sems, kv_send, kv_recv, tok_send, tok_recv, tok_self = refs[3:14]
+    tok_out, out_out, dw_out, small_out = refs[:4]
+    own_s, other_s, grads_s, ht_s, tok_s, own_sems, kv_send, kv_recv, tok_send, tok_recv, tok_self = refs[4:15]
+    b_send, b_recv, b_self, x_ref, dq_ref, after_ref, w_ref, dwo_ref, in_sems = refs[15:24]
     if inside:
-        slab_s, core_s, plane_s, z_s, sm_s, sm_in, g_send, g_recv, s_send, s_recv = refs[14:]
+        slab_s, core_s, plane_s, mine_s, z_s, sm_s, sm_in, g_send, g_recv, s_send, s_recv = refs[24:]
     d, t = 2 * lax.axis_index("plane") + lax.axis_index("core"), lax.axis_index("tensor")
     core = d % 2
-    count, width = x_ref.shape
+    count, width = x_all.shape
     per = tok_out.shape[1]
     rows_in = per * BLOCK
     holder = t % 2 == core
     bits = [1 << k for k in range(1, nd.bit_length() - 1)]
+    loads = [
+        pltpu.make_async_copy(far, near, in_sems.at[k])
+        for k, (far, near) in enumerate(
+            ((dq_all, dq_ref), (w_all, w_ref), (x_all, x_ref), (after_all, after_ref), (dwo_all, dwo_ref))
+        )
+    ]
+    own = [pltpu.make_async_copy(a.at[:, core], own_s.at[k], own_sems.at[k]) for k, a in enumerate((dk_all, dv_all))]
+    for copy in own + loads:
+        copy.start()
     greet(nd, nt, d, t)
 
     order = [lax.rem(t + s, nt) for s in list(range(1, nt)) + [0]]
-    own = [pltpu.make_async_copy(a.at[:, core], own_s.at[k], own_sems.at[k]) for k, a in enumerate((dk_all, dv_all))]
-    for copy in own:
-        copy.start()
     exchanged = []
     for s, source in enumerate(order):
         pair = []
@@ -993,8 +976,14 @@
                     kv_send.at[k, s], kv_recv.at[k, s], (flip(d, 1), t),
                 )
             )
-            pair[-1].start()
         exchanged.append(pair)
+    for copy in exchanged[0] + exchanged[1]:
+        copy.start()
+    b_copies = []
+    for m in range(out_out.shape[0]):
+        there = out_out.at[m, :, core]
+        b_copies.append(pltpu.make_async_copy(back.at[2 * m + core], there, b_self.at[m]))
+        b_copies.append(remote(back.at[2 * m + 1 - core], there, b_send.at[m], b_recv.at[m], (flip(d, 1), t)))
     gain = gain_ref[:1]
 
     def norms(rows):
@@ -1002,33 +991,29 @@
         scale = rms_scale(x)
         return x * scale, scale
 
-    def fill(bundle, at, source, first):
-        lines = source.shape[0] // share
-        for k in range(lines):
-            slab = first // share + k
-            slab_s[bundle, slab // nt, slab % nt, at : at + source.shape[1] // width * share] = jnp.concatenate(
-                [
-                    source[k * share : (k + 1) * share, m * width : (m + 1) * width]
-                    for m in range(source.shape[1] // width)
-                ]
-            ).astype(BF16)
-
-    halves = [(0, nt // 2), (nt // 2, nt)]
     routes = [[1] + bits, [1] + bits[::-1]]
+    rows_of_slab = width // nd
+
+    def fill(bundle, which, left, right):
+        for k in range(nd):
+            lines = slice(k * rows_of_slab, (k + 1) * rows_of_slab)
+            if k % 2 == 0:
+                both = matmul(left[lines.start : lines.stop + rows_of_slab, :], right)
+                slab_s[bundle, which, k : k + 2] = both.astype(BF16).reshape(2, rows_of_slab, width)
 
     def stage_copies(bundle, stage):
         copies, adds = [], []
-        for h, (lo, hi) in enumerate(halves):
-            bit, part = routes[h][stage], pl.ds(lo, hi - lo)
+        for h in range(2):
+            bit = routes[h][stage]
             for k, mask in enumerate(masks_of(routes[h][stage + 1 :])):
                 buffer = core_s.at[bundle] if stage == 0 else plane_s.at[bundle, stage - 1]
                 copies.append(
                     remote(
-                        slab_s.at[bundle, flips(flip(d, bit), mask), part], buffer.at[k, part],
+                        slab_s.at[bundle, h, flips(flip(d, bit), mask)], buffer.at[h, k],
                         g_send.at[bundle, h, stage, k], g_recv.at[bundle, h, stage, k], (flip(d, bit), t),
                     )
                 )
-                adds.append((flips(d, mask), lo, hi, buffer, k))
+                adds.append((h, flips(d, mask), buffer, k))
         return copies, adds
 
     def stage_start(bundle, stage):
@@ -1039,9 +1024,16 @@
         copies, adds = stage_copies(bundle, stage)
         for copy in copies:
             copy.wait()
-        for mine, lo, hi, buffer, k in adds:
-            both = slab_s[bundle, mine, lo:hi].astype(F32) + buffer[k, lo:hi].astype(F32)
-            slab_s[bundle, mine, lo:hi] = both.astype(BF16)
+        last = stage == len(bits)
+        totals = []
+        for h, mine, buffer, k in adds:
+            total = slab_s[bundle, h, mine].astype(F32) + buffer[h, k].astype(F32)
+            if last:
+                totals.append(total.reshape(nt, share, width))
+            else:
+                slab_s[bundle, h, mine] = total.astype(BF16)
+        if last:
+            mine_s[bundle] = jnp.concatenate(totals, axis=1).astype(BF16)
 
     def z_copies(bundle):
         copies = []
@@ -1049,7 +1041,7 @@
             to = lax.rem(t + s, nt)
             copies.append(
                 remote(
-                    slab_s.at[bundle, d, to], z_s.at[bundle, s],
+                    mine_s.at[bundle, to], z_s.at[bundle, s],
                     g_send.at[bundle, 2, 0, s], g_recv.at[bundle, 2, 0, s], (d, to),
                 )
             )
@@ -1064,23 +1056,27 @@
             copies.append(remote(sm_s, sm_in.at[k], s_send.at[k], s_recv.at[k], (d, lax.rem(t + s, nt))))
         return copies
 
-    d_gain = jnp.zeros((8, width), F32)
-    sends = []
+    sends, gains = [], []
     to_core = d - core + t % 2
-    for s, source in enumerate(order):
-        if s == 0:
-            for copy in own:
-                copy.wait()
+
+    def sum_group(s):
+        source = order[s]
         for copy in exchanged[s]:
             copy.wait()
+        for copy in exchanged[s + 2] if s + 2 < nt else []:
+            copy.start()
         rows = pl.ds(pl.multiple_of(source * rows_in, rows_in), rows_in)
         grads_s[rows, :width] = dq_ref[rows, :]
         for k in range(2):
             total = own_s[k, pl.ds(per * source, per)].astype(F32) + other_s[k, pl.ds(per * source, per)].astype(F32)
             grads_s[rows, (k + 1) * width : (k + 2) * width] = total.reshape(rows_in, width).astype(BF16)
+
+    def token_group(s):
+        source = order[s]
+        rows = pl.ds(pl.multiple_of(source * rows_in, rows_in), rows_in)
         dh = right_t(grads_s[rows, :], w_ref[...])
         normed, scale = norms(rows)
-        d_gain = d_gain + jnp.sum((dh * normed).reshape(rows_in // 8, 8, width), axis=0)
+        gains.append(jnp.sum((dh * normed).reshape(rows_in // 8, 8, width), axis=0))
         tok = after_ref[rows, :] + rms_back(dh, normed, scale, gain)
         tok_s[s] = tok.astype(BF16).reshape(per, BLOCK, width)
         here = (source == t) & holder
@@ -1090,56 +1086,67 @@
         pl.when(jnp.logical_not(here))(far.start)
         pl.when(here)(near.start)
         sends.append((here, far, near))
-        if s == 0:
-            for r in range(0, count, rows_in):
-                lines = slice(r, r + rows_in)
-                normed, scale = norms(lines)
-                ht_s[:, lines] = (normed * gain).astype(BF16).T
-            if inside:
-                for r in range(0, width, 8 * share):
-                    lines = slice(r, r + 8 * share)
-                    dwo = dwo_ref[lines, :].astype(F32)
-                    fill(0, 0, jnp.concatenate([matmul(ht_s[lines, :], dq_ref[...]), dwo], axis=1), r)
-                stage_start(0, 0)
-        if s == 1 and inside:
-            stage_done(0, 0)
-            stage_start(0, 1)
-
+
+    for copy in own + loads:
+        copy.wait()
+    for r in range(0, count, rows_in):
+        lines = slice(r, r + rows_in)
+        normed, scale = norms(lines)
+        ht_s[:, lines] = (normed * gain).astype(BF16).T
+    if inside:
+        slab_s[0, 1] = dwo_ref[...].reshape(nd, rows_of_slab, width)
+        fill(0, 0, ht_s, dq_ref[...])
+        stage_start(0, 0)
+    for s in range(nt // 2):
+        sum_group(s)
+        token_group(s)
+    if inside:
+        stage_done(0, 0)
+        stage_start(0, 1)
+    for s in range(nt // 2, nt):
+        sum_group(s)
+    if inside:
+        for which in range(2):
+            fill(1, which, ht_s, grads_s[:, (which + 1) * width : (which + 2) * width])
+        stage_start(1, 0)
+    for s in range(nt // 2, nt):
+        token_group(s)
+
+    for copy in b_copies:
+        copy.start()
     small = small_ref[...]
     line = lax.broadcasted_iota(jnp.int32, small.shape, 0)
-    small = small + jnp.where(line == 0, jnp.sum(d_gain, axis=0, keepdims=True), 0.0)
+    small = small + jnp.where(line == small.shape[0] - 2, jnp.sum(sum(gains), axis=0, keepdims=True), 0.0)
+    small = small + jnp.where(line == small.shape[0] - 1, jnp.sum(ffn_ref[...], axis=0, keepdims=True), 0.0)
     if inside:
         sm_s[...] = small
         tiny = small_copies(0)
         for copy in tiny:
             copy.start()
-        for stage in range(1, len(bits)):
-            stage_done(0, stage)
-            stage_start(0, stage + 1)
-        for r in range(0, width, 8 * share):
-            fill(1, 0, matmul(ht_s[r : r + 8 * share, :], grads_s[:, width:]), r)
-        stage_start(1, 0)
-        stage_done(0, len(bits))
-        first_z = z_copies(0)
-        for copy in first_z:
-            copy.start()
         for stage in range(len(bits) + 1):
             for copy in tiny:
                 copy.wait()
             sm_s[...] += sm_in[stage]
+            tiny = small_copies(stage + 1)
+            for copy in tiny:
+                copy.start()
             stage_done(1, stage)
             if stage < len(bits):
                 stage_start(1, stage + 1)
-            tiny = small_copies(stage + 1)
-            for copy in tiny:
-                copy.start()
+                stage_done(0, stage + 1)
+                if stage + 1 < len(bits):
+                    stage_start(0, stage + 2)
+                else:
+                    first_z = z_copies(0)
+                    for copy in first_z:
+                        copy.start()
         second_z = z_copies(1)
         for copy in second_z:
             copy.start()
         for copy in first_z + second_z + tiny:
             copy.wait()
         for bundle in range(2):
-            total = slab_s[bundle, d, t].astype(F32)
+            total = mine_s[bundle, t].astype(F32)
             for s in range(1, nt):
                 total = total + z_s[bundle, s].astype(F32)
             dw_out[bundle * 2 * share : (bundle + 1) * 2 * share] = total
@@ -1151,6 +1158,8 @@
             dw_out[lines, : 3 * width] = matmul(ht_s[lines, :], grads_s[...]).astype(BF16)
             dw_out[lines, 3 * width :] = dwo_ref[lines, :]
 
+    for copy in b_copies:
+        copy.wait()
     for here, far, near in sends:
         pl.when(jnp.logical_not(here))(far.wait_send)
         pl.when(here)(near.wait)
@@ -1162,7 +1171,7 @@
             pl.when(jnp.logical_not(here))(back.wait_recv)
 
 
-def finish(x, dq, dk_all, dv_all, after, w_qkv, gains, dwo, small, share, micro):
+def finish(x, dq, dk_all, dv_all, after, w_qkv, gains, dwo, small, gain_ffn, back, share, micro):
     count, width = x.shape
     nd, nt = 2 * lax.axis_size("plane"), lax.axis_size("tensor")
     inside = 2 * share % 16 == 0 and nd >= 8
@@ -1178,14 +1187,18 @@
         pltpu.VMEM((width, count), BF16),
         pltpu.VMEM((nt, per, BLOCK, width), BF16),
         dma((2,)), dma((2, nt)), dma((2, nt)), dma((nt,)), dma((nt,)), dma,
+        dma((micro,)), dma((micro,)), dma((micro,)),
+        pltpu.VMEM(x.shape, x.dtype), pltpu.VMEM(dq.shape, dq.dtype), pltpu.VMEM(after.shape, after.dtype),
+        pltpu.VMEM(w_qkv.shape, w_qkv.dtype), pltpu.VMEM(dwo.shape, dwo.dtype), dma((5,)),
     ]
     if inside:
         most = max(nd // 2, nt)
         stages = nd.bit_length() - 1
         scratch += [
-            pltpu.VMEM((2, nd, nt, 2 * share, width), BF16),
-            pltpu.VMEM((2, nd // 2, nt, 2 * share, width), BF16),
-            pltpu.VMEM((2, stages - 1, nd // 4, nt, 2 * share, width), BF16),
+            pltpu.VMEM((2, 2, nd, nt * share, width), BF16),
+            pltpu.VMEM((2, 2, nd // 2, nt * share, width), BF16),
+            pltpu.VMEM((2, stages - 1, 2, nd // 4, nt * share, width), BF16),
+            pltpu.VMEM((2, nt, 2 * share, width), BF16),
             pltpu.VMEM((2, nt, 2 * share, width), BF16),
             pltpu.VMEM(small.shape, F32),
             pltpu.VMEM((stages + nt,) + small.shape, F32),
@@ -1193,20 +1206,73 @@
         ]
     return pl.pallas_call(
         functools.partial(finish_kernel, nd, nt, share, inside),
-        in_specs=[vmem, vmem, ANY, ANY, vmem, vmem, vmem, vmem, vmem],
-        out_specs=[vmem, vmem, vmem],
+        in_specs=[ANY, ANY, ANY, ANY, ANY, ANY, vmem, ANY, vmem, vmem, ANY],
+        out_specs=[vmem, vmem, vmem, vmem],
         out_shape=[
+            shaped((micro, per, 2, BLOCK, width), BF16),
             shaped((micro, per, 2, BLOCK, width), BF16),
             shaped((4 * share, width), F32) if inside else shaped((width, 4 * width), BF16),
             shaped(small.shape, F32),
         ],
         scratch_shapes=scratch,
         compiler_params=pltpu.CompilerParams(
-            collective_id=1, has_side_effects=True, vmem_limit_bytes=60 << 20
+            collective_id=1, has_side_effects=True, vmem_limit_bytes=62 << 20
         ),
         cost_estimate=cost(24 * count * width * width, 16 * count * width),
         name="finish",
-    )(x, dq, dk_all, dv_all, after, w_qkv, gains, dwo, small)
+    )(x, dq, dk_all, dv_all, after, w_qkv, gains, dwo, small, gain_ffn, back.reshape(nt, per, BLOCK, width))
+
+
+def emit_kernel(heads, share, tok_ref, out_ref, dw_ref, ffn_ref, small_ref, tok, out, *rest):
+    grads, ups, gains, mixes = rest[:4], rest[4:6], rest[6:8], rest[8:10]
+    tok[...] = tok_ref[...].astype(F32)
+    out[...] = out_ref[...]
+
+    @pl.when(pl.program_id(0) == 0)
+    def _():
+        for grad, k in zip(grads, (0, 2, 3, 1)):
+            grad[...] = dw_ref[k * share : (k + 1) * share]
+        half = ffn_ref.shape[0] // 2
+        for k, up in enumerate(ups):
+            up[...] = ffn_ref[k * half : (k + 1) * half].astype(F32)
+        width = small_ref.shape[1]
+        place = (
+            (lax.axis_index("plane") * 2 + lax.axis_index("core")) * lax.axis_size("tensor") + lax.axis_index("tensor")
+        ) * share
+        row = lax.broadcasted_iota(jnp.int32, (width, share), 0)
+        col = lax.broadcasted_iota(jnp.int32, (width, share), 1)
+        exact = dict(preferred_element_type=F32, precision=lax.Precision.HIGHEST)
+        own = jnp.dot(small_ref[small_ref.shape[0] - 8 :, :], (row == place + col).astype(F32), **exact)
+        for k, gain in enumerate(gains):
+            gain[...] = own[6 + k : 7 + k]
+        lines = 2 * heads * BLOCK // width
+        sums = jnp.concatenate(
+            [small_ref[:lines, k * BLOCK : (k + 1) * BLOCK] for k in range(width // BLOCK)]
+        )[:, :heads]
+        mixes[0][...] = sums[:heads].T * (width // heads) ** (-0.5)
+        mixes[1][...] = sums[heads:]
+
+
+def emit(tok, out, dw, ffn, small, heads, share):
+    width = small.shape[1]
+    micro, per, cores, block, _ = tok.shape
+    rows = per * cores * block
+
+    def part(k):
+        return pl.BlockSpec((1, rows, width), lambda i: (i, 0, 0))
+
+    shaped = jax.ShapeDtypeStruct
+    small_shapes = [(share, width)] * 4 + [(ffn.shape[0] // 2, width)] * 2 + [(1, share)] * 2 + [(heads, heads)] * 2
+    return pl.pallas_call(
+        functools.partial(emit_kernel, heads, share),
+        grid=(micro,),
+        in_specs=[part(0), part(1), whole(dw.shape), whole(ffn.shape), whole(small.shape)],
+        out_specs=[part(0), part(1)] + [whole(shape) for shape in small_shapes],
+        out_shape=[shaped((micro, rows, width), F32), shaped((micro, rows, width), BF16)]
+        + [shaped(shape, F32) for shape in small_shapes],
+        compiler_params=pltpu.CompilerParams(vmem_limit_bytes=62 << 20),
+        name="emit",
+    )(tok.reshape(micro, rows, width), out.reshape(micro, rows, width), dw, ffn, small)
 
 
 def per_device(
@@ -1224,16 +1290,13 @@
     d, t = 2 * lax.axis_index("plane") + lax.axis_index("core"), lax.axis_index("tensor")
     core = d % 2
 
-    place = (d * nt + t) * share
-    gains = lax.dynamic_update_slice(jnp.zeros((8, width), BF16), jnp.stack([norm_attn, norm_ffn]), (0, place))
-    fill = jnp.zeros((-(4 * share + 8) % 16, width), BF16)
-    bundle = jnp.concatenate([w_query, w_key, w_value, w_out, gains, fill])
     later = jnp.concatenate([w_up, w_down])
     own_rows = lax.all_gather(later, ("plane", "core"), axis=0, tiled=False)
-    x, query, k_all, v_all, segs, w_qkv, all_out, gains, later = start(tokens, segments, bundle, later, share)
+    x, query, k_all, v_all, segs, mail, later, w_qkv, all_out, gains = start(
+        tokens, out_grad, segments, [w_query, w_key, w_value, w_out], [norm_attn, norm_ffn], later
+    )
     k_all, v_all = (a.reshape(2 * blocks, BLOCK, width) for a in (k_all, v_all))
-    x, out_grad = lax.optimization_barrier((x, out_grad))
-    grad_turns = to_sequences(out_grad)
+    dy = lax.all_to_all(mail, "tensor", 0, 0, tiled=True).reshape(count, width)
     rest_rows = lax.all_gather(later, ("plane", "core"), axis=0, tiled=False)
 
     def by_lane(mix):
@@ -1243,54 +1306,42 @@
     post = by_lane(post_mix)
 
     attended, u, lse = attend(query, k_all, v_all, segs, pre, post)
-    *out_turns, grad_after, grad_attended, grad_w_out, grad_gain_ffn, part_both = feed_forward(
-        x, attended, grad_turns, all_out, gains[1:2], own_rows, rest_rows
+    output, grad_after, grad_attended, grad_w_out, grad_gain_ffn, part_both = feed_forward(
+        x, attended, dy, all_out, gains[1:2], own_rows, rest_rows
     )
-    grad_gain_ffn = jnp.sum(grad_gain_ffn, axis=0)
-    out = from_sequences(out_turns, micro)
+    back = lax.all_to_all(output.reshape(nt, count // nt, width), "tensor", 0, 0, tiled=True)
     if part_both.ndim > 3:
         part_both = lax.dynamic_slice_in_dim(jnp.concatenate([part_both[:, ::-1]] * 2, axis=1), nt - 1 - t, nt, 1)
         part_both = lax.psum_scatter(part_both, ("plane", "core"), scatter_dimension=0, tiled=False)
-    part_both = lax.psum_scatter(part_both, "tensor", scatter_dimension=0, tiled=False).astype(F32)
-    part_both = part_both.reshape((2,) + w_up.shape)
-
-    grad_query, grad_key, grad_value, d_pre, d_post = attend_back(
+    part_both = lax.psum_scatter(part_both, "tensor", scatter_dimension=0, tiled=False)
+    part_both = part_both.reshape(2 * w_up.shape[0], w_up.shape[1])
+
+    grad_query, grad_key, grad_value, small = attend_back(
         query, grad_attended, u, lse, k_all, v_all, segs, pre, post
     )
-
-    def spread(d_mix):
-        total = d_mix.reshape(heads, 8, heads, head_width).sum((1, 3)).reshape(-1)
-        return jnp.pad(total, (0, width - total.shape[0]))
-
-    small = jnp.zeros((8, width), F32).at[1].set(grad_gain_ffn)
-    small = small.at[2].set(spread(d_pre)).at[3].set(spread(d_post))
-    x, out = lax.optimization_barrier((x, out))
-    d_tokens, owned, small = finish(
+    d_tokens, out, owned, small = finish(
         x, grad_query, grad_key.reshape(blocks, 2, BLOCK, width), grad_value.reshape(blocks, 2, BLOCK, width),
-        grad_after, w_qkv, gains, grad_w_out, small, share, micro,
+        grad_after, w_qkv, gains, grad_w_out, small, grad_gain_ffn, back, share, micro,
     )
-    d_tokens = d_tokens.reshape(tokens.shape).astype(F32)
     if owned.dtype == BF16:
         owned = lax.psum_scatter(owned, AXES, scatter_dimension=0, tiled=True).astype(F32)
-        owned = [owned[:, k * width : (k + 1) * width] for k in range(4)]
+        owned = jnp.concatenate([owned[:, k * width : (k + 1) * width] for k in (0, 3, 1, 2)])
         small = lax.psum(small, AXES)
-    else:
-        owned = [owned[k * share : (k + 1) * share] for k in (0, 2, 3, 1)]
-    gain_grads = lax.dynamic_slice_in_dim(small, place, share, 1)
-    pairs = heads * heads
+    d_tokens, out, *grads = emit(d_tokens, out, owned, part_both, small, heads, share)
+    d_query, d_key, d_value, d_out, d_up, d_down, d_gain_attn, d_gain_ffn, d_pre, d_post = grads
     return (
-        out,
-        d_tokens,
-        owned[0],
-        owned[1],
-        owned[2],
-        owned[3],
-        gain_grads[0],
-        gain_grads[1],
-        small[2, :pairs].reshape(heads, heads).T * head_width ** (-0.5),
-        small[3, :pairs].reshape(heads, heads),
-        part_both[0],
-        part_both[1],
+        out.reshape(tokens.shape),
+        d_tokens.reshape(tokens.shape),
+        d_query,
+        d_key,
+        d_value,
+        d_out,
+        d_gain_attn.reshape(share),
+        d_gain_ffn.reshape(share),
+        d_pre,
+        d_post,
+        d_up,
+        d_down,
     )
 
 

time: 402 us -> 382 us (0.950)
  local copies, waits for them, and re-layouts: 16.2 us -> 6.77 us
  other arithmetic: 8.12 us -> 1.25 us
    pallas_call x1, Pallas kernels: 79.1 us -> 60.9 us  [finish(): pl.pallas_call(functools.partial(finish_kernel, nd, nt, share, inside), i...]
    pallas_call x1, Pallas kernels: 65.5 us -> 80.2 us  [attend_back(): pl.pallas_call(functools.partial(backward_kernel, heads, groups), grid=(b...]
    ppermute x8 -> x0, starting transfers between devices: 14.6 us -> none  [send(): return lax.ppermute(x, AXES, pairs)]
    all_to_all x0 -> x2, starting transfers between devices: none -> 12.9 us  [the longest x1 9.3 us: per_device(): dy = lax.all_to_all(mail, 'tensor', 0, 0, tiled=True).reshape(count, width)]
    pallas_call x1, Pallas kernels: 33.6 us -> 39.5 us  [attend(): pl.pallas_call(functools.partial(forward_kernel, heads, groups, most), gr...]
    unnamed x36 -> x11, local copies, waits for them, and re-layouts: 7.14 us -> 2.82 us
  transfers between devices with their start and end apart: 11 -> 5, of which waited for: 1 -> 1; matrix products, arithmetic and copies ran while one was open for 4% -> 1% of each run, Pallas kernels for 67% -> 70%
where the time goes in v4:
time: 382 us; the launch traced here: 376 us
  Pallas kernels  339 us (89%)
  between operations  14.1 us (4%)
  starting transfers between devices  13 us (3%)
  local copies, waits for them, and re-layouts  6.77 us (2%)
    pallas_call x1, Pallas kernels, start(): pl.pallas_call(functools.partial(start_kernel, nd, nt, share, halves), in...  81.5 us
    pallas_call x1, Pallas kernels, attend_back(): pl.pallas_call(functools.partial(backward_kernel, heads, groups), grid=(b...  80.2 us
    pallas_call x1, Pallas kernels, feed_forward(): pl.pallas_call(functools.partial(middle_kernel, rb, nd, nt, share, inside...  71.9 us
    pallas_call x1, Pallas kernels, finish(): pl.pallas_call(functools.partial(finish_kernel, nd, nt, share, inside), i...  60.9 us
    pallas_call x1, Pallas kernels, attend(): pl.pallas_call(functools.partial(forward_kernel, heads, groups, most), gr...  39.5 us
    all_to_all x1, starting transfers between devices, per_device(): dy = lax.all_to_all(mail, 'tensor', 0, 0, tiled=True).reshape(count, width)  9.3 us
  transfers between devices with their start and end apart: 5, of which 1 were waited for; matrix products, arithmetic and copies ran while one was open for 1% of the time, Pallas kernels for 70%

profile of v4, /device:TPU:0, one launch (start us, length us, event | category | flops | bytes accessed | tf_op | source)
XLA Modules:
  0.0 376.3 jit_solution(11543056038208716681)
XLA Ops:
  7.2 0.0 all-gather.5.cloned.1.call-start
  7.2 0.9 constant_dynamic-update-slice_fusion.1
  8.1 0.9 constant_dynamic-update-slice_fusion.refs_3_
  9.1 0.0 copy-start
  9.1 0.7 copy-done
  9.8 0.0 all-gather.5.cloned.1.call-update
  9.8 0.0 all-gather.7.cloned.1.call-start
  9.9 1.2 maximum_convert_fusion.refs_8_
  11.1 81.5 %start.1 = (bf16[1024,768]{1,0:T(8,128)(2,1)}, bf16[1024,768]{1,0:T(8,128)(2,1)}, bf16[8,2,128,768]{3,2,1,0:T(8,128)(2,1)}, bf16[8,2,128,768]{3,2,1,0:T(8,128)(2...) custom-call(bf16[2,2,2,128,768]{4,3,2,1,0:T(8,128)(2,1)} %bitcast.33, ...), custom_call_target="tpu_custom_call" | custom-call | tf_op jit(solution)/shard_map/start/pallas_call | solution.py:665
  92.6 0.0 all-gather.7.cloned.1.call-update
  92.6 0.0 copy-start.4
  92.6 0.0 copy-start.3
  92.6 9.3 %all-to-all-start = ((bf16[4,2,128,768]{3,2,1,0:T(8,128)(2,1)}), bf16[4,2,128,768]{3,2,1,0:T(8,128)(2,1)S(1)}, u32[]{:S(2)}, u32[]{:S(2)}) async-start(bf16[4,2,128,768]{3,2,1,0:T(8,128)(2,1)} %get-tuple-element.60), calls=%async_computation | async-start | bytes 3145728 | tf_op jit(solution)/shard_map/all_to_all | solution.py:1299
  102.0 0.1 copy.28
  102.0 0.1 broadcast_in_dim.11
  102.2 0.7 convert_element_type.21.pre_ref
  102.9 0.1 broadcast_in_dim.12
  103.0 0.7 reshape.84.post_ref
  103.7 1.3 slice.3.refs_3_
  105.0 39.5 %attend.1 = (bf16[1024,768]{1,0:T(8,128)(2,1)}, bf16[8,12,128,768]{3,2,1,0:T(8,128)(2,1)}, f32[8,1536,128]{2,1,0:T(8,128)}) custom-call(bf16[1024,768]{1,0:T(8,128)(2,1)} %get-tuple-element.52.q_ref, bf16[16,128,768]{2,1,0:T(8,128)(2,1)} %bitcast.40, bf16[16,128,768]{2,1,0:T(8,128)(2,1)} %bitcast.42, s32[16,128]{1,0:T(8,128)} %get-tuple-element.55.seg_low, ...), custom_call_target="tpu_custom_call" | custom-call | flops 38654705664 | bytes 37748736 | tf_op jit(solution)/shard_map/attend/pallas_call | solution.py:248
  144.5 0.0 all-to-all-done
  144.5 0.0 copy-start.1
  144.5 0.0 all-gather.5.cloned.1.call-done
  144.5 2.6 all-gather.7.cloned.1.call-done
  147.1 71.9 %feed_forward.1 = (bf16[1024,768]{1,0:T(8,128)(2,1)}, f32[1024,768]{1,0:T(8,128)}, bf16[1024,768]{1,0:T(8,128)(2,1)}, bf16[768,768]{1,0:T(8,128)(2,1)}, f32[8,768]{1,0:T(8,128)}, /*index=5*/bf16[4,192,768]{2,1,0:T(8,128)(2,1)}) custom-call(bf16[1024,768]{1,0:T(8,128)(2,1)} %get-tuple-element.51.refs_0_.x_all, bf16[1024,768]{1,0:T(8,128)(2,1)} %get-tuple-element.56.refs_1_, ...), custom_call_target="tpu_custom_call" | custom-call | flops 28991029248 | bytes 9437184 | tf_op jit(solution)/shard_map/feed_forward/pallas_call | solution.py:901
  219.1 0.0 reduce-scatter.2.cloned.1.call-update
  219.1 3.6 all-to-all-start.1
  222.7 80.2 %attend_back.1 = (bf16[1024,768]{1,0:T(8,128)(2,1)}, bf16[16,128,768]{2,1,0:T(8,128)(2,1)}, bf16[16,128,768]{2,1,0:T(8,128)(2,1)}, f32[8,768]{1,0:T(8,128)}) custom-call(bf16[1024,768]{1,0:T(8,128)(2,1)} %get-tuple-element.52.q_ref, bf16[1024,768]{1,0:T(8,128)(2,1)} %get-tuple-element.61.g_ref, bf16[8,12,128,768]{3,2,1,0:T(8,128)(2,1)} %get-tuple-element.62.u_ref, ...), custom_call_target="tpu_custom_call" | custom-call | flops 96636764160 | bytes 37748736 | tf_op jit(solution)/shard_map/attend_back/pallas_call | solution.py:409
  302.9 1.2 copy-done.2
  304.1 60.9 %finish.1 = (bf16[2,2,2,128,768]{4,3,2,1,0:T(8,128)(2,1)}, bf16[2,2,2,128,768]{4,3,2,1,0:T(8,128)(2,1)}, f32[96,768]{1,0:T(8,128)}, f32[8,768]{1,0:T(8,128)}) custom-call(bf16[1024,768]{1,0:T(8,128)(2,1)} %get-tuple-element.51.refs_0_.x_all, bf16[1024,768]{1,0:T(8,128)(2,1)} %get-tuple-element.64.dq_all, bf16[8,2,128,768]{3,2,1,0:T(8,128)(2,1)} %bitcast.51, ...), custom_call_target="tpu_custom_call" | custom-call | flops 14495514624 | bytes 12582912 | tf_op jit(solution)/shard_map/finish/pallas_call | solution.py:1207
  365.0 0.0 reduce-scatter.2.cloned.1.call-done
  365.0 4.5 %emit.1 = (f32[2,512,768]{2,1,0:T(8,128)}, bf16[2,512,768]{2,1,0:T(8,128)(2,1)}, f32[24,768]{1,0:T(8,128)}, f32[24,768]{1,0:T(8,128)}, f32[24,768]{1,0:T(8,128)}...) custom-call(bf16[2,512,768]{2,1,0:T(8,128)(2,1)} %bitcast.28, ...), custom_call_target="tpu_custom_call" | custom-call | tf_op jit(solution)/shard_map/emit/pallas_call | solution.py:1266
  (7 shorter events, 0.0 us)
Async XLA Ops:
  7.2 137.3 %all-gather.5.cloned.1.call-start = ((), (), s32[]{:S(2)}) async-start(), calls=%async_computation.4 | async-start | bytes 2654208 | tf_op jit(solution)/shard_map/all_gather | solution.py:1294
  9.1 0.7 copy-start
  9.8 137.3 %all-gather.7.cloned.1.call-start = ((), (), s32[]{:S(2)}) async-start(), calls=%async_computation.5 | async-start | bytes 7962624 | tf_op jit(solution)/shard_map/all_gather | solution.py:1300
  92.6 9.3 %copy-start.4 = (bf16[12,12]{1,0:T(8,128)(2,1)S(1)}, bf16[12,12]{1,0:T(8,128)(2,1)}, u32[]{:S(2)}) copy-start(bf16[12,12]{1,0:T(8,128)(2,1)} %param.21) | copy-start | bytes 868
  92.6 10.2 %copy-start.3 = (bf16[12,12]{1,0:T(8,128)(2,1)S(1)}, bf16[12,12]{1,0:T(8,128)(2,1)}, u32[]{:S(2)}) copy-start(bf16[12,12]{1,0:T(8,128)(2,1)} %param.22) | copy-start | bytes 868
  92.6 51.8 %all-to-all-start = ((bf16[4,2,128,768]{3,2,1,0:T(8,128)(2,1)}), bf16[4,2,128,768]{3,2,1,0:T(8,128)(2,1)S(1)}, u32[]{:S(2)}, u32[]{:S(2)}) async-start(bf16[4,2,128,768]{3,2,1,0:T(8,128)(2,1)} %get-tuple-element.60), calls=%async_computation | async-start | bytes 3145728 | tf_op jit(solution)/shard_map/all_to_all | solution.py:1299
  101.9 263.1 %reduce-scatter.2.cloned.1.call-start = ((), (), s32[]{:S(2)}) async-start(), calls=%async_computation.3 | async-start | bytes 1474560 | tf_op jit(solution)/shard_map/reduce_scatter | solution.py:1316
  144.5 2.6 copy-start.1
  219.1 83.8 %all-to-all-start.1 = ((bf16[4,256,768]{2,1,0:T(8,128)(2,1)}), bf16[4,256,768]{2,1,0:T(8,128)(2,1)S(1)}, u32[]{:S(2)}, u32[]{:S(2)}) async-start(bf16[4,256,768]{2,1,0:T(8,128)(2,1)} %bitcast.31), calls=%async_computation.1 | async-start | bytes 3145728 | tf_op jit(solution)/shard_map/all_to_all | solution.py:1312
  302.9 1.2 copy-start.2
Sparse Core Ops, SparseCore 0:
  10.5 37.5 all-gather.4
  92.7 54.3 all-gather.6
  219.2 43.9 reduce-scatter.1

commit v5 on v4

--- a/solution.py
+++ b/solution.py
@@ -465,10 +465,7 @@
     core = d % 2
     partners = [(d, lax.rem(t + s, nt)) for s in range(1, nt)]
     partners += [(flip(d, 1), lax.rem(t + s, nt)) for s in range(nt)]
-    bit = 2
-    while bit < nd:
-        partners.append((flip(d, bit), t))
-        bit *= 2
+    partners += [(flips(d, mask), t) for mask in range(2, nd, 2)]
     for partner in partners:
         pl.semaphore_signal(barrier, inc=1, device_id=device(partner), device_id_type=MESH)
     pl.semaphore_wait(barrier, len(partners))
@@ -483,14 +480,15 @@
 def start_kernel(
     nd, nt, share, halves, *refs,
 ):
-    tokens, grads, segments, later = refs[:4]
+    tokens, grads, segments, later, pre_mix, post_mix = refs[:6]
+    refs = refs[2:]
     if halves:
         weights, norms = refs[4:8], refs[8]
-        x_out, q_out, k_out, v_out, seg_out, mail_out, later_out, w_out, o_out, gain_out = refs[9:19]
-        wg_s, w_send, w_recv = refs[19:22]
+        x_out, q_out, k_out, v_out, seg_out, pre_out, post_out, mail_out, later_out, w_out, o_out, gain_out, near_out = refs[9:22]
+        wg_s, w_send, w_recv, n_send, n_recv, n_self = refs[22:28]
     else:
         w_out, gain_out = refs[4:6]
-        x_out, q_out, k_out, v_out, seg_out, mail_out, later_out = refs[6:13]
+        x_out, q_out, k_out, v_out, seg_out, pre_out, post_out, mail_out, later_out = refs[6:15]
     (g_send, g_recv, g_self, l_send, l_recv, x_s, kv_s, x_send, x_recv, x_self, kv_send, kv_recv, kv_self, seg_send, seg_recv, seg_self) = refs[-16:]
     d, t = 2 * lax.axis_index("plane") + lax.axis_index("core"), lax.axis_index("tensor")
     core = d % 2
@@ -517,8 +515,12 @@
             copy = remote(slab, slab, w_send.at[0, 0, s], w_recv.at[0, 0, s], (d, lax.rem(t + s, nt)))
             copy.start()
             z_copies.append(copy)
-        for copy in z_copies:
-            copy.wait()
+
+    heads = pre_mix.shape[0]
+    lane = lax.broadcasted_iota(jnp.int32, (heads, width), 1) // (width // heads)
+    member = (lane == lax.broadcasted_iota(jnp.int32, (heads, width), 0)).astype(BF16)
+    pre_out[...] = (left_t(pre_mix[...], member) * (width // heads) ** (-0.5)).astype(BF16)
+    post_out[...] = matmul(post_mix[...], member)
 
     g_copies = []
     for m in range(micro):
@@ -552,6 +554,11 @@
     l_copies = []
     for s in range(1, nt):
         l_copies.append(remote(later, later_out.at[s - 1], l_send.at[s], l_recv.at[s], (d, lax.rem(t + s, nt))))
+    if halves:
+        l_copies.append(pltpu.make_async_copy(later, near_out.at[d // 2], n_self))
+        for mask in range(2, nd, 2):
+            to = (flips(d, mask), t)
+            l_copies.append(remote(later, near_out.at[d // 2], n_send.at[mask // 2], n_recv.at[mask // 2], to))
     for copy in l_copies:
         copy.start()
 
@@ -559,6 +566,8 @@
         bits = [1 << k for k in range(1, nd.bit_length() - 1)]
         routes = [bits + [1], bits[::-1] + [1]]
         have = [[0] for _ in halves]
+        for copy in z_copies:
+            copy.wait()
         for stage in range(len(bits) + 1):
             copies = []
             for h, (lo, hi) in enumerate(halves):
@@ -630,7 +639,7 @@
         seg_there.wait_recv()
 
 
-def start(tokens, grads, segments, weights, norms, later):
+def start(tokens, grads, segments, pre_mix, post_mix, weights, norms, later):
     micro, _, rows, width = tokens.shape
     nd, nt = 2 * lax.axis_size("plane"), lax.axis_size("tensor")
     count = rows * nt // 2
@@ -647,11 +656,13 @@
     if inside:
         halves, given = [(0, middle), (middle, length)], [*weights, jnp.stack(norms).astype(F32)]
         given_specs = [vmem] * 4 + [SCALARS]
-        gathered_specs = [vmem, vmem, vmem]
+        gathered_specs = [vmem, vmem, vmem, vmem]
         gathered = [shaped((width, 3 * width), BF16), shaped((width, width), BF16), shaped((8, width), F32)]
+        gathered.append(shaped((nd // 2,) + later.shape, BF16))
         scratch = [
             pltpu.VMEM((nd, nt, length, width), BF16),
             dma((3, nd.bit_length(), most)), dma((3, nd.bit_length(), most)),
+            dma((nd // 2,)), dma((nd // 2,)), dma,
         ]
     else:
         place = (lax.axis_index("plane") * 2 * nt + lax.axis_index("core") * nt + lax.axis_index("tensor")) * share
@@ -664,14 +675,16 @@
         halves, given, given_specs, gathered_specs, gathered, scratch = [], [w_qkv, gains], [vmem, vmem], [], [], []
     results = pl.pallas_call(
         functools.partial(start_kernel, nd, nt, share, halves),
-        in_specs=[ANY, ANY, ANY, ANY] + given_specs,
-        out_specs=[vmem, vmem, ANY, ANY, ANY, vmem, ANY] + gathered_specs,
+        in_specs=[ANY, ANY, ANY, ANY, vmem, vmem] + given_specs,
+        out_specs=[vmem, vmem, ANY, ANY, ANY, vmem, vmem, vmem, ANY] + gathered_specs,
         out_shape=[
             shaped((count, width), BF16),
             shaped((count, width), BF16),
             shaped((blocks, 2, BLOCK, width), BF16),
             shaped((blocks, 2, BLOCK, width), BF16),
             shaped((2 * blocks, BLOCK), jnp.int32),
+            shaped((pre_mix.shape[0], width), BF16),
+            shaped((pre_mix.shape[0], width), F32),
             shaped((nt, per, BLOCK, width), BF16),
             shaped((nt - 1,) + later.shape, BF16),
             *gathered,
@@ -694,9 +707,16 @@
         grads.reshape(micro, rows // TILE, 2, BLOCK, width),
         segments.reshape(micro, 2 * blocks, BLOCK),
         later,
+        pre_mix,
+        post_mix,
         *given,
     )
-    return results if inside else (*results, w_qkv, w_out, gains)
+    if inside:
+        rest = [results[8]] + [send(results[8], by_bit(mask)) for mask in range(2, nd, 2)]
+        return (*results[:8], results[12], rest, *results[9:12])
+    near = lax.all_gather(later, ("plane", "core"), axis=0, tiled=False).reshape(nd // 2, 2, *later.shape)
+    rest = lax.all_gather(results[8], ("plane", "core"), axis=0, tiled=False).reshape(nd // 2, 2, *results[8].shape)
+    return (*results[:8], near, [rest], w_qkv, w_out, gains)
 
 
 def gelu_parts(v):
@@ -708,11 +728,13 @@
 
 
 def middle_kernel(rb, nd, nt, share, inside, *refs):
-    x_ref, att_ref, w_out, gain_ref, own_ref, rest_ref, dy_all = refs[:7]
-    out_ref, after_ref, datt_ref, dwo_ref, dgain_ref, part_ref = refs[7:13]
-    dy_ref, h_s, ht_s, dyt_s, o_s, dh_s, hid_s, dhid_s, w_s, dy_sem = refs[13:23]
+    x_ref, att_ref, w_out, gain_ref, near_all, dy_all = refs[:6]
+    pieces = nd // 2 if inside else 1
+    rest_all, refs = refs[6 : 6 + pieces], refs[pieces - 1 :]
+    mail_ref, after_ref, datt_ref, dwo_ref, dgain_ref, part_ref, last_ref = refs[7:14]
+    dy_ref, h_s, ht_s, dyt_s, o_s, dh_s, hid_s, dhid_s, w_s, dy_sem, w_self = refs[14:25]
     if inside:
-        g_s, core_s, plane_s, c_send, c_recv, p_send, p_recv = refs[23:]
+        g_s, core_s, plane_s, c_send, c_recv, p_send, p_recv, w_send, w_recv = refs[25:]
     step = pl.program_id(0)
     d, t = 2 * lax.axis_index("plane") + lax.axis_index("core"), lax.axis_index("tensor")
     count, width = x_ref.shape
@@ -720,10 +742,25 @@
     bits = [1 << k for k in range(1, nd.bit_length() - 1)]
     routes = [bits, bits[::-1]]
 
+    def weight_copies(k):
+        if not inside:
+            return [pltpu.make_async_copy(rest_all[0].at[:, :, k - 1] if k else near_all, w_s.at[k], w_self.at[k, 0])]
+        pairs = [(near_all, w_s.at[k, :, d % 2])]
+        if k:
+            pairs = [(rest_all[j].at[k - 1], w_s.at[k, flips(d, 2 * j) // 2, d % 2]) for j in range(pieces)]
+        copies = []
+        for j, (rows, there) in enumerate(pairs):
+            copies.append(pltpu.make_async_copy(rows, there, w_self.at[k, j]))
+            copies.append(remote(rows, there, w_send.at[k, j], w_recv.at[k, j], (flip(d, 1), t)))
+        return copies
+
     @pl.when(step == 0)
     def _():
         if inside:
             greet(nd, nt, d, t)
+        for k in range(nt):
+            for copy in weight_copies(k):
+                copy.start()
         dy_copy = pltpu.make_async_copy(dy_all, dy_ref, dy_sem)
         dy_copy.start()
         for r in parts:
@@ -731,21 +768,21 @@
             after = x_ref[rows, :].astype(F32) + matmul(att_ref[rows, :], w_out[...])
             after_ref[rows, :] = after
             o_s[rows, :] = after
-            h = (after * rms_scale(after) * gain_ref[...]).astype(BF16)
+            h = (after * rms_scale(after) * gain_ref[1:2]).astype(BF16)
             h_s[rows, :] = h
             ht_s[:, rows] = h.T
             dh_s[rows, :] = jnp.zeros((rb, width), F32)
-        for k in range(2):
-            w_s[k] = own_ref[:, k * share : (k + 1) * share]
         dy_copy.wait()
         for r in parts:
             rows = slice(r, r + rb)
             dyt_s[:, rows] = dy_ref[rows, :].T
 
-    @pl.when((step > 0) & (step < nt))
-    def _():
-        for k in range(2):
-            w_s[k] = rest_ref[:, 0, k * share : (k + 1) * share]
+    for k in range(nt):
+
+        @pl.when(step == k)
+        def _(k=k):
+            for copy in weight_copies(k):
+                copy.wait()
 
     def core_copies(slot):
         return [
@@ -775,8 +812,12 @@
             copy.wait()
         for j, mask in enumerate(masks_of(bits)):
             mine = flips(d, mask)
-            g_s[slot, mine] = (g_s[slot, mine].astype(F32) + core_s[slot, j].astype(F32)).astype(BF16)
-        for copy in plane_copies(slot, 0):
+            total = (g_s[slot, mine].astype(F32) + core_s[slot, j].astype(F32)).astype(BF16)
+            if isinstance(k, int):
+                last_ref[j] = total
+            else:
+                g_s[slot, mine] = total
+        for copy in [] if isinstance(k, int) else plane_copies(slot, 0):
             copy.start()
 
     def plane_done(k, stage):
@@ -793,7 +834,7 @@
             for copy in plane_copies(slot, stage + 1):
                 copy.start()
         else:
-            part_ref[lax.rem(t + nt - k, nt)] = g_s[slot, d]
+            mail_ref[lax.rem(t + nt - k, nt), : 2 * share] = g_s[slot, d]
 
     def when(condition, stage, *args):
         if inside:
@@ -801,7 +842,7 @@
 
     @pl.when(step < nt)
     def _():
-        up, down = (w_s[k].reshape(width, -1) for k in range(2))
+        up, down = (w_s[step, :, :, k * share : (k + 1) * share].reshape(width, -1) for k in range(2))
         for point, r in enumerate(parts):
             rows = slice(r, r + rb)
             v = matmul(h_s[rows, :], up)
@@ -823,6 +864,7 @@
                         g_s[slot, r // share + e, k * share : (k + 1) * share] = grad
                     else:
                         part_ref[r // share + e, 0, k] = grad
+                        last_ref[...] = jnp.zeros(last_ref.shape, BF16)
         if inside:
             for copy in core_copies(slot):
                 copy.start()
@@ -835,9 +877,9 @@
 
     @pl.when(step == nt)
     def _():
-        gain = gain_ref[...]
+        gain = gain_ref[1:2]
         total = jnp.zeros((8, width), F32)
-        out_ref[...] = o_s[...].astype(BF16)
+        mail_ref[:, mail_ref.shape[1] - count // nt :] = o_s[...].astype(BF16).reshape(nt, count // nt, width)
         for point, r in enumerate(parts):
             rows = slice(r, r + rb)
             after = after_ref[rows, :]
@@ -855,21 +897,20 @@
         if inside:
             plane_done(step - 2, len(bits) - 1)
         dgain_ref[...] = total
-        if inside:
-            for stage in range(len(bits) - 1):
-                plane_done(nt - 1, stage)
         dwo_ref[...] = left_t(att_ref[...], hid_s[...]).astype(BF16)
         if inside:
-            plane_done(nt - 1, len(bits) - 1)
-
-
-def feed_forward(x, attended, dy, w_out, gain, own, rest):
+            part_ref[...] = jnp.zeros(part_ref.shape, BF16)
+            mail_ref[lax.rem(t + 1, nt), : 2 * share] = jnp.zeros((2 * share, width), BF16)
+
+
+def feed_forward(x, attended, dy, w_out, gain, near, rest, nd):
     count, width = x.shape
-    nd, nt, units = own.shape[0], rest.shape[1] + 1, own.shape[2]
-    share = own.shape[1] // 2
+    nt, units = rest[0].shape[-3] + 1, rest[0].shape[-1]
+    share = rest[0].shape[-2] // 2
     inside = share % 16 == 0 and nd >= 8
     rb = 256
     rows = whole((count, width))
+    mail = (nt, count // nt + (2 * share if inside else 0), width)
     dma = pltpu.SemaphoreType.DMA
     scratch = [
         pltpu.VMEM((count, width), BF16),
@@ -880,18 +921,19 @@
         pltpu.VMEM((count, width), F32),
         pltpu.VMEM((count, units), BF16),
         pltpu.VMEM((count, units), BF16),
-        pltpu.VMEM((2, nd, share, units), BF16),
-        dma,
+        pltpu.VMEM((nt, nd // 2, 2, 2 * share, units), BF16),
+        dma, dma((nt, nd // 2)),
     ]
     if inside:
         stages = nd.bit_length() - 2
-        grads, grads_spec = jax.ShapeDtypeStruct((nt, 2 * share, units), BF16), whole((nt, 2 * share, units))
+        grads, grads_spec = jax.ShapeDtypeStruct((8, units), BF16), whole((8, units))
         scratch += [
             pltpu.VMEM((2, nd, 2 * share, units), BF16),
             pltpu.VMEM((2, nd // 2, 2 * share, units), BF16),
             pltpu.VMEM((2, stages, nd // 4, 2 * share, units), BF16),
             dma((2, nd // 2)), dma((2, nd // 2)),
             dma((2, stages, 2, nd // 4)), dma((2, stages, 2, nd // 4)),
+            dma((nt, nd // 2)), dma((nt, nd // 2)),
         ]
         params = dict(collective_id=2, has_side_effects=True)
     else:
@@ -902,24 +944,23 @@
         functools.partial(middle_kernel, rb, nd, nt, share, inside),
         grid=(nt + 1,),
         in_specs=[
-            rows, rows, whole((width, width)), whole((1, width)), whole(own.shape),
-            pl.BlockSpec((nd, 1, 2 * share, units), lambda s: (0, jnp.clip(s - 1, 0, nt - 2), 0, 0)),
-            ANY,
-        ],
-        out_specs=[rows, rows, rows, whole((width, width)), whole((8, width)), grads_spec],
+            rows, rows, whole((width, width)), whole((8, width)), ANY, ANY,
+        ] + [ANY] * len(rest),
+        out_specs=[whole(mail), rows, rows, whole((width, width)), whole((8, width)), grads_spec, whole((nd // 2, 2 * share, units))],
         out_shape=[
-            jax.ShapeDtypeStruct((count, width), BF16),
+            jax.ShapeDtypeStruct(mail, BF16),
             jax.ShapeDtypeStruct((count, width), F32),
             jax.ShapeDtypeStruct((count, width), BF16),
             jax.ShapeDtypeStruct((width, width), BF16),
             jax.ShapeDtypeStruct((8, width), F32),
             grads,
+            jax.ShapeDtypeStruct((nd // 2, 2 * share, units), BF16),
         ],
         scratch_shapes=scratch,
         compiler_params=pltpu.CompilerParams(vmem_limit_bytes=62 << 20, **params),
         cost_estimate=cost(12 * count * width * nt * units, 4 * nd * nt * share * units),
         name="feed_forward",
-    )(x, attended, w_out, gain, own, rest, dy)
+    )(x, attended, w_out, gain, near, dy, *rest)
 
 
 def masks_of(bits):
@@ -942,11 +983,12 @@
     nd, nt, share, inside, x_all, dq_all, dk_all, dv_all, after_all, w_all, gain_ref, dwo_all, small_ref,
     ffn_ref, back, *refs,
 ):
-    tok_out, out_out, dw_out, small_out = refs[:4]
-    own_s, other_s, grads_s, ht_s, tok_s, own_sems, kv_send, kv_recv, tok_send, tok_recv, tok_self = refs[4:15]
-    b_send, b_recv, b_self, x_ref, dq_ref, after_ref, w_ref, dwo_ref, in_sems = refs[15:24]
+    last_refs, refs = refs[: nd // 2], refs[nd // 2 :]
+    tok_out, out_out, dw_out, small_out, last_out = refs[:5]
+    own_s, other_s, grads_s, ht_s, tok_s, own_sems, kv_send, kv_recv, tok_send, tok_recv, tok_self = refs[5:16]
+    b_send, b_recv, b_self, x_ref, dq_ref, after_ref, w_ref, dwo_ref, in_sems, last4_s, last_sems, last_s, l_send, l_recv = refs[16:30]
     if inside:
-        slab_s, core_s, plane_s, mine_s, z_s, sm_s, sm_in, g_send, g_recv, s_send, s_recv = refs[24:]
+        slab_s, core_s, plane_s, mine_s, z_s, sm_s, sm_in, g_send, g_recv, s_send, s_recv = refs[30:]
     d, t = 2 * lax.axis_index("plane") + lax.axis_index("core"), lax.axis_index("tensor")
     core = d % 2
     count, width = x_all.shape
@@ -961,6 +1003,7 @@
         )
     ]
     own = [pltpu.make_async_copy(a.at[:, core], own_s.at[k], own_sems.at[k]) for k, a in enumerate((dk_all, dv_all))]
+    loads += [pltpu.make_async_copy(far, last4_s.at[k], last_sems.at[k]) for k, far in enumerate(last_refs)]
     for copy in own + loads:
         copy.start()
     greet(nd, nt, d, t)
@@ -980,10 +1023,14 @@
     for copy in exchanged[0] + exchanged[1]:
         copy.start()
     b_copies = []
+    skip = back.shape[1] - rows_in
     for m in range(out_out.shape[0]):
-        there = out_out.at[m, :, core]
-        b_copies.append(pltpu.make_async_copy(back.at[2 * m + core], there, b_self.at[m]))
-        b_copies.append(remote(back.at[2 * m + 1 - core], there, b_send.at[m], b_recv.at[m], (flip(d, 1), t)))
+        for k in range(per):
+            there, lines = out_out.at[m, k, core], pl.ds(skip + k * BLOCK, BLOCK)
+            b_copies.append(pltpu.make_async_copy(back.at[2 * m + core, lines], there, b_self.at[m, k]))
+            b_copies.append(
+                remote(back.at[2 * m + 1 - core, lines], there, b_send.at[m, k], b_recv.at[m, k], (flip(d, 1), t))
+            )
     gain = gain_ref[:1]
 
     def norms(rows):
@@ -1089,6 +1136,9 @@
 
     for copy in own + loads:
         copy.wait()
+    last_s[...] = sum(last4_s[k].astype(F32) for k in range(last4_s.shape[0])).astype(BF16)
+    last = remote(last_s, last_out, l_send, l_recv, (d, lax.rem(t + 1, nt)))
+    last.start()
     for r in range(0, count, rows_in):
         lines = slice(r, r + rows_in)
         normed, scale = norms(lines)
@@ -1158,7 +1208,7 @@
             dw_out[lines, : 3 * width] = matmul(ht_s[lines, :], grads_s[...]).astype(BF16)
             dw_out[lines, 3 * width :] = dwo_ref[lines, :]
 
-    for copy in b_copies:
+    for copy in b_copies + [last]:
         copy.wait()
     for here, far, near in sends:
         pl.when(jnp.logical_not(here))(far.wait_send)
@@ -1171,7 +1221,7 @@
             pl.when(jnp.logical_not(here))(back.wait_recv)
 
 
-def finish(x, dq, dk_all, dv_all, after, w_qkv, gains, dwo, small, gain_ffn, back, share, micro):
+def finish(x, dq, dk_all, dv_all, after, w_qkv, gains, dwo, small, gain_ffn, back, last, share, micro):
     count, width = x.shape
     nd, nt = 2 * lax.axis_size("plane"), lax.axis_size("tensor")
     inside = 2 * share % 16 == 0 and nd >= 8
@@ -1187,9 +1237,10 @@
         pltpu.VMEM((width, count), BF16),
         pltpu.VMEM((nt, per, BLOCK, width), BF16),
         dma((2,)), dma((2, nt)), dma((2, nt)), dma((nt,)), dma((nt,)), dma,
-        dma((micro,)), dma((micro,)), dma((micro,)),
+        dma((micro, per)), dma((micro, per)), dma((micro, per)),
         pltpu.VMEM(x.shape, x.dtype), pltpu.VMEM(dq.shape, dq.dtype), pltpu.VMEM(after.shape, after.dtype),
         pltpu.VMEM(w_qkv.shape, w_qkv.dtype), pltpu.VMEM(dwo.shape, dwo.dtype), dma((5,)),
+        pltpu.VMEM((nd // 2,) + last[0].shape, BF16), dma((nd // 2,)), pltpu.VMEM(last[0].shape, BF16), dma, dma,
     ]
     if inside:
         most = max(nd // 2, nt)
@@ -1206,13 +1257,14 @@
         ]
     return pl.pallas_call(
         functools.partial(finish_kernel, nd, nt, share, inside),
-        in_specs=[ANY, ANY, ANY, ANY, ANY, ANY, vmem, ANY, vmem, vmem, ANY],
-        out_specs=[vmem, vmem, vmem, vmem],
+        in_specs=[ANY, ANY, ANY, ANY, ANY, ANY, vmem, ANY, vmem, vmem, ANY] + [ANY] * len(last),
+        out_specs=[vmem, vmem, vmem, vmem, vmem],
         out_shape=[
             shaped((micro, per, 2, BLOCK, width), BF16),
             shaped((micro, per, 2, BLOCK, width), BF16),
             shaped((4 * share, width), F32) if inside else shaped((width, 4 * width), BF16),
             shaped(small.shape, F32),
+            shaped(last[0].shape, BF16),
         ],
         scratch_shapes=scratch,
         compiler_params=pltpu.CompilerParams(
@@ -1220,10 +1272,10 @@
         ),
         cost_estimate=cost(24 * count * width * width, 16 * count * width),
         name="finish",
-    )(x, dq, dk_all, dv_all, after, w_qkv, gains, dwo, small, gain_ffn, back.reshape(nt, per, BLOCK, width))
-
-
-def emit_kernel(heads, share, tok_ref, out_ref, dw_ref, ffn_ref, small_ref, tok, out, *rest):
+    )(x, dq, dk_all, dv_all, after, w_qkv, gains, dwo, small, gain_ffn, back, *last)
+
+
+def emit_kernel(heads, share, tok_ref, out_ref, dw_ref, ffn_ref, last_ref, small_ref, tok, out, *rest):
     grads, ups, gains, mixes = rest[:4], rest[4:6], rest[6:8], rest[8:10]
     tok[...] = tok_ref[...].astype(F32)
     out[...] = out_ref[...]
@@ -1232,9 +1284,13 @@
     def _():
         for grad, k in zip(grads, (0, 2, 3, 1)):
             grad[...] = dw_ref[k * share : (k + 1) * share]
-        half = ffn_ref.shape[0] // 2
+        half = last_ref.shape[0] // 2
         for k, up in enumerate(ups):
-            up[...] = ffn_ref[k * half : (k + 1) * half].astype(F32)
+            lines = slice(k * half, (k + 1) * half)
+            total = last_ref[lines].astype(F32)
+            for z in range(ffn_ref.shape[0]):
+                total = total + ffn_ref[z, lines].astype(F32)
+            up[...] = total
         width = small_ref.shape[1]
         place = (
             (lax.axis_index("plane") * 2 + lax.axis_index("core")) * lax.axis_size("tensor") + lax.axis_index("tensor")
@@ -1253,7 +1309,7 @@
         mixes[1][...] = sums[heads:]
 
 
-def emit(tok, out, dw, ffn, small, heads, share):
+def emit(tok, out, dw, ffn, last, small, heads, share):
     width = small.shape[1]
     micro, per, cores, block, _ = tok.shape
     rows = per * cores * block
@@ -1262,17 +1318,17 @@
         return pl.BlockSpec((1, rows, width), lambda i: (i, 0, 0))
 
     shaped = jax.ShapeDtypeStruct
-    small_shapes = [(share, width)] * 4 + [(ffn.shape[0] // 2, width)] * 2 + [(1, share)] * 2 + [(heads, heads)] * 2
+    small_shapes = [(share, width)] * 4 + [(last.shape[0] // 2, width)] * 2 + [(1, share)] * 2 + [(heads, heads)] * 2
     return pl.pallas_call(
         functools.partial(emit_kernel, heads, share),
         grid=(micro,),
-        in_specs=[part(0), part(1), whole(dw.shape), whole(ffn.shape), whole(small.shape)],
+        in_specs=[part(0), part(1), whole(dw.shape), whole((ffn.shape[0],) + last.shape), whole(last.shape), whole(small.shape)],
         out_specs=[part(0), part(1)] + [whole(shape) for shape in small_shapes],
         out_shape=[shaped((micro, rows, width), F32), shaped((micro, rows, width), BF16)]
         + [shaped(shape, F32) for shape in small_shapes],
         compiler_params=pltpu.CompilerParams(vmem_limit_bytes=62 << 20),
         name="emit",
-    )(tok.reshape(micro, rows, width), out.reshape(micro, rows, width), dw, ffn, small)
+    )(tok.reshape(micro, rows, width), out.reshape(micro, rows, width), dw, ffn, last, small)
 
 
 def per_device(
@@ -1291,43 +1347,37 @@
     core = d % 2
 
     later = jnp.concatenate([w_up, w_down])
-    own_rows = lax.all_gather(later, ("plane", "core"), axis=0, tiled=False)
-    x, query, k_all, v_all, segs, mail, later, w_qkv, all_out, gains = start(
-        tokens, out_grad, segments, [w_query, w_key, w_value, w_out], [norm_attn, norm_ffn], later
+    x, query, k_all, v_all, segs, pre, post, mail, near, rest, w_qkv, all_out, gains = start(
+        tokens, out_grad, segments, pre_mix, post_mix, [w_query, w_key, w_value, w_out], [norm_attn, norm_ffn], later
     )
     k_all, v_all = (a.reshape(2 * blocks, BLOCK, width) for a in (k_all, v_all))
     dy = lax.all_to_all(mail, "tensor", 0, 0, tiled=True).reshape(count, width)
-    rest_rows = lax.all_gather(later, ("plane", "core"), axis=0, tiled=False)
-
-    def by_lane(mix):
-        return jnp.repeat(mix.astype(F32), head_width, axis=1)
-
-    pre = (by_lane(pre_mix.T) * head_width ** (-0.5)).astype(BF16)
-    post = by_lane(post_mix)
-
     attended, u, lse = attend(query, k_all, v_all, segs, pre, post)
-    output, grad_after, grad_attended, grad_w_out, grad_gain_ffn, part_both = feed_forward(
-        x, attended, dy, all_out, gains[1:2], own_rows, rest_rows
+    mail, grad_after, grad_attended, grad_w_out, grad_gain_ffn, part_both, last_both = feed_forward(
+        x, attended, dy, all_out, gains, near, rest, nd
     )
-    back = lax.all_to_all(output.reshape(nt, count // nt, width), "tensor", 0, 0, tiled=True)
+    back = lax.all_to_all(mail, "tensor", 0, 0, tiled=True)
+    last_both = [last_both[0]] + [send(last_both[k], by_bit(2 * k)) for k in range(1, nd // 2)]
     if part_both.ndim > 3:
         part_both = lax.dynamic_slice_in_dim(jnp.concatenate([part_both[:, ::-1]] * 2, axis=1), nt - 1 - t, nt, 1)
         part_both = lax.psum_scatter(part_both, ("plane", "core"), scatter_dimension=0, tiled=False)
-    part_both = lax.psum_scatter(part_both, "tensor", scatter_dimension=0, tiled=False)
-    part_both = part_both.reshape(2 * w_up.shape[0], w_up.shape[1])
+        part_both = lax.psum_scatter(part_both, "tensor", scatter_dimension=0, tiled=False)
+        part_both = part_both.reshape(1, 2 * w_up.shape[0], w_up.shape[1])
+    else:
+        part_both = back
 
     grad_query, grad_key, grad_value, small = attend_back(
         query, grad_attended, u, lse, k_all, v_all, segs, pre, post
     )
-    d_tokens, out, owned, small = finish(
+    d_tokens, out, owned, small, last_both = finish(
         x, grad_query, grad_key.reshape(blocks, 2, BLOCK, width), grad_value.reshape(blocks, 2, BLOCK, width),
-        grad_after, w_qkv, gains, grad_w_out, small, grad_gain_ffn, back, share, micro,
+        grad_after, w_qkv, gains, grad_w_out, small, grad_gain_ffn, back, last_both, share, micro,
     )
     if owned.dtype == BF16:
         owned = lax.psum_scatter(owned, AXES, scatter_dimension=0, tiled=True).astype(F32)
         owned = jnp.concatenate([owned[:, k * width : (k + 1) * width] for k in (0, 3, 1, 2)])
         small = lax.psum(small, AXES)
-    d_tokens, out, *grads = emit(d_tokens, out, owned, part_both, small, heads, share)
+    d_tokens, out, *grads = emit(d_tokens, out, owned, part_both, last_both, small, heads, share)
     d_query, d_key, d_value, d_out, d_up, d_down, d_gain_attn, d_gain_ffn, d_pre, d_post = grads
     return (
         out.reshape(tokens.shape),

time: 382 us -> 369 us (0.966)
  between operations: 14.1 us -> 1.1 us
  starting transfers between devices: 13 us -> 22.5 us
  Pallas kernels: 339 us -> 335 us
  local copies, waits for them, and re-layouts: 6.77 us -> 2.79 us
    pallas_call x1, Pallas kernels: 71.9 us -> 63.4 us  [feed_forward(): pl.pallas_call(functools.partial(middle_kernel, rb, nd, nt, share, inside...]
    ppermute x0 -> x6, starting transfers between devices: none -> 7.04 us  [send(): return lax.ppermute(x, AXES, pairs)]
    pallas_call x1, Pallas kernels: 60.9 us -> 64.7 us  [finish(): pl.pallas_call(functools.partial(finish_kernel, nd, nt, share, inside), i...]
  transfers between devices with their start and end apart: 5 -> 8, of which waited for: 1 -> 0; matrix products, arithmetic and copies ran while one was open for 1% -> 0% of each run, Pallas kernels for 70% -> 33%
where the time goes in v5:
time: 369 us; the launch traced here: 364 us
  Pallas kernels  335 us (91%)
  starting transfers between devices  22.5 us (6%)
    pallas_call x1, Pallas kernels, start(): pl.pallas_call(functools.partial(start_kernel, nd, nt, share, halves), in...  82.2 us
    pallas_call x1, Pallas kernels, attend_back(): pl.pallas_call(functools.partial(backward_kernel, heads, groups), grid=(b...  80.2 us
    pallas_call x1, Pallas kernels, finish(): pl.pallas_call(functools.partial(finish_kernel, nd, nt, share, inside), i...  64.7 us
    pallas_call x1, Pallas kernels, feed_forward(): pl.pallas_call(functools.partial(middle_kernel, rb, nd, nt, share, inside...  63.4 us
    pallas_call x1, Pallas kernels, attend(): pl.pallas_call(functools.partial(forward_kernel, heads, groups, most), gr...  39.2 us
    all_to_all x1, starting transfers between devices, per_device(): dy = lax.all_to_all(mail, 'tensor', 0, 0, tiled=True).reshape(count, width)  10.7 us
  transfers between devices with their start and end apart: 8, of which 0 were waited for; matrix products, arithmetic and copies ran while one was open for 0% of the time, Pallas kernels for 33%

profile of v5, /device:TPU:0, one launch (start us, length us, event | category | flops | bytes accessed | tf_op | source)
XLA Modules:
  0.0 364.2 jit_solution(8795016295897697597)
XLA Ops:
  0.6 1.2 maximum_convert_fusion.refs_10_
  1.9 1.7 pad_maximum_fusion.refs_3_
  3.6 82.2 %start.1 = (bf16[1024,768]{1,0:T(8,128)(2,1)}, bf16[1024,768]{1,0:T(8,128)(2,1)}, bf16[8,2,128,768]{3,2,1,0:T(8,128)(2,1)}, bf16[8,2,128,768]{3,2,1,0:T(8,128)(2...) custom-call(bf16[2,2,2,128,768]{4,3,2,1,0:T(8,128)(2,1)} %bitcast.30, ...), custom_call_target="tpu_custom_call" | custom-call | tf_op jit(solution)/shard_map/start/pallas_call | solution.py:676
  85.8 1.0 collective-permute-start.2
  86.8 1.0 collective-permute-start.1
  87.9 1.5 collective-permute-start
  89.3 10.7 %all-to-all-start = ((bf16[4,2,128,768]{3,2,1,0:T(8,128)(2,1)}), bf16[4,2,128,768]{3,2,1,0:T(8,128)(2,1)S(1)}, u32[]{:S(2)}, u32[]{:S(2)}) async-start(bf16[4,2,128,768]{3,2,1,0:T(8,128)(2,1)} %get-tuple-element.66), calls=%async_computation | async-start | bytes 3145728 | tf_op jit(solution)/shard_map/all_to_all | solution.py:1354
  100.0 39.2 %attend.1 = (bf16[1024,768]{1,0:T(8,128)(2,1)}, bf16[8,12,128,768]{3,2,1,0:T(8,128)(2,1)}, f32[8,1536,128]{2,1,0:T(8,128)}) custom-call(bf16[1024,768]{1,0:T(8,128)(2,1)} %get-tuple-element.56.q_ref, bf16[16,128,768]{2,1,0:T(8,128)(2,1)} %bitcast.37, bf16[16,128,768]{2,1,0:T(8,128)(2,1)} %bitcast.39, s32[16,128]{1,0:T(8,128)} %get-tuple-element.59.seg_low, ...), custom_call_target="tpu_custom_call" | custom-call | flops 38654705664 | bytes 37748736 | tf_op jit(solution)/shard_map/attend/pallas_call | solution.py:248
  139.2 0.0 collective-permute-done.2.refs_9_
  139.2 0.0 collective-permute-done.1.refs_8_
  139.3 0.0 collective-permute-done.refs_7_
  139.3 0.0 all-to-all-done
  139.3 0.0 copy-start
  139.3 1.1 copy-done
  140.4 63.4 %feed_forward.1 = (bf16[4,448,768]{2,1,0:T(8,128)(2,1)}, f32[1024,768]{1,0:T(8,128)}, bf16[1024,768]{1,0:T(8,128)(2,1)}, bf16[768,768]{1,0:T(8,128)(2,1)}, f32[8...) custom-call(bf16[1024,768]{1,0:T(8,128)(2,1)} %get-tuple-element.55.refs_0_.x_all, ...), custom_call_target="tpu_custom_call" | custom-call | flops 28991029248 | bytes 9437184 | tf_op jit(solution)/shard_map/feed_forward/pallas_call | solution.py:943
  203.9 0.0 copy-start.1
  203.9 4.8 %all-to-all-start.1 = ((bf16[4,448,768]{2,1,0:T(8,128)(2,1)}), bf16[4,448,768]{2,1,0:T(8,128)(2,1)}, u32[]{:S(2)}, u32[]{:S(2)}) async-start(bf16[4,448,768]{2,1,0:T(8,128)(2,1)} %get-tuple-element.79), calls=%async_computation.1 | async-start | bytes 5505024 | tf_op jit(solution)/shard_map/all_to_all | solution.py:1359
  208.7 0.8 slice_bitcast_fusion
  209.5 1.5 collective-permute-start.5
  210.9 0.4 collective-permute-start.4
  211.3 1.6 collective-permute-start.3
  212.9 80.2 %attend_back.1 = (bf16[1024,768]{1,0:T(8,128)(2,1)}, bf16[16,128,768]{2,1,0:T(8,128)(2,1)}, bf16[16,128,768]{2,1,0:T(8,128)(2,1)}, f32[8,768]{1,0:T(8,128)}) custom-call(bf16[1024,768]{1,0:T(8,128)(2,1)} %get-tuple-element.56.q_ref, bf16[1024,768]{1,0:T(8,128)(2,1)} %get-tuple-element.68.g_ref, bf16[8,12,128,768]{3,2,1,0:T(8,128)(2,1)} %get-tuple-element.69.u_ref, ...), custom_call_target="tpu_custom_call" | custom-call | flops 96636764160 | bytes 37748736 | tf_op jit(solution)/shard_map/attend_back/pallas_call | solution.py:409
  293.1 0.0 collective-permute-done.5.refs_3_
  293.2 0.0 collective-permute-done.4.refs_2_
  293.2 0.0 collective-permute-done.3.refs_1_
  293.2 0.0 copy-start.4
  293.2 0.0 all-to-all-done.1.back.ffn_ref
  293.2 0.7 copy-done.2
  293.9 0.1 copy-done.3
  294.0 0.1 copy-done.4
  294.1 64.7 %finish.1 = (bf16[2,2,2,128,768]{4,3,2,1,0:T(8,128)(2,1)}, bf16[2,2,2,128,768]{4,3,2,1,0:T(8,128)(2,1)}, f32[96,768]{1,0:T(8,128)}, f32[8,768]{1,0:T(8,128)}, bf16[192,768]{1,0:T(8,128)(2,1)}) custom-call(bf16[1024,768]{1,0:T(8,128)(2,1)} %get-tuple-element.55.refs_0_.x_all, bf16[1024,768]{1,0:T(8,128)(2,1)} %get-tuple-element.71.dq_all, ...), custom_call_target="tpu_custom_call" | custom-call | flops 14495514624 | bytes 12582912 | tf_op jit(solution)/shard_map/finish/pallas_call | solution.py:1258
  358.8 5.1 %emit.1 = (f32[2,512,768]{2,1,0:T(8,128)}, bf16[2,512,768]{2,1,0:T(8,128)(2,1)}, f32[24,768]{1,0:T(8,128)}, f32[24,768]{1,0:T(8,128)}, f32[24,768]{1,0:T(8,128)}...) custom-call(bf16[2,512,768]{2,1,0:T(8,128)(2,1)} %bitcast.32, ...), custom_call_target="tpu_custom_call" | custom-call | tf_op jit(solution)/shard_map/emit/pallas_call | solution.py:1322
  (3 shorter events, 0.0 us)
Async XLA Ops:
  85.8 53.5 %collective-permute-start.2 = (bf16[3,192,768]{2,1,0:T(8,128)(2,1)}, bf16[3,192,768]{2,1,0:T(8,128)(2,1)}, u32[]{:S(2)}, u32[]{:S(2)}) collective-permute-start(bf16[3,192,768]{2,1,0:T(8,128)(2,1)} %get-tuple-element.67.refs_6_), channel_id=1, source_target_pairs={{0,24},{1,25},{2,26},{3,27},{4,28},{5,29},{6,30},{7,31},{8,16},{9,... | collective-permute-start | bytes 2654216 | tf_op jit(solution)/shard_map/ppermute | solution.py:56
  86.8 52.4 %collective-permute-start.1 = (bf16[3,192,768]{2,1,0:T(8,128)(2,1)}, bf16[3,192,768]{2,1,0:T(8,128)(2,1)}, u32[]{:S(2)}, u32[]{:S(2)}) collective-permute-start(bf16[3,192,768]{2,1,0:T(8,128)(2,1)} %get-tuple-element.67.refs_6_), channel_id=1, source_target_pairs={{0,16},{1,17},{2,18},{3,19},{4,20},{5,21},{6,22},{7,23},{8,24},{9,... | collective-permute-start | bytes 2654216 | tf_op jit(solution)/shard_map/ppermute | solution.py:56
  87.9 51.4 %collective-permute-start = (bf16[3,192,768]{2,1,0:T(8,128)(2,1)}, bf16[3,192,768]{2,1,0:T(8,128)(2,1)}, u32[]{:S(2)}, u32[]{:S(2)}) collective-permute-start(bf16[3,192,768]{2,1,0:T(8,128)(2,1)} %get-tuple-element.67.refs_6_), channel_id=1, source_target_pairs={{0,8},{1,9},{2,10},{3,11},{4,12},{5,13},{6,14},{7,15},{8,0},{9,1},... | collective-permute-start | bytes 2654216 | tf_op jit(solution)/shard_map/ppermute | solution.py:56
  89.3 49.9 %all-to-all-start = ((bf16[4,2,128,768]{3,2,1,0:T(8,128)(2,1)}), bf16[4,2,128,768]{3,2,1,0:T(8,128)(2,1)S(1)}, u32[]{:S(2)}, u32[]{:S(2)}) async-start(bf16[4,2,128,768]{3,2,1,0:T(8,128)(2,1)} %get-tuple-element.66), calls=%async_computation | async-start | bytes 3145728 | tf_op jit(solution)/shard_map/all_to_all | solution.py:1354
  139.3 1.1 copy-start
  203.9 4.8 %copy-start.1 = (bf16[4,192,768]{2,1,0:T(8,128)(2,1)S(1)}, bf16[4,192,768]{2,1,0:T(8,128)(2,1)}, u32[]{:S(2)}) copy-start(bf16[4,192,768]{2,1,0:T(8,128)(2,1)} %get-tuple-element.80) | copy-start | bytes 3538948
  203.9 89.3 %all-to-all-start.1 = ((bf16[4,448,768]{2,1,0:T(8,128)(2,1)}), bf16[4,448,768]{2,1,0:T(8,128)(2,1)}, u32[]{:S(2)}, u32[]{:S(2)}) async-start(bf16[4,448,768]{2,1,0:T(8,128)(2,1)} %get-tuple-element.79), calls=%async_computation.1 | async-start | bytes 5505024 | tf_op jit(solution)/shard_map/all_to_all | solution.py:1359
  209.5 83.7 %collective-permute-start.5 = (bf16[192,768]{1,0:T(8,128)(2,1)S(1)}, bf16[192,768]{1,0:T(8,128)(2,1)S(1)}, u32[]{:S(2)}, u32[]{:S(2)}) collective-permute-start(bf16[192,768]{1,0:T(8,128)(2,1)S(1)} %get-tuple-element.110), channel_id=1, source_target_pairs={{0,24},{1,25},{2,26},{3,27},{4,28},{5,29},{6,30},{7,31},{8,16},{9,... | collective-permute-start | bytes 884744 | tf_op jit(solution)/shard_map/ppermute | solution.py:56
  210.9 82.2 %collective-permute-start.4 = (bf16[192,768]{1,0:T(8,128)(2,1)S(1)}, bf16[192,768]{1,0:T(8,128)(2,1)S(1)}, u32[]{:S(2)}, u32[]{:S(2)}) collective-permute-start(bf16[192,768]{1,0:T(8,128)(2,1)S(1)} %get-tuple-element.111), channel_id=1, source_target_pairs={{0,16},{1,17},{2,18},{3,19},{4,20},{5,21},{6,22},{7,23},{8,24},{9,... | collective-permute-start | bytes 884744 | tf_op jit(solution)/shard_map/ppermute | solution.py:56
  211.3 81.9 %collective-permute-start.3 = (bf16[192,768]{1,0:T(8,128)(2,1)S(1)}, bf16[192,768]{1,0:T(8,128)(2,1)S(1)}, u32[]{:S(2)}, u32[]{:S(2)}) collective-permute-start(bf16[192,768]{1,0:T(8,128)(2,1)S(1)} %get-tuple-element.112), channel_id=1, source_target_pairs={{0,8},{1,9},{2,10},{3,11},{4,12},{5,13},{6,14},{7,15},{8,0},{9,1},... | collective-permute-start | bytes 884744 | tf_op jit(solution)/shard_map/ppermute | solution.py:56
  293.1 0.7 copy-start.2
  293.2 0.8 copy-start.3
  293.2 0.9 copy-start.4
